TPU v7x, 32 devices: a whole 2x2x4 slice. The times are simulated.
32 devices in a mesh: wide: 16 (over z, x, core), narrow: 2 (over y).
Axes of the slice: x: 2, y: 2, z: 4, core: 2. Of those that a mesh axis runs over, the one named last changes fastest.
Arguments:
- tokens: bfloat16 [32768, 768], P('wide', 'narrow'), may hold values from -6 to 6
- lengths: int32 [256], P('wide'), may hold values from 32 to 128
- mask_pos: int32 [256, 38], P('wide'), may hold values from 0 to 127, as said below
- mask_vector: bfloat16 [768], P('narrow'), may hold values from -6 to 6
- norm1_gain: bfloat16 [768], P('narrow'), may hold values from 0.099609375 to 1.8984375
- in_left: bfloat16 [4, 192, 192], P('narrow'), may hold values from -0.4375 to 0.4375
- in_right: bfloat16 [4, 192, 576], P('narrow'), may hold values from -0.4375 to 0.4375
- filter_weight: bfloat16 [128, 768], P(None, 'narrow'), may hold values from -0.0625 to 0.0625
- decay: float32 [768], P('narrow'), may hold values from 0.005 to 0.1
- skip_gain: bfloat16 [768], P('narrow'), may hold values from -4 to 4
- out_left: bfloat16 [4, 192, 192], P('narrow'), may hold values from -0.4375 to 0.4375
- out_right: bfloat16 [4, 192, 192], P('narrow'), may hold values from -0.4375 to 0.4375
- norm2_gain: bfloat16 [768], P('narrow'), may hold values from 0.099609375 to 1.8984375
- up_left: bfloat16 [4, 192, 192], P('narrow'), may hold values from -0.4375 to 0.4375
- up_right: bfloat16 [4, 192, 1536], P('narrow'), may hold values from -0.4375 to 0.4375
- down_left: bfloat16 [4, 768, 192], P('narrow'), may hold values from -0.21875 to 0.21875
- down_right: bfloat16 [4, 192, 192], P('narrow'), may hold values from -0.4375 to 0.4375
- cotangent: bfloat16 [32768, 768], P('wide', 'narrow'), may hold values from -6 to 6
Outputs:
- output: bfloat16 [32768, 768], P('wide', 'narrow')
- tokens_grad: float32 [32768, 768], P('wide', 'narrow')
- mask_vector_grad: float32 [768], P('narrow')
- norm1_gain_grad: float32 [768], P('narrow')
- in_left_grad: float32 [4, 192, 192], P('narrow')
- in_right_grad: float32 [4, 192, 576], P('narrow')
- filter_weight_grad: float32 [128, 768], P(None, 'narrow')
- decay_grad: float32 [768], P('narrow')
- skip_gain_grad: float32 [768], P('narrow')
- out_left_grad: float32 [4, 192, 192], P('narrow')
- out_right_grad: float32 [4, 192, 192], P('narrow')
- norm2_gain_grad: float32 [768], P('narrow')
- up_left_grad: float32 [4, 192, 192], P('narrow')
- up_right_grad: float32 [4, 192, 1536], P('narrow')
- down_left_grad: float32 [4, 768, 192], P('narrow')
- down_right_grad: float32 [4, 192, 192], P('narrow')
- penalty: float32 [], replicated
Inputs may be any that keep to these rules, and one draw needn't show every extreme that they name: `mask_pos`: the 38 positions of one sequence are all different.
All inputs are finite; a program needn't handle non-finite values.
Results may differ from a plain program's by a relative error of at most 0.02.
Values may be sent and summed in bfloat16 or wider, within the bound.
No kernel may reach another device: no remote copies, remote signals or barrier semaphores. Data moves between devices by JAX's collectives and lax.ppermute only.
A program may use at most 256 MiB of HBM per device.

v0:
```python
import functools

import jax
import jax.numpy as jnp
import numpy as np
from jax import lax
from jax.experimental import pallas as pl
from jax.experimental.pallas import tpu as pltpu
from jax.sharding import PartitionSpec as P

D = 768
NB = 4
ORDER = 128
LEN = 128
BS = 192
FB = 768
GROUP = BS // NB
HALF = D // 2
QUARTER = BS // 4

epsilon = 1e-05
penalty_weight = 0.005

bf16 = jnp.bfloat16
f32 = jnp.float32

TILE = 512
BACK_TILE = 256
VMEM = 60 << 20

FILTER_ROW = 6 * QUARTER
VECTOR_ROW = FILTER_ROW + ORDER // 4
MIX_W = VECTOR_ROW + 16
FFN_W = 7 * QUARTER
FFN_G = 1280
MIX_G = 768


def transform_tables():
    t = np.arange(LEN, dtype=np.float64)[:, None]
    k = np.arange(LEN, dtype=np.float64)[None, :]
    angle = np.pi * (2 * k + 1) * t / (2 * LEN)
    forward = np.concatenate([np.cos(angle), np.sin(angle)], axis=1)
    return forward.astype(bf16), (forward.T / LEN).astype(bf16)


def feature_parts():
    t = np.arange(LEN, dtype=np.float64)[None, :]
    freqs = (np.arange(ORDER // 2, dtype=np.float64)[:, None] + 1.0) * (3.1 / (ORDER // 2))
    table = np.concatenate([np.sin(t * freqs), np.cos(t * freqs)], axis=0)
    parts = []
    for _ in range(3):
        part = table.astype(bf16)
        parts.append(part)
        table = table - part.astype(np.float64)
    return np.stack(parts)


def nn(a, b):
    return lax.dot_general(a, b, (((1,), (0,)), ((), ())), preferred_element_type=f32)


def nt(a, b):
    return lax.dot_general(a, b, (((1,), (1,)), ((), ())), preferred_element_type=f32)


def tn(a, b):
    return lax.dot_general(a, b, (((0,), (0,)), ((), ())), preferred_element_type=f32)


def exact_nt(a, b):
    return lax.dot_general(
        a,
        b,
        (((1,), (1,)), ((), ())),
        preferred_element_type=f32,
        precision=lax.Precision.HIGHEST,
    )


def fold(values):
    out = values[:, :LEN]
    for start in range(LEN, values.shape[1], LEN):
        out = out + values[:, start : start + LEN]
    return out


def rows_of(block, size):
    return pl.ds(pl.multiple_of(block * size, size), size)


def column(cols_ref, index):
    return cols_ref[:, index : index + 1]


def place_halves(dst_ref, side, own, other):
    dst_ref[rows_of(side, HALF), :] = own
    dst_ref[rows_of(1 - side, HALF), :] = other


def regroup(dst_ref, block, values):
    for g in range(NB):
        dst_ref[g * BS + block * GROUP : g * BS + (block + 1) * GROUP, :] = values[
            g * GROUP : (g + 1) * GROUP, :
        ]


def block(ref, index, size=BS):
    return ref[index * size : (index + 1) * size, :]


def norm_stats(values):
    center = values - jnp.sum(values, axis=0, keepdims=True) * (1.0 / D)
    spread = jnp.sum(center * center, axis=0, keepdims=True) * (1.0 / D)
    scale_row = lax.rsqrt(spread + epsilon)
    return center * scale_row, scale_row


def norm_back(grad, normed, scale_row, gain):
    scaled = grad * gain
    first = jnp.sum(scaled, axis=0, keepdims=True) * (1.0 / D)
    second = jnp.sum(scaled * normed, axis=0, keepdims=True) * (1.0 / D)
    return scale_row * (scaled - first - normed * second)


def pack_kernel(
    s_ref, il, ir, ol, orr, ul, ur, dl, dr, weight, mask, gain1, gain2, skip, decay, mix_ref, ffn_ref
):
    def pairs(ref):
        return jnp.concatenate([ref[0], ref[1]], axis=1)

    q = QUARTER
    mix_ref[0:q, :] = pairs(il)
    wide_in = pairs(ir)
    for c in range(3):
        mix_ref[(1 + c) * q : (2 + c) * q, :] = wide_in[:, c * HALF : (c + 1) * HALF]
    mix_ref[4 * q : 5 * q, :] = pairs(ol)
    mix_ref[5 * q : 6 * q, :] = pairs(orr)
    mix_ref[FILTER_ROW:VECTOR_ROW, :] = weight[...]
    rest = decay[...].reshape(1, HALF)
    rows = [item[...].reshape(1, HALF).astype(f32) for item in (mask, gain1, gain2, skip)]
    for _ in range(3):
        part = rest.astype(bf16).astype(f32)
        rows.append(part)
        rest = rest - part
    line = lax.broadcasted_iota(jnp.int32, (16, HALF), 0)
    vectors = jnp.zeros((16, HALF), f32)
    for index, row in enumerate(rows):
        vectors = jnp.where(line == index, row, vectors)
    mix_ref[VECTOR_ROW:, :] = vectors.astype(bf16)
    for c in range(4):
        ffn_ref[c * q : (c + 1) * q, :] = ur[0][:, c * HALF : (c + 1) * HALF]
    for c in range(2):
        ffn_ref[(4 + c) * q : (5 + c) * q, :] = dl[0][:, c * HALF : (c + 1) * HALF]
    ffn_ref[6 * q : 7 * q, :] = jnp.concatenate([ul[0], dr[0]], axis=1)


def pack_weights(scalars, mixer_weights, dense_weights, filter_weight, vectors):
    def quarter(item):
        return pl.BlockSpec((2, QUARTER, item.shape[2]), lambda i, s: (0, s[1], 0))

    def eighth(item):
        return pl.BlockSpec((1, QUARTER, item.shape[2]), lambda i, s: (s[2], s[1], 0))

    return pl.pallas_call(
        pack_kernel,
        out_shape=(
            jax.ShapeDtypeStruct((MIX_W, HALF), bf16),
            jax.ShapeDtypeStruct((FFN_W, HALF), bf16),
        ),
        grid_spec=pltpu.PrefetchScalarGridSpec(
            num_scalar_prefetch=1,
            grid=(1,),
            in_specs=[quarter(item) for item in mixer_weights]
            + [eighth(item) for item in dense_weights]
            + [pl.BlockSpec((ORDER // 4, HALF), lambda i, s: (s[1], 0))]
            + [whole(item.shape) for item in vectors],
            out_specs=(whole((MIX_W, HALF)), whole((FFN_W, HALF))),
        ),
        name="pack_weights",
    )(scalars, *mixer_weights, *dense_weights, filter_weight, *vectors)


def unpack_narrow(dst, other, row, piece, base):
    for j in range(2):
        dst[2 * other + j, pl.ds(row, QUARTER), :] = piece[
            base : base + QUARTER, j * BS : (j + 1) * BS
        ]


def own_blocks(dst, side, src):
    for j in range(2):
        dst[2 * side + j] = src[j]


def filter_kernel(
    s_ref, own, mine, p0, p1, p2, p3, feats, fwd, taps_ref, spec_ref, pen_ref, cols_ref, weight
):
    side = s_ref[0]
    q = ORDER // 4
    for p, piece in enumerate((p0, p1, p2, p3)):
        row = pl.multiple_of(jnp.bitwise_xor(s_ref[1], p) * q, q)
        weight[pl.ds(row, q), :] = piece[FILTER_ROW:VECTOR_ROW, :]
    for which, src, rows in ((side, own, mine), (1 - side, weight, p0)):
        table = src[...]
        basis = tn(table, feats[2]) + tn(table, feats[1]) + tn(table, feats[0])
        taps_ref[rows_of(which, HALF), :] = basis
        vectors = rows[VECTOR_ROW:, :].astype(f32)
        vectors = jnp.concatenate([vectors, jnp.zeros((LEN - 16, HALF), f32)], axis=0)
        vectors = vectors.T
        lane = lax.broadcasted_iota(jnp.int32, (HALF, LEN), 1)
        decay = vectors[:, 4:5] + vectors[:, 5:6] + vectors[:, 6:7]
        cols_ref[rows_of(which, HALF), :] = jnp.where(lane == 4, decay, vectors)
    positions = lax.broadcasted_iota(jnp.int32, (1, LEN), 1).astype(f32)
    taps = taps_ref[...] * jnp.exp(-column(cols_ref, 4) * positions)
    taps_ref[...] = taps
    spec_ref[...] = nn(taps.astype(bf16), fwd[...])
    total = jnp.sum(jnp.sum(taps * taps, axis=0, keepdims=True), axis=1, keepdims=True)
    pen_ref[...] = jnp.broadcast_to(total * penalty_weight, (8, LEN))


def whole(shape):
    return pl.BlockSpec(shape, lambda *_: (0,) * len(shape))


def filter_call(scalars, own, mine, pieces, feats, fwd):
    ins = (own, mine) + tuple(pieces) + (feats, fwd)
    outs = (
        jax.ShapeDtypeStruct((D, LEN), f32),
        jax.ShapeDtypeStruct((D, 2 * LEN), f32),
        jax.ShapeDtypeStruct((8, LEN), f32),
        jax.ShapeDtypeStruct((D, LEN), f32),
    )
    return pl.pallas_call(
        filter_kernel,
        out_shape=outs,
        grid_spec=pltpu.PrefetchScalarGridSpec(
            num_scalar_prefetch=1,
            grid=(1,),
            in_specs=[whole(item.shape) for item in ins],
            out_specs=tuple(whole(item.shape) for item in outs),
            scratch_shapes=[pltpu.VMEM((ORDER, HALF), bf16)],
        ),
        name="filter_spectrum",
    )(scalars, *ins)


def mixer_forward_kernel(
    s_ref,
    own,
    oth,
    marks,
    cols,
    spec,
    fwd,
    inv,
    il,
    ir,
    ol,
    orr,
    p0,
    p1,
    p2,
    p3,
    middle,
    first,
    kept,
    scale,
    wil,
    wir,
    wol,
    wor,
    enter,
    half,
    conv,
):
    side = s_ref[0]

    @pl.when(pl.program_id(0) == 0)
    def _():
        other = 1 - side
        own_blocks(wil, side, il)
        own_blocks(wir, side, ir)
        own_blocks(wol, side, ol)
        own_blocks(wor, side, orr)
        q = QUARTER
        for p, piece in enumerate((p0, p1, p2, p3)):
            row = pl.multiple_of(jnp.bitwise_xor(s_ref[1], p) * q, q)
            unpack_narrow(wil, other, row, piece, 0)
            at = pl.ds(row, q)
            wir[2 * other, at, 0:HALF] = piece[q : 2 * q, :]
            wir[2 * other, at, HALF : 3 * BS] = piece[2 * q : 3 * q, 0:BS]
            wir[2 * other + 1, at, 0:BS] = piece[2 * q : 3 * q, BS:HALF]
            wir[2 * other + 1, at, BS : 3 * BS] = piece[3 * q : 4 * q, :]
            unpack_narrow(wol, other, row, piece, 4 * q)
            unpack_narrow(wor, other, row, piece, 5 * q)

    place_halves(enter, side, own[...].T.astype(f32), oth[...].T.astype(f32))
    valid = marks[0:1, :]
    masked = marks[1:2, :]
    tokens = enter[...]
    entered = tokens + masked * (column(cols, 0) - tokens)
    enter[...] = entered
    normed, scale_row = norm_stats(entered)
    scale[...] = jnp.broadcast_to(scale_row, scale.shape)
    half[...] = (normed * column(cols, 1)).astype(bf16)
    first[0] = half[...]
    for b in range(NB):
        regroup(first.at[1], b, tn(wil[b], block(half, b)).astype(bf16))
    for g in range(NB):
        projected = tn(wir[g], block(first.at[1], g))
        rows = slice(g * BS, (g + 1) * BS)
        for part in range(3):
            kept[part, rows, :] = projected[part * BS : (part + 1) * BS, :].astype(bf16)
        source = (projected[:BS] * projected[2 * BS :] * valid).astype(bf16)
        half[rows, :] = source
    for s in range(TILE // LEN):
        lanes = slice(s * LEN, (s + 1) * LEN)
        wave = nn(half[:, lanes], fwd[...])
        wc, ws = wave[:, :LEN], wave[:, LEN:]
        hc, hs = spec[:, :LEN], spec[:, LEN:]
        product = jnp.concatenate(
            [(wc * hc - ws * hs).astype(bf16), (wc * hs + ws * hc).astype(bf16)], axis=1
        )
        conv[:, lanes] = nn(product, inv[...])
    inner = conv[...] + column(cols, 3) * half[...].astype(f32)
    kept[3] = inner.astype(bf16)
    half[...] = (kept[1].astype(f32) * inner).astype(bf16)
    for b in range(NB):
        regroup(kept.at[4], b, tn(wol[b], block(half, b)).astype(bf16))
    for g in range(NB):
        rows = slice(g * BS, (g + 1) * BS)
        middle[rows, :] = enter[rows, :] + tn(wor[g], block(kept.at[4], g))


def mixer_forward(scalars, own, oth, marks, cols, spec, fwd, inv, weights):
    row_count = own.shape[0] // 2
    steps = row_count // TILE
    ins = (own, oth, marks, cols, spec, fwd, inv) + tuple(weights)
    in_specs = [
        pl.BlockSpec((TILE, HALF), lambda i, s: (s[0] * steps + i, 0)),
        pl.BlockSpec((TILE, HALF), lambda i, s: (i, 0)),
        pl.BlockSpec((8, TILE), lambda i, s: (0, i)),
    ] + [whole(item.shape) for item in ins[3:]]
    full = [(NB, BS, BS), (NB, BS, 3 * BS), (NB, BS, BS), (NB, BS, BS)]
    outs = [
        jax.ShapeDtypeStruct((D, row_count), f32),
        jax.ShapeDtypeStruct((2, D, row_count), bf16),
        jax.ShapeDtypeStruct((5, D, row_count), bf16),
        jax.ShapeDtypeStruct((8, row_count), f32),
    ] + [jax.ShapeDtypeStruct(shape, bf16) for shape in full]
    out_specs = [
        pl.BlockSpec((D, TILE), lambda i, s: (0, i)),
        pl.BlockSpec((2, D, TILE), lambda i, s: (0, 0, i)),
        pl.BlockSpec((5, D, TILE), lambda i, s: (0, 0, i)),
        pl.BlockSpec((8, TILE), lambda i, s: (0, i)),
    ] + [whole(shape) for shape in full]
    return pl.pallas_call(
        mixer_forward_kernel,
        out_shape=tuple(outs),
        grid_spec=pltpu.PrefetchScalarGridSpec(
            num_scalar_prefetch=1,
            grid=(steps,),
            in_specs=in_specs,
            out_specs=tuple(out_specs),
            scratch_shapes=[
                pltpu.VMEM((D, TILE), f32),
                pltpu.VMEM((D, TILE), bf16),
                pltpu.VMEM((D, TILE), f32),
            ],
        ),
        compiler_params=pltpu.CompilerParams(vmem_limit_bytes=VMEM),
        name="mixer_forward",
        cost_estimate=pl.CostEstimate(
            flops=row_count * 2 * 1500000, bytes_accessed=row_count * 20000, transcendentals=0
        ),
    )(scalars, *ins)


ACC_SHAPES = ((NB, BS, 2 * FB), (NB, BS, FB), (NB, BS, BS), (NB, BS, BS), (D, LEN))


def dense_kernel(
    s_ref,
    middle,
    own,
    oth,
    cols,
    ul,
    ur,
    dl,
    dr,
    p0,
    p1,
    p2,
    p3,
    p4,
    p5,
    p6,
    p7,
    out_own,
    out_send,
    grad_middle,
    keep,
    send,
    packed_dr,
    wul,
    wur,
    wdl,
    wdr,
    gur,
    gdl,
    gul,
    gdr,
    ggain,
    top,
    half,
    moved3,
    moved4,
    hid,
    act,
    slope,
    gated,
    back,
    outs,
    *,
    steps,
):
    side = s_ref[0]

    @pl.when(pl.program_id(0) == 0)
    def _():
        other = 1 - side
        own_blocks(wul, side, ul)
        own_blocks(wur, side, ur)
        own_blocks(wdl, side, dl)
        own_blocks(wdr, side, dr)
        q = QUARTER
        for p, piece in enumerate((p0, p1, p2, p3, p4, p5, p6, p7)):
            row = pl.multiple_of(jnp.bitwise_xor(s_ref[1], p & 3) * q, q)
            at = pl.ds(row, q)
            blk = 2 * other + jnp.bitwise_xor(s_ref[2], p >> 2)
            for c in range(4):
                wur[blk, at, c * HALF : (c + 1) * HALF] = piece[c * q : (c + 1) * q, :]
            for c in range(2):
                wdl[blk, at, c * HALF : (c + 1) * HALF] = piece[(4 + c) * q : (5 + c) * q, :]
            wul[blk, at, :] = piece[6 * q : 7 * q, :BS]
            wdr[blk, at, :] = piece[6 * q : 7 * q, BS:]
        for acc in (gur, gdl, gul, gdr, ggain):
            acc[...] = jnp.zeros(acc.shape, f32)

    gain = column(cols, 2)
    normed, scale_row = norm_stats(middle[...])
    half[...] = (normed * gain).astype(bf16)
    for b in range(NB):
        regroup(moved3, b, tn(wul[b], block(half, b)).astype(bf16))
    for g in range(NB):
        rows = slice(g * FB, (g + 1) * FB)
        both = tn(wur[g], block(moved3, g))
        gate, up = both[:FB], both[FB:]
        chance = 0.5 + 0.5 * lax.erf(gate * 0.7071067811865476)
        density = jnp.exp(gate * gate * -0.5) * 0.3989422804014327
        active = gate * chance
        hid[rows, :] = (active * up).astype(bf16)
        act[rows, :] = active.astype(bf16)
        slope[rows, :] = (up * (chance + gate * density)).astype(bf16)
        regroup(moved4, g, nn(wdl[g], hid[rows, :]).astype(bf16))
    for g in range(NB):
        rows = slice(g * BS, (g + 1) * BS)
        outs[rows, :] = (middle[rows, :] + tn(wdr[g], block(moved4, g))).astype(bf16)
    out_own[...] = outs[rows_of(side, HALF), :].T
    out_send[...] = outs[rows_of(1 - side, HALF), :].T
    place_halves(top, side, own[...].T, oth[...].T)
    for g in range(NB):
        grad = block(top, g)
        regroup(back, g, nn(wdr[g], grad).astype(bf16))
        gdr[g] += nt(block(moved4, g), grad)
    for b in range(NB):
        rows = slice(b * FB, (b + 1) * FB)
        returned = block(back, b)
        grad_hidden = tn(wdl[b], returned)
        gdl[b] += nt(returned, hid[rows, :])
        gated[:FB, :] = (grad_hidden * slope[rows, :].astype(f32)).astype(bf16)
        gated[FB:, :] = (grad_hidden * act[rows, :].astype(f32)).astype(bf16)
        moved = block(moved3, b)
        gur[b] += nt(moved, gated[...])
        regroup(moved4, b, nn(wur[b], gated[...]).astype(bf16))
    grads = []
    for b in range(NB):
        returned = block(moved4, b)
        grads.append(nn(wul[b], returned))
        gul[b] += nt(block(half, b), returned)
    grad_in = jnp.concatenate(grads, axis=0)
    ggain[...] += fold(grad_in * normed)
    grad_middle[...] = top[...].astype(f32) + norm_back(grad_in, normed, scale_row, gain)

    @pl.when(pl.program_id(0) == steps - 1)
    def _():
        sums = exact_nt(jnp.ones((16, LEN), f32), ggain[...]).astype(bf16)

        def write(dst, j):
            part = BS // 2
            for y in range(2):
                b = 2 * y + j
                for c in range(4):
                    dst[y, c * BS : (c + 1) * BS, :] = gur[b, :, c * HALF : (c + 1) * HALF].astype(
                        bf16
                    )
                for c in range(2):
                    at = (4 + c) * BS
                    dst[y, at : at + BS, :] = gdl[b, :, c * HALF : (c + 1) * HALF].astype(bf16)
                at = 6 * BS
                for lane in range(2):
                    dst[y, at : at + part, lane * BS : (lane + 1) * BS] = gul[
                        2 * y + lane, j * part : (j + 1) * part, :
                    ].astype(bf16)
                at += part
                dst[y, at : at + 16, :] = sums[:, y * HALF : (y + 1) * HALF]
                dst[y, at + 16 :, :] = jnp.zeros((FFN_G - at - 16, HALF), bf16)

        core = s_ref[3]
        for c in range(2):

            @pl.when(core == c)
            def _():
                write(keep, c)
                write(send, 1 - c)

        for y in range(2):
            for j in range(2):
                packed_dr[y, :, j * BS : (j + 1) * BS] = gdr[2 * y + j].astype(bf16)


def dense(scalars, middle, own, oth, cols, weights):
    row_count = own.shape[0] // 2
    steps = row_count // TILE

    def own_rows(i, s):
        return (s[0] * steps + i, 0)

    ins = [middle, own, oth, cols] + list(weights)
    in_specs = [
        pl.BlockSpec((D, TILE), lambda i, s: (0, i)),
        pl.BlockSpec((TILE, HALF), own_rows),
        pl.BlockSpec((TILE, HALF), lambda i, s: (i, 0)),
        whole(cols.shape),
    ] + [whole(item.shape) for item in weights]
    half_shape = (2, FFN_G, HALF)
    outs = [
        jax.ShapeDtypeStruct((2 * row_count, HALF), bf16),
        jax.ShapeDtypeStruct((row_count, HALF), bf16),
        jax.ShapeDtypeStruct((D, row_count), f32),
        jax.ShapeDtypeStruct(half_shape, bf16),
        jax.ShapeDtypeStruct(half_shape, bf16),
        jax.ShapeDtypeStruct((2, BS, HALF), bf16),
    ]
    out_specs = [
        pl.BlockSpec((TILE, HALF), own_rows),
        pl.BlockSpec((TILE, HALF), lambda i, s: (i, 0)),
        pl.BlockSpec((D, TILE), lambda i, s: (0, i)),
        whole(half_shape),
        whole(half_shape),
        whole((2, BS, HALF)),
    ]
    full = [(NB, BS, BS), (NB, BS, 2 * FB), (NB, BS, FB), (NB, BS, BS)]
    scratch = [pltpu.VMEM(shape, bf16) for shape in full]
    scratch += [pltpu.VMEM(shape, f32) for shape in ACC_SHAPES]
    scratch += [pltpu.VMEM((D, TILE), bf16) for _ in range(4)]
    scratch += [pltpu.VMEM((NB * FB, TILE), bf16) for _ in range(3)]
    scratch += [pltpu.VMEM((2 * FB, TILE), bf16)]
    scratch += [pltpu.VMEM((D, TILE), bf16) for _ in range(2)]
    return pl.pallas_call(
        functools.partial(dense_kernel, steps=steps),
        out_shape=tuple(outs),
        grid_spec=pltpu.PrefetchScalarGridSpec(
            num_scalar_prefetch=1,
            grid=(steps,),
            in_specs=in_specs,
            out_specs=tuple(out_specs),
            scratch_shapes=scratch,
        ),
        compiler_params=pltpu.CompilerParams(vmem_limit_bytes=VMEM),
        name="dense",
        cost_estimate=pl.CostEstimate(
            flops=row_count * 2 * 8000000, bytes_accessed=row_count * 10000, transcendentals=0
        ),
    )(scalars, *ins)


BACK_SHAPES = (
    (NB, BS, BS),
    (NB, BS, BS),
    (D, LEN),
    (D, 2 * LEN),
    (NB, BS, 3 * BS),
    (NB, BS, BS),
    (D, LEN),
    (D, LEN),
)


def mixer_backward_kernel(
    s_ref,
    grad_middle,
    first,
    kept,
    scale,
    marks,
    cols,
    spec,
    fwd,
    inv,
    wil,
    wir,
    wol,
    wor,
    taps,
    feats,
    packed_dr,
    out_own,
    out_send,
    keep,
    send,
    gol,
    gor,
    gskip,
    gspec,
    gir,
    gil,
    gmask,
    ggain,
    back,
    half,
    conv,
    inner_grad,
    total,
    proj,
    *,
    steps,
    share,
):
    side = s_ref[0]

    @pl.when(pl.program_id(0) == 0)
    def _():
        for acc in (gol, gor, gskip, gspec, gir, gil, gmask, ggain):
            acc[...] = jnp.zeros(acc.shape, f32)

    valid = marks[0:1, :]
    half[...] = grad_middle[...].astype(bf16)
    for g in range(NB):
        grad = block(half, g)
        regroup(back, g, nn(wor[g], grad).astype(bf16))
        gor[g] += nt(block(kept.at[4], g), grad)
    for b in range(NB):
        rows = slice(b * BS, (b + 1) * BS)
        returned = block(back, b)
        grad_mixed = nn(wol[b], returned)
        gate = kept[1, rows, :].astype(f32)
        inner = kept[3, rows, :].astype(f32)
        gol[b] += nt((gate * inner).astype(bf16), returned)
        grad_inner = grad_mixed * gate
        inner_grad[rows, :] = grad_inner
        conv[rows, :] = grad_inner.astype(bf16)
        proj[b * 3 * BS + BS : b * 3 * BS + 2 * BS, :] = (grad_mixed * inner).astype(bf16)
        source = (
            kept[0, rows, :].astype(f32) * kept[2, rows, :].astype(f32) * valid
        ).astype(bf16)
        half[rows, :] = source
        gskip[rows, :] += fold(grad_inner * source.astype(f32))
    hc, hs = spec[:, :LEN], spec[:, LEN:]
    for s in range(BACK_TILE // LEN):
        lanes = slice(s * LEN, (s + 1) * LEN)
        wave = nn(conv[:, lanes], fwd[...])
        wc, ws = wave[:, :LEN], wave[:, LEN:]
        seen = nn(half[:, lanes], fwd[...])
        sc, ss = seen[:, :LEN], seen[:, LEN:]
        gspec[:, :LEN] += wc * sc + ws * ss
        gspec[:, LEN:] += ws * sc - wc * ss
        product = jnp.concatenate(
            [(wc * hc + ws * hs).astype(bf16), (ws * hc - wc * hs).astype(bf16)], axis=1
        )
        total[:, lanes] = nn(product, inv[...])
    for g in range(NB):
        rows = slice(g * BS, (g + 1) * BS)
        grad_source = (total[rows, :] + cols[rows, 3:4] * inner_grad[rows, :]) * valid
        start = g * 3 * BS
        proj[start : start + BS, :] = (grad_source * kept[2, rows, :].astype(f32)).astype(bf16)
        proj[start + 2 * BS : start + 3 * BS, :] = (
            grad_source * kept[0, rows, :].astype(f32)
        ).astype(bf16)

    masked = marks[1:2, :]
    for g in range(NB):
        grad = proj[g * 3 * BS : (g + 1) * 3 * BS, :]
        regroup(back, g, nn(wir[g], grad).astype(bf16))
        gir[g] += nt(block(first.at[1], g), grad)
    gain = column(cols, 1)
    grads = []
    for b in range(NB):
        returned = block(back, b)
        grads.append(nn(wil[b], returned))
        gil[b] += nt(block(first.at[0], b), returned)
    grad_in = jnp.concatenate(grads, axis=0)
    normed = first[0].astype(f32) * (1.0 / gain)
    ggain[...] += fold(grad_in * normed)
    entered = grad_middle[...] + norm_back(grad_in, normed, scale[0:1, :], gain)
    gmask[...] += fold(entered * masked)
    total[...] = entered * (1.0 - masked)
    out_own[...] = total[rows_of(side, HALF), :].T
    out_send[...] = total[rows_of(1 - side, HALF), :].astype(bf16).T

    @pl.when(pl.program_id(0) == steps - 1)
    def _():
        spectrum = gspec[...]
        high = spectrum.astype(bf16)
        low = (spectrum - high.astype(f32)).astype(bf16)
        grad_taps = nn(high, inv[...]) + nn(low, inv[...])
        tap = taps[...]
        grad_taps = grad_taps + tap * (2.0 * penalty_weight * share)
        positions = lax.broadcasted_iota(jnp.int32, (1, LEN), 1).astype(f32)
        decayed = grad_taps * jnp.exp(-column(cols, 4) * positions)
        high = decayed.astype(bf16)
        low = (decayed - high.astype(f32)).astype(bf16)
        sum_weight = (nt(feats[0], high) + nt(feats[1], high) + nt(feats[0], low)).astype(bf16)
        grad_decay = grad_taps * tap * (-positions)
        ones = jnp.ones((16, LEN), f32)
        line = lax.broadcasted_iota(jnp.int32, (16, D), 0)
        vectors = exact_nt(ones, gmask[...])
        vectors = jnp.where(line == 1, exact_nt(ones, ggain[...]), vectors)
        vectors = jnp.where(line == 2, exact_nt(ones, gskip[...]), vectors)
        vectors = jnp.where(line == 3, exact_nt(ones, grad_decay), vectors).astype(bf16)

        def write(dst, j):
            part = BS // 2
            few = ORDER // 2
            for y in range(2):
                lanes = slice(y * HALF, (y + 1) * HALF)
                b = 2 * y + j
                dst[y, 0:BS, :] = gir[b, :, :HALF].astype(bf16)
                dst[y, BS : 2 * BS, 0:BS] = gir[b, :, HALF:].astype(bf16)
                dst[y, BS : 2 * BS, BS:] = gil[b].astype(bf16)
                dst[y, 2 * BS : 3 * BS, 0:BS] = gol[b].astype(bf16)
                dst[y, 2 * BS : 3 * BS, BS:] = gor[b].astype(bf16)
                at = 3 * BS
                dst[y, at : at + part, :] = packed_dr[y, j * part : (j + 1) * part, :]
                at += part
                dst[y, at : at + few, :] = sum_weight[j * few : (j + 1) * few, lanes]
                at += few
                dst[y, at : at + 16, :] = vectors[:, lanes]
                dst[y, at + 16 :, :] = jnp.zeros((MIX_G - at - 16, HALF), bf16)

        core = s_ref[3]
        for c in range(2):

            @pl.when(core == c)
            def _():
                write(keep, c)
                write(send, 1 - c)


def mixer_backward(share, scalars, streams, constants, weights, finals):
    row_count = streams[0].shape[1]
    steps = row_count // BACK_TILE
    ins = list(streams) + list(constants) + list(weights) + list(finals)
    in_specs = [
        pl.BlockSpec((D, BACK_TILE), lambda i, s: (0, i)),
        pl.BlockSpec((2, D, BACK_TILE), lambda i, s: (0, 0, i)),
        pl.BlockSpec((5, D, BACK_TILE), lambda i, s: (0, 0, i)),
        pl.BlockSpec((8, BACK_TILE), lambda i, s: (0, i)),
        pl.BlockSpec((8, BACK_TILE), lambda i, s: (0, i)),
    ] + [whole(item.shape) for item in ins[5:]]
    half_shape = (2, MIX_G, HALF)
    outs = [
        jax.ShapeDtypeStruct((2 * row_count, HALF), f32),
        jax.ShapeDtypeStruct((row_count, HALF), bf16),
        jax.ShapeDtypeStruct(half_shape, bf16),
        jax.ShapeDtypeStruct(half_shape, bf16),
    ]
    out_specs = [
        pl.BlockSpec((BACK_TILE, HALF), lambda i, s: (s[0] * steps + i, 0)),
        pl.BlockSpec((BACK_TILE, HALF), lambda i, s: (i, 0)),
        whole(half_shape),
        whole(half_shape),
    ]
    scratch = [pltpu.VMEM(shape, f32) for shape in BACK_SHAPES]
    scratch += [
        pltpu.VMEM((D, BACK_TILE), bf16),
        pltpu.VMEM((D, BACK_TILE), bf16),
        pltpu.VMEM((D, BACK_TILE), bf16),
        pltpu.VMEM((D, BACK_TILE), f32),
        pltpu.VMEM((D, BACK_TILE), f32),
        pltpu.VMEM((3 * D, BACK_TILE), bf16),
    ]
    return pl.pallas_call(
        functools.partial(mixer_backward_kernel, steps=steps, share=share),
        out_shape=tuple(outs),
        grid_spec=pltpu.PrefetchScalarGridSpec(
            num_scalar_prefetch=1,
            grid=(steps,),
            in_specs=in_specs,
            out_specs=tuple(out_specs),
            scratch_shapes=scratch,
        ),
        compiler_params=pltpu.CompilerParams(vmem_limit_bytes=VMEM),
        name="mixer_backward",
        cost_estimate=pl.CostEstimate(
            flops=row_count * 2 * 6000000, bytes_accessed=row_count * 20000, transcendentals=0
        ),
    )(scalars, *ins)


def place_parts(s_ref, parts, halves):
    quarter = parts[0].shape[0]
    few = quarter // 4
    for where, part in enumerate(parts):
        core = jnp.bitwise_xor(s_ref[3], where >> 1)
        start = jnp.bitwise_xor(s_ref[4], where & 1) * quarter
        for k in range(4):
            row = pl.multiple_of(start + jnp.bitwise_xor(s_ref[5], k) * few, few)
            halves[core, pl.ds(row, few), :] = part[k * few : (k + 1) * few, :]


def dense_unpack_kernel(s_ref, p0, p1, p2, p3, gain, ul, ur, dl, halves):
    place_parts(s_ref, (p0, p1, p2, p3), halves)
    part = BS // 2
    at = 6 * BS
    gain[...] = halves[0, at + part : at + part + 16, :].astype(f32)[0]
    for j in range(2):
        for c in range(4):
            ur[j, :, c * HALF : (c + 1) * HALF] = halves[j, c * BS : (c + 1) * BS, :].astype(f32)
        for c in range(2):
            dl[j, :, c * HALF : (c + 1) * HALF] = halves[
                j, (4 + c) * BS : (5 + c) * BS, :
            ].astype(f32)
        for lane in range(2):
            ul[lane, j * part : (j + 1) * part, :] = halves[
                j, at : at + part, lane * BS : (lane + 1) * BS
            ].astype(f32)


def mixer_unpack_kernel(s_ref, p0, p1, p2, p3, mask, gain, skip, decay, weight, il, ir, ol, orr, dr, halves):
    place_parts(s_ref, (p0, p1, p2, p3), halves)
    part = BS // 2
    few = ORDER // 2
    at = 3 * BS
    vectors = halves[0, at + part + few : at + part + few + 16, :].astype(f32)
    for index, dst in enumerate((mask, gain, skip, decay)):
        dst[...] = vectors[index]
    for j in range(2):
        ir[j, :, :HALF] = halves[j, 0:BS, :].astype(f32)
        ir[j, :, HALF:] = halves[j, BS : 2 * BS, :BS].astype(f32)
        il[j] = halves[j, BS : 2 * BS, BS:].astype(f32)
        ol[j] = halves[j, 2 * BS : 3 * BS, :BS].astype(f32)
        orr[j] = halves[j, 2 * BS : 3 * BS, BS:].astype(f32)
        for lane in range(2):
            dr[lane, j * part : (j + 1) * part, :] = halves[
                j, at : at + part, lane * BS : (lane + 1) * BS
            ].astype(f32)
        weight[j * few : (j + 1) * few, :] = halves[
            j, at + part : at + part + few, :
        ].astype(f32)


def unpack(kernel, scalars, parts, shapes, name):
    outs = tuple(jax.ShapeDtypeStruct(shape, f32) for shape in shapes)
    rows = 2 * parts[0].shape[0]
    return pl.pallas_call(
        kernel,
        out_shape=outs,
        grid_spec=pltpu.PrefetchScalarGridSpec(
            num_scalar_prefetch=1,
            grid=(1,),
            in_specs=[whole(item.shape) for item in parts],
            out_specs=tuple(whole(shape) for shape in shapes),
            scratch_shapes=[pltpu.VMEM((2, rows, HALF), bf16)],
        ),
        compiler_params=pltpu.CompilerParams(vmem_limit_bytes=VMEM),
        name=name,
    )(scalars, *parts)


DENSE_OUTS = ((HALF,), (2, BS, BS), (2, BS, 2 * FB), (2, BS, FB))
MIXER_OUTS = (
    (HALF,),
    (HALF,),
    (HALF,),
    (HALF,),
    (ORDER, HALF),
    (2, BS, BS),
    (2, BS, 3 * BS),
    (2, BS, BS),
    (2, BS, BS),
    (2, BS, BS),
)


def corners_kernel(s_ref, *refs):
    for index in range(4):
        kept, got, out = refs[index], refs[4 + index], refs[8 + index]
        out[...] = (kept[...].astype(f32) + got[...].astype(f32)).astype(bf16)


def corners(scalars, kept, got):
    rows = kept.shape[1] // 2
    shape = jax.ShapeDtypeStruct((rows, HALF), bf16)

    def spec(over_y, over_x):
        def at(i, s):
            y = 1 - s[0] if over_y else s[0]
            x = 1 - s[4] if over_x else s[4]
            return (y, x, 0)

        return pl.BlockSpec((None, rows, HALF), at)

    specs = [spec(False, False), spec(False, True), spec(True, False), spec(True, True)]
    return pl.pallas_call(
        corners_kernel,
        out_shape=(shape,) * 4,
        grid_spec=pltpu.PrefetchScalarGridSpec(
            num_scalar_prefetch=1,
            grid=(1,),
            in_specs=specs + specs,
            out_specs=(whole((rows, HALF)),) * 4,
        ),
        compiler_params=pltpu.CompilerParams(vmem_limit_bytes=VMEM),
        name="sum_corners",
    )(scalars, *([kept] * 4 + [got] * 4))


def columns_kernel(s_ref, a, b, c, d, own, one, two, three, total):
    total[...] = (
        a[...].astype(f32) + b[...].astype(f32) + c[...].astype(f32) + d[...].astype(f32)
    )
    few = total.shape[0] // 4
    for k, out in enumerate((own, one, two, three)):
        row = pl.multiple_of(jnp.bitwise_xor(s_ref[5], k) * few, few)
        out[...] = total[pl.ds(row, few), :].astype(bf16)


def columns(scalars, parts):
    rows = parts[0].shape[0]
    shape = jax.ShapeDtypeStruct((rows // 4, HALF), bf16)
    return pl.pallas_call(
        columns_kernel,
        out_shape=(shape,) * 4,
        grid_spec=pltpu.PrefetchScalarGridSpec(
            num_scalar_prefetch=1,
            grid=(1,),
            in_specs=[whole((rows, HALF))] * 4,
            out_specs=(whole((rows // 4, HALF)),) * 4,
            scratch_shapes=[pltpu.VMEM((rows, HALF), f32)],
        ),
        compiler_params=pltpu.CompilerParams(vmem_limit_bytes=VMEM),
        name="sum_columns",
    )(scalars, *parts)


def swap_narrow(values):
    return lax.ppermute(values, "narrow", [(0, 1), (1, 0)])


def swap_wide(values, bit, size):
    return lax.ppermute(values, "wide", [(i, i ^ (1 << bit)) for i in range(size)])


def swap_both(values, bit, size):
    flip = 2 << bit
    return lax.ppermute(
        values, ("wide", "narrow"), [(i, i ^ flip ^ 1) for i in range(2 * size)]
    )


def shift_wide(values, flip, size):
    return lax.ppermute(values, "wide", [(i, i ^ flip) for i in range(size)])


def add_low(*items):
    total = items[0].astype(f32)
    for item in items[1:]:
        total = total + item.astype(f32)
    return total.astype(bf16)


def over_corners(parts, size):
    own, over_x, over_y, over_both = parts
    return (
        own,
        swap_wide(over_x, 1, size),
        swap_narrow(over_y),
        swap_both(over_both, 1, size),
    )


def over_columns(parts, size):
    own, *others = parts
    packed = add_low(
        own, *(shift_wide(item, (k + 1) << 2, size) for k, item in enumerate(others))
    )
    bit = 4
    while 1 << bit < size:
        packed = add_low(packed, swap_wide(packed, bit, size))
        bit += 1
    return jnp.concatenate(
        [packed] + [shift_wide(packed, k << 2, size) for k in (1, 2, 3)], axis=0
    )


def over_rows(near, size):
    far = swap_wide(near, 1, size)
    return (near, far, swap_wide(near, 0, size), swap_wide(far, 0, size))


def gather_pieces(piece, bits, size):
    pieces = [swap_narrow(piece)]
    for bit in bits:
        pieces = pieces + [swap_wide(item, bit, size) for item in pieces]
    return pieces


def on_device(
    wide_size,
    tokens,
    lengths,
    mask_pos,
    mask_vector,
    norm1_gain,
    in_left,
    in_right,
    filter_weight,
    decay,
    skip_gain,
    out_left,
    out_right,
    norm2_gain,
    up_left,
    up_right,
    down_left,
    down_right,
    cotangent,
):
    index = lax.axis_index("wide")
    side = lax.axis_index("narrow")
    row_count = tokens.shape[0] // 2
    scalars = jnp.stack(
        [side, index & 3, (index >> 2) & 1, index & 1, (index >> 1) & 1, (index >> 2) & 3]
    ).astype(jnp.int32)
    share = 1.0 / (2 * wide_size)

    def sent_rows(values):
        return lax.dynamic_slice_in_dim(values, (1 - side) * row_count, row_count, 0)

    mixer_weights = (in_left, in_right, out_left, out_right)
    dense_weights = (up_left, up_right, jnp.swapaxes(down_left, 1, 2), down_right)
    vectors = (mask_vector, norm1_gain, norm2_gain, skip_gain, decay)
    mix_piece, ffn_piece = pack_weights(
        scalars, mixer_weights, dense_weights, filter_weight, vectors
    )
    first, third = gather_pieces(mix_piece, (1,), wide_size)
    mix_pieces = (first, swap_wide(first, 0, wide_size), third, swap_wide(third, 0, wide_size))
    y0, z0, x0, xz0 = gather_pieces(ffn_piece, (2, 1), wide_size)
    ffn_pieces = tuple(
        piece
        for near in ((y0, x0), (z0, xz0))
        for item in near
        for piece in (item, swap_wide(item, 0, wide_size))
    )
    tokens_other = swap_narrow(sent_rows(tokens))
    cot_other = swap_narrow(sent_rows(cotangent))

    positions = jnp.arange(LEN, dtype=jnp.int32)
    valid = (positions[None, :] < lengths[:, None]).astype(f32)
    masked = jnp.any(mask_pos[:, :, None] == positions[None, None, :], axis=1).astype(f32)
    marks = jnp.stack([valid, masked]).reshape(2, 2, row_count)
    marks = lax.dynamic_index_in_dim(marks, side, 1, keepdims=False)
    marks = jnp.concatenate([marks, jnp.zeros((6, row_count), f32)], axis=0)

    fwd, inv = (jnp.asarray(item) for item in transform_tables())
    feats = jnp.asarray(feature_parts())
    taps, spec, penalty, cols = filter_call(
        scalars, filter_weight, mix_piece, mix_pieces, feats, fwd
    )

    middle, first, kept, scale, *full = mixer_forward(
        scalars, tokens, tokens_other, marks, cols, spec, fwd, inv, mixer_weights + mix_pieces
    )
    output, output_sent, grad_middle, ffn_keep, ffn_send, packed_dr = dense(
        scalars, middle, cotangent, cot_other, cols, dense_weights + ffn_pieces
    )
    output_other = swap_narrow(output_sent)
    ffn_parts = corners(scalars, ffn_keep, swap_wide(ffn_send, 0, wide_size))
    grad_middle, *ffn_parts = lax.optimization_barrier((grad_middle, *ffn_parts))
    ffn_parts = over_corners(ffn_parts, wide_size)
    tokens_grad, grad_sent, mix_keep, mix_send = mixer_backward(
        share,
        scalars,
        (grad_middle, first, kept, scale, marks),
        (cols, spec, fwd, inv),
        full,
        (taps, feats, packed_dr),
    )
    mix_keep, mix_send, output_other, *ffn_parts = lax.optimization_barrier(
        (mix_keep, mix_send, output_other, *ffn_parts)
    )
    mix_parts = corners(scalars, mix_keep, swap_wide(mix_send, 0, wide_size))
    ffn_parts = columns(scalars, ffn_parts)
    mix_parts = columns(scalars, over_corners(mix_parts, wide_size))
    grad_sent, *mix_parts = lax.optimization_barrier((grad_sent, *mix_parts))
    grad_other = swap_narrow(grad_sent)
    ffn_near = over_columns(ffn_parts, wide_size)
    mix_near = over_columns(mix_parts, wide_size)
    ffn_parts = over_rows(ffn_near, wide_size)
    mix_near, grad_other = lax.optimization_barrier((mix_near, grad_other))
    mix_parts = over_rows(mix_near, wide_size)
    gain_two, g_ul, g_ur, g_dl = unpack(
        dense_unpack_kernel, scalars, ffn_parts, DENSE_OUTS, "dense_unpack"
    )
    g_mask, g_gain, g_skip, g_decay, g_filter, g_il, g_ir, g_ol, g_or, g_dr = unpack(
        mixer_unpack_kernel, scalars, mix_parts, MIXER_OUTS, "mixer_unpack"
    )
    start = (1 - side) * row_count
    output = lax.dynamic_update_slice_in_dim(output, output_other, start, 0)
    tokens_grad = lax.dynamic_update_slice_in_dim(tokens_grad, grad_other.astype(f32), start, 0)
    return (
        output,
        tokens_grad,
        g_mask,
        g_gain,
        g_il,
        g_ir,
        g_filter,
        g_decay,
        g_skip,
        g_ol,
        g_or,
        gain_two,
        g_ul,
        g_ur,
        jnp.swapaxes(g_dl, 1, 2),
        g_dr,
        penalty[0, 0],
    )


def solution(mesh):
    placed = (
        P("wide", "narrow"),
        P("wide"),
        P("wide", None),
        P("narrow"),
        P("narrow"),
        P("narrow", None, None),
        P("narrow", None, None),
        P(None, "narrow"),
        P("narrow"),
        P("narrow"),
        P("narrow", None, None),
        P("narrow", None, None),
        P("narrow"),
        P("narrow", None, None),
        P("narrow", None, None),
        P("narrow", None, None),
        P("narrow", None, None),
        P("wide", "narrow"),
    )
    return jax.shard_map(
        functools.partial(on_device, mesh.shape["wide"]),
        mesh=mesh,
        in_specs=placed,
        out_specs=(
            P("wide", "narrow"),
            P("wide", "narrow"),
            P("narrow"),
            P("narrow"),
            P("narrow", None, None),
            P("narrow", None, None),
            P(None, "narrow"),
            P("narrow"),
            P("narrow"),
            P("narrow", None, None),
            P("narrow", None, None),
            P("narrow"),
            P("narrow", None, None),
            P("narrow", None, None),
            P("narrow", None, None),
            P("narrow", None, None),
            P(),
        ),
        check_vma=False,
    )
```

profile of v0, /device:TPU:0, one launch (start us, length us, event | category | flops | bytes accessed | tf_op | source)
XLA Modules:
  0.0 200.8 jit_solution(14910664517362103002)
XLA Ops:
  1.3 2.9 %pack_weights.1 = (bf16[336,384]{1,0:T(8,128)(2,1)}, bf16[336,384]{1,0:T(8,128)(2,1)}) custom-call(s32[6]{0:T(128)} %stack.34.s_ref, bf16[2,192,192]{2,1,0:T(8,128)(2,1)} %il.3, bf16[2,192,576]{2,1,0:T(8,128)(2,1)} %ir.3, bf16[2,192,192]{2,1,0:T(8,128)(2,1)} %ol.3, bf16[2,192,192]{2,1,0:T(8,128)(2,1)} %orr.3, bf16[2,192,192]{2,1,0:T(8,128)(2,1)} %ul.3, ...), custom_call_target="tpu_custom_call" | custom-call | tf_op jit(solution)/shard_map/pack_weights/pallas_call | solution.py:165
  4.2 3.0 %collective-permute-start.1 = (bf16[336,384]{1,0:T(8,128)(2,1)}, bf16[336,384]{1,0:T(8,128)(2,1)S(1)}, u32[]{:S(2)}, u32[]{:S(2)}) collective-permute-start(bf16[336,384]{1,0:T(8,128)(2,1)} %get-tuple-element.90.mine), channel_id=1, source_target_pairs={{0,1},{1,0},{2,3},{3,2},{4,5},{5,4},{6,7},{7,6},{8,9},{9,8},{10,11... | collective-permute-start | bytes 774152 | tf_op jit(solution)/shard_map/ppermute | solution.py:960
  7.3 2.0 %collective-permute-start = (bf16[1024,384]{1,0:T(8,128)(2,1)S(1)}, bf16[1024,384]{1,0:T(8,128)(2,1)}, u32[]{:S(2)}, u32[]{:S(2)}) collective-permute-start(bf16[1024,384]{1,0:T(8,128)(2,1)S(1)} %constant_dynamic-slice_fusion.1), channel_id=1, source_target_pairs={{0,1},{1,0},{2,3},{3,2},{4,5},{5,4},{6,7},{7,6},{8,9},{9,8},{10,11... | collective-permute-start | bytes 2359304 | tf_op jit(solution)/shard_map/ppermute | solution.py:960
  9.4 5.1 %collective-permute-done.1.p0 = bf16[336,384]{1,0:T(8,128)(2,1)S(1)} collective-permute-done((bf16[336,384]{1,0:T(8,128)(2,1)}, bf16[336,384]{1,0:T(8,128)(2,1)S(1)}, u32[]{:S(2)}, u32[]{:S(2)}) %collective-permute-start.1) | collective-permute-done | bytes 258080 | tf_op jit(solution)/shard_map/ppermute | solution.py:960
  14.4 2.0 %collective-permute-start.3 = (bf16[336,384]{1,0:T(8,128)(2,1)S(1)}, bf16[336,384]{1,0:T(8,128)(2,1)S(1)}, u32[]{:S(2)}, u32[]{:S(2)}) collective-permute-start(bf16[336,384]{1,0:T(8,128)(2,1)S(1)} %collective-permute-done.1.p0), channel_id=1, source_target_pairs={{0,4},{2,6},{4,0},{6,2},{8,12},{10,14},{12,8},{14,10},{16,20},{18,... | collective-permute-start | bytes 774152 | tf_op jit(solution)/shard_map/ppermute | solution.py:964
  16.5 3.6 %collective-permute-done.6.p0 = bf16[336,384]{1,0:T(8,128)(2,1)} collective-permute-done((bf16[336,384]{1,0:T(8,128)(2,1)}, bf16[336,384]{1,0:T(8,128)(2,1)}, u32[]{:S(2)}, u32[]{:S(2)}) %collective-permute-start.6) | collective-permute-done | bytes 258080 | tf_op jit(solution)/shard_map/ppermute | solution.py:960
  20.1 2.1 %collective-permute-start.10 = (bf16[336,384]{1,0:T(8,128)(2,1)}, bf16[336,384]{1,0:T(8,128)(2,1)S(1)}, u32[]{:S(2)}, u32[]{:S(2)}) collective-permute-start(bf16[336,384]{1,0:T(8,128)(2,1)} %collective-permute-done.6.p0), channel_id=1, source_target_pairs={{0,8},{2,10},{4,12},{6,14},{8,0},{10,2},{12,4},{14,6},{16,24},{18,... | collective-permute-start | bytes 774152 | tf_op jit(solution)/shard_map/ppermute | solution.py:964
  31.1 3.9 %filter_spectrum.1 = (f32[768,128]{1,0:T(8,128)}, f32[768,256]{1,0:T(8,128)}, f32[8,128]{1,0:T(8,128)}, f32[768,128]{1,0:T(8,128)}) custom-call(s32[6]{0:T(128)} %stack.34.s_ref, bf16[128,384]{1,0:T(8,128)(2,1)} %own.3, bf16[336,384]{1,0:T(8,128)(2,1)} %get-tuple-element.90.mine, bf16[336,384]{1,0:T(8,128)(2,1)} %copy-done.15, bf16[336,384]{1,0:T(8,128)(2,1)} %copy-done.17, ...), custom_call_target="tpu_custom_call" | custom-call | tf_op jit(solution)/shard_map/filter_spectrum/pallas_call | solution.py:234
  35.5 2.8 %collective-permute-done.12.p6 = bf16[336,384]{1,0:T(8,128)(2,1)S(1)} collective-permute-done((bf16[336,384]{1,0:T(8,128)(2,1)S(1)}, bf16[336,384]{1,0:T(8,128)(2,1)S(1)}, u32[]{:S(2)}, u32[]{:S(2)}) %collective-permute-start.12) | collective-permute-done | bytes 258080 | tf_op jit(solution)/shard_map/ppermute | solution.py:964
  38.8 12.6 %mixer_forward.1 = (f32[768,1024]{1,0:T(8,128)}, bf16[2,768,1024]{2,1,0:T(8,128)(2,1)}, bf16[5,768,1024]{2,1,0:T(8,128)(2,1)}, f32[8,1024]{1,0:T(8,128)}, bf16[4...) custom-call(s32[6]{0:T(128)} %stack.34.s_ref, ...), custom_call_target="tpu_custom_call" | custom-call | flops 3072000000 | bytes 20480000 | tf_op jit(solution)/shard_map/mixer_forward/pallas_call | solution.py:358
  53.7 32.0 %dense.1 = (bf16[2048,384]{1,0:T(8,128)(2,1)}, bf16[1024,384]{1,0:T(8,128)(2,1)}, f32[768,1024]{1,0:T(8,128)}, bf16[2,1280,384]{2,1,0:T(8,128)(2,1)}, bf16[2,128...) custom-call(s32[6]{0:T(128)} %stack.34.s_ref, f32[768,1024]{1,0:T(8,128)} %get-tuple-element.93.middle, ...), custom_call_target="tpu_custom_call" | custom-call | flops 16384000000 | bytes 10240000 | tf_op jit(solution)/shard_map/dense/pallas_call | solution.py:572
  85.8 1.8 collective-permute-start.15
  87.6 2.3 %collective-permute-done.14.refs_4_.refs_5_.refs_6_.refs_7_ = bf16[2,1280,384]{2,1,0:T(8,128)(2,1)S(1)} collective-permute-done((bf16[2,1280,384]{2,1,0:T(8,128)(2,1)}, bf16[2,1280,384]{2,1,0:T(8,128)(2,1)S(1)}, u32[]{:S(2)}, u32[]{:S(2)}) %collective-permute-start.14) | collective-permute-done | bytes 1966112 | tf_op jit(solution)/shard_map/ppermute | solution.py:964
  91.2 4.1 %sum_corners.2 = (bf16[640,384]{1,0:T(8,128)(2,1)}, bf16[640,384]{1,0:T(8,128)(2,1)}, bf16[640,384]{1,0:T(8,128)(2,1)}, bf16[640,384]{1,0:T(8,128)(2,1)}) custom-call(s32[6]{0:T(128)} %stack.34.s_ref, bf16[2,1280,384]{2,1,0:T(8,128)(2,1)} %get-tuple-element.97.refs_0_.refs_1_.refs_2_.refs_3_, ...), custom_call_target="tpu_custom_call" | custom-call | tf_op jit(solution)/shard_map/sum_corners/pallas_call | solution.py:917
  98.8 21.4 %mixer_backward.1 = (f32[2048,384]{1,0:T(8,128)}, bf16[1024,384]{1,0:T(8,128)(2,1)}, bf16[2,768,384]{2,1,0:T(8,128)(2,1)}, bf16[2,768,384]{2,1,0:T(8,128)(2,1)}) custom-call(s32[6]{0:T(128)} %stack.34.s_ref, f32[768,1024]{1,0:T(8,128)} %get-tuple-element.103.grad_middle, bf16[2,768,1024]{2,1,0:T(8,128)(2,1)} %get-tuple-element.104.first, ...), custom_call_target="tpu_custom_call" | custom-call | flops 12288000000 | bytes 20480000 | tf_op jit(solution)/shard_map/mixer_backward/pallas_call | solution.py:795
  120.2 6.8 %collective-permute-done.17.c = bf16[640,384]{1,0:T(8,128)(2,1)S(1)} collective-permute-done((bf16[640,384]{1,0:T(8,128)(2,1)}, bf16[640,384]{1,0:T(8,128)(2,1)S(1)}, u32[]{:S(2)}, u32[]{:S(2)}) %collective-permute-start.17) | collective-permute-done | bytes 491552 | tf_op jit(solution)/shard_map/ppermute | solution.py:960
  127.9 3.3 %sum_columns.3 = (bf16[160,384]{1,0:T(8,128)(2,1)}, bf16[160,384]{1,0:T(8,128)(2,1)}, bf16[160,384]{1,0:T(8,128)(2,1)}, bf16[160,384]{1,0:T(8,128)(2,1)}) custom-call(s32[6]{0:T(128)} %stack.34.s_ref, bf16[640,384]{1,0:T(8,128)(2,1)} %get-tuple-element.149.a, bf16[640,384]{1,0:T(8,128)(2,1)} %copy-done.6, bf16[640,384]{1,0:T(8,128)(2,1)} %copy-done.7, ...), custom_call_target="tpu_custom_call" | custom-call | tf_op jit(solution)/shard_map/sum_columns/pallas_call | solution.py:944
  131.2 1.8 collective-permute-start.33
  133.0 2.6 %collective-permute-start.34 = (bf16[160,384]{1,0:T(8,128)(2,1)}, bf16[160,384]{1,0:T(8,128)(2,1)S(1)}, u32[]{:S(2)}, u32[]{:S(2)}) collective-permute-start(bf16[160,384]{1,0:T(8,128)(2,1)} %get-tuple-element.155), channel_id=1, source_target_pairs={{0,16},{2,18},{4,20},{6,22},{8,24},{10,26},{12,28},{14,30},{16,0},... | collective-permute-start | bytes 368648 | tf_op jit(solution)/shard_map/ppermute | solution.py:975
  136.6 3.3 %sum_corners.3 = (bf16[384,384]{1,0:T(8,128)(2,1)}, bf16[384,384]{1,0:T(8,128)(2,1)}, bf16[384,384]{1,0:T(8,128)(2,1)}, bf16[384,384]{1,0:T(8,128)(2,1)}) custom-call(s32[6]{0:T(128)} %stack.34.s_ref, bf16[2,768,384]{2,1,0:T(8,128)(2,1)} %get-tuple-element.123.refs_0_.refs_1_.refs_2_.refs_3_, ...), custom_call_target="tpu_custom_call" | custom-call | tf_op jit(solution)/shard_map/sum_corners/pallas_call | solution.py:917
  143.5 1.9 collective-permute-done.34
  145.4 2.5 %collective-permute-start.38 = (bf16[160,384]{1,0:T(8,128)(2,1)S(1)}, bf16[160,384]{1,0:T(8,128)(2,1)S(1)}, u32[]{:S(2)}, u32[]{:S(2)}) collective-permute-start(bf16[160,384]{1,0:T(8,128)(2,1)S(1)} %add_convert_fusion), channel_id=1, source_target_pairs={{0,24},{2,26},{4,28},{6,30},{8,16},{10,18},{12,20},{14,22},{16,8},... | collective-permute-start | bytes 368648 | tf_op jit(solution)/shard_map/ppermute | solution.py:975
  151.0 4.7 %collective-permute-done.21.c = bf16[384,384]{1,0:T(8,128)(2,1)S(1)} collective-permute-done((bf16[384,384]{1,0:T(8,128)(2,1)}, bf16[384,384]{1,0:T(8,128)(2,1)S(1)}, u32[]{:S(2)}, u32[]{:S(2)}) %collective-permute-start.21) | collective-permute-done | bytes 294944 | tf_op jit(solution)/shard_map/ppermute | solution.py:960
  156.5 2.8 %sum_columns.2 = (bf16[96,384]{1,0:T(8,128)(2,1)}, bf16[96,384]{1,0:T(8,128)(2,1)}, bf16[96,384]{1,0:T(8,128)(2,1)}, bf16[96,384]{1,0:T(8,128)(2,1)}) custom-call(s32[6]{0:T(128)} %stack.34.s_ref, bf16[384,384]{1,0:T(8,128)(2,1)} %get-tuple-element.125.a, bf16[384,384]{1,0:T(8,128)(2,1)} %copy-done.10, bf16[384,384]{1,0:T(8,128)(2,1)} %copy-done.12, ...), custom_call_target="tpu_custom_call" | custom-call | tf_op jit(solution)/shard_map/sum_columns/pallas_call | solution.py:944
  162.2 3.5 %collective-permute-start.24 = (bf16[96,384]{1,0:T(8,128)(2,1)}, bf16[96,384]{1,0:T(8,128)(2,1)S(1)}, u32[]{:S(2)}, u32[]{:S(2)}) collective-permute-start(bf16[96,384]{1,0:T(8,128)(2,1)} %get-tuple-element.135), channel_id=1, source_target_pairs={{0,16},{2,18},{4,20},{6,22},{8,24},{10,26},{12,28},{14,30},{16,0},... | collective-permute-start | bytes 221192 | tf_op jit(solution)/shard_map/ppermute | solution.py:975
  166.1 3.2 %collective-permute-done.24 = bf16[96,384]{1,0:T(8,128)(2,1)S(1)} collective-permute-done((bf16[96,384]{1,0:T(8,128)(2,1)}, bf16[96,384]{1,0:T(8,128)(2,1)S(1)}, u32[]{:S(2)}, u32[]{:S(2)}) %collective-permute-start.24) | collective-permute-done | bytes 73760 | tf_op jit(solution)/shard_map/ppermute | solution.py:975
  169.3 2.7 %collective-permute-done.25 = bf16[96,384]{1,0:T(8,128)(2,1)S(1)} collective-permute-done((bf16[96,384]{1,0:T(8,128)(2,1)}, bf16[96,384]{1,0:T(8,128)(2,1)S(1)}, u32[]{:S(2)}, u32[]{:S(2)}) %collective-permute-start.25) | collective-permute-done | bytes 73760 | tf_op jit(solution)/shard_map/ppermute | solution.py:975
  173.9 3.5 %collective-permute-start.26 = (bf16[96,384]{1,0:T(8,128)(2,1)S(1)}, bf16[96,384]{1,0:T(8,128)(2,1)S(1)}, u32[]{:S(2)}, u32[]{:S(2)}) collective-permute-start(bf16[96,384]{1,0:T(8,128)(2,1)S(1)} %add_convert_fusion.1), channel_id=1, source_target_pairs={{0,8},{2,10},{4,12},{6,14},{8,0},{10,2},{12,4},{14,6},{16,24},{18,... | collective-permute-start | bytes 221192 | tf_op jit(solution)/shard_map/ppermute | solution.py:975
  177.4 1.9 collective-permute-done.28
  183.6 5.4 %collective-permute-done.30.p1 = bf16[384,384]{1,0:T(8,128)(2,1)S(1)} collective-permute-done((bf16[384,384]{1,0:T(8,128)(2,1)S(1)}, bf16[384,384]{1,0:T(8,128)(2,1)S(1)}, u32[]{:S(2)}, u32[]{:S(2)}) %collective-permute-start.30) | collective-permute-done | bytes 294944 | tf_op jit(solution)/shard_map/ppermute | solution.py:964
  190.7 4.4 %dense_unpack.1 = (f32[384]{0:T(512)}, f32[2,192,192]{2,1,0:T(8,128)}, f32[2,192,1536]{2,1,0:T(8,128)}, f32[2,192,768]{2,1,0:T(8,128)}) custom-call(s32[6]{0:T(128)} %stack.34.s_ref, bf16[640,384]{1,0:T(8,128)(2,1)} %copy-done.2, bf16[640,384]{1,0:T(8,128)(2,1)} %copy-done.4, bf16[640,384]{1,0:T(8,128)(2,1)} %copy-done.5, ...), custom_call_target="tpu_custom_call" | custom-call | tf_op jit(solution)/shard_map/dense_unpack/pallas_call | solution.py:868
  197.1 3.7 %mixer_unpack.1 = (f32[384]{0:T(512)}, f32[384]{0:T(512)}, f32[384]{0:T(512)}, f32[384]{0:T(512)}, f32[128,384]{1,0:T(8,128)}, /*index=5*/f32[2,192,192]{2,1,0:T...) custom-call(s32[6]{0:T(128)} %stack.34.s_ref, ...), custom_call_target="tpu_custom_call" | custom-call | tf_op jit(solution)/shard_map/mixer_unpack/pallas_call | solution.py:868
  (139 shorter events, 40.2 us)
Async XLA Ops:
  4.2 10.2 %collective-permute-start.1 = (bf16[336,384]{1,0:T(8,128)(2,1)}, bf16[336,384]{1,0:T(8,128)(2,1)S(1)}, u32[]{:S(2)}, u32[]{:S(2)}) collective-permute-start(bf16[336,384]{1,0:T(8,128)(2,1)} %get-tuple-element.90.mine), channel_id=1, source_target_pairs={{0,1},{1,0},{2,3},{3,2},{4,5},{5,4},{6,7},{7,6},{8,9},{9,8},{10,11... | collective-permute-start | bytes 774152 | tf_op jit(solution)/shard_map/ppermute | solution.py:960
  7.2 12.9 %collective-permute-start.6 = (bf16[336,384]{1,0:T(8,128)(2,1)}, bf16[336,384]{1,0:T(8,128)(2,1)}, u32[]{:S(2)}, u32[]{:S(2)}) collective-permute-start(bf16[336,384]{1,0:T(8,128)(2,1)} %get-tuple-element.94), channel_id=1, source_target_pairs={{0,1},{1,0},{2,3},{3,2},{4,5},{5,4},{6,7},{7,6},{8,9},{9,8},{10,11... | collective-permute-start | bytes 774152 | tf_op jit(solution)/shard_map/ppermute | solution.py:960
  7.3 30.9 %collective-permute-start = (bf16[1024,384]{1,0:T(8,128)(2,1)S(1)}, bf16[1024,384]{1,0:T(8,128)(2,1)}, u32[]{:S(2)}, u32[]{:S(2)}) collective-permute-start(bf16[1024,384]{1,0:T(8,128)(2,1)S(1)} %constant_dynamic-slice_fusion.1), channel_id=1, source_target_pairs={{0,1},{1,0},{2,3},{3,2},{4,5},{5,4},{6,7},{7,6},{8,9},{9,8},{10,11... | collective-permute-start | bytes 2359304 | tf_op jit(solution)/shard_map/ppermute | solution.py:960
  14.4 14.2 %collective-permute-start.3 = (bf16[336,384]{1,0:T(8,128)(2,1)S(1)}, bf16[336,384]{1,0:T(8,128)(2,1)S(1)}, u32[]{:S(2)}, u32[]{:S(2)}) collective-permute-start(bf16[336,384]{1,0:T(8,128)(2,1)S(1)} %collective-permute-done.1.p0), channel_id=1, source_target_pairs={{0,4},{2,6},{4,0},{6,2},{8,12},{10,14},{12,8},{14,10},{16,20},{18,... | collective-permute-start | bytes 774152 | tf_op jit(solution)/shard_map/ppermute | solution.py:964
  16.5 12.4 %collective-permute-start.2 = (bf16[336,384]{1,0:T(8,128)(2,1)S(1)}, bf16[336,384]{1,0:T(8,128)(2,1)S(1)}, u32[]{:S(2)}, u32[]{:S(2)}) collective-permute-start(bf16[336,384]{1,0:T(8,128)(2,1)S(1)} %collective-permute-done.1.p0), channel_id=1, source_target_pairs={{0,2},{2,0},{4,6},{6,4},{8,10},{10,8},{12,14},{14,12},{16,18},{18,... | collective-permute-start | bytes 774152 | tf_op jit(solution)/shard_map/ppermute | solution.py:964
  23.4 29.5 %collective-permute-start.5 = (bf16[1024,384]{1,0:T(8,128)(2,1)S(1)}, bf16[1024,384]{1,0:T(8,128)(2,1)}, u32[]{:S(2)}, u32[]{:S(2)}) collective-permute-start(bf16[1024,384]{1,0:T(8,128)(2,1)S(1)} %constant_dynamic-slice_fusion), channel_id=1, source_target_pairs={{0,1},{1,0},{2,3},{3,2},{4,5},{5,4},{6,7},{7,6},{8,9},{9,8},{10,11... | collective-permute-start | bytes 2359304 | tf_op jit(solution)/shard_map/ppermute | solution.py:960
  26.9 8.6 %collective-permute-start.8 = (bf16[336,384]{1,0:T(8,128)(2,1)}, bf16[336,384]{1,0:T(8,128)(2,1)S(1)}, u32[]{:S(2)}, u32[]{:S(2)}) collective-permute-start(bf16[336,384]{1,0:T(8,128)(2,1)} %collective-permute-done.6.p0), channel_id=1, source_target_pairs={{0,4},{2,6},{4,0},{6,2},{8,12},{10,14},{12,8},{14,10},{16,20},{18,... | collective-permute-start | bytes 774152 | tf_op jit(solution)/shard_map/ppermute | solution.py:964
  28.6 9.6 %collective-permute-start.12 = (bf16[336,384]{1,0:T(8,128)(2,1)S(1)}, bf16[336,384]{1,0:T(8,128)(2,1)S(1)}, u32[]{:S(2)}, u32[]{:S(2)}) collective-permute-start(bf16[336,384]{1,0:T(8,128)(2,1)S(1)} %collective-permute-done.10.p4), channel_id=1, source_target_pairs={{0,4},{2,6},{4,0},{6,2},{8,12},{10,14},{12,8},{14,10},{16,20},{18,... | collective-permute-start | bytes 774152 | tf_op jit(solution)/shard_map/ppermute | solution.py:964
  30.4 21.0 %collective-permute-start.7 = (bf16[336,384]{1,0:T(8,128)(2,1)}, bf16[336,384]{1,0:T(8,128)(2,1)}, u32[]{:S(2)}, u32[]{:S(2)}) collective-permute-start(bf16[336,384]{1,0:T(8,128)(2,1)} %collective-permute-done.6.p0), channel_id=1, source_target_pairs={{0,2},{2,0},{4,6},{6,4},{8,10},{10,8},{12,14},{14,12},{16,18},{18,... | collective-permute-start | bytes 774152 | tf_op jit(solution)/shard_map/ppermute | solution.py:964
  35.5 16.0 %collective-permute-start.11 = (bf16[336,384]{1,0:T(8,128)(2,1)S(1)}, bf16[336,384]{1,0:T(8,128)(2,1)S(1)}, u32[]{:S(2)}, u32[]{:S(2)}) collective-permute-start(bf16[336,384]{1,0:T(8,128)(2,1)S(1)} %collective-permute-done.10.p4), channel_id=1, source_target_pairs={{0,2},{2,0},{4,6},{6,4},{8,10},{10,8},{12,14},{14,12},{16,18},{18,... | collective-permute-start | bytes 774152 | tf_op jit(solution)/shard_map/ppermute | solution.py:964
  38.3 13.2 %collective-permute-start.9 = (bf16[336,384]{1,0:T(8,128)(2,1)S(1)}, bf16[336,384]{1,0:T(8,128)(2,1)S(1)}, u32[]{:S(2)}, u32[]{:S(2)}) collective-permute-start(bf16[336,384]{1,0:T(8,128)(2,1)S(1)} %collective-permute-done.8.p2), channel_id=1, source_target_pairs={{0,2},{2,0},{4,6},{6,4},{8,10},{10,8},{12,14},{14,12},{16,18},{18,... | collective-permute-start | bytes 774152 | tf_op jit(solution)/shard_map/ppermute | solution.py:964
  38.3 14.7 %collective-permute-start.13 = (bf16[336,384]{1,0:T(8,128)(2,1)S(1)}, bf16[336,384]{1,0:T(8,128)(2,1)S(1)}, u32[]{:S(2)}, u32[]{:S(2)}) collective-permute-start(bf16[336,384]{1,0:T(8,128)(2,1)S(1)} %collective-permute-done.12.p6), channel_id=1, source_target_pairs={{0,2},{2,0},{4,6},{6,4},{8,10},{10,8},{12,14},{14,12},{16,18},{18,... | collective-permute-start | bytes 774152 | tf_op jit(solution)/shard_map/ppermute | solution.py:964
  85.8 34.4 %collective-permute-start.15 = (bf16[1024,384]{1,0:T(8,128)(2,1)}, bf16[1024,384]{1,0:T(8,128)(2,1)S(1)}, u32[]{:S(2)}, u32[]{:S(2)}) collective-permute-start(bf16[1024,384]{1,0:T(8,128)(2,1)} %get-tuple-element.115), channel_id=1, source_target_pairs={{0,1},{1,0},{2,3},{3,2},{4,5},{5,4},{6,7},{7,6},{8,9},{9,8},{10,11... | collective-permute-start | bytes 2359304 | tf_op jit(solution)/shard_map/ppermute | solution.py:960
  95.3 24.9 %collective-permute-start.16 = (bf16[640,384]{1,0:T(8,128)(2,1)}, bf16[640,384]{1,0:T(8,128)(2,1)S(1)}, u32[]{:S(2)}, u32[]{:S(2)}) collective-permute-start(bf16[640,384]{1,0:T(8,128)(2,1)} %get-tuple-element.117), channel_id=1, source_target_pairs={{0,4},{2,6},{4,0},{6,2},{8,12},{10,14},{12,8},{14,10},{16,20},{18,... | collective-permute-start | bytes 1474568 | tf_op jit(solution)/shard_map/ppermute | solution.py:964
  97.0 30.0 %collective-permute-start.17 = (bf16[640,384]{1,0:T(8,128)(2,1)}, bf16[640,384]{1,0:T(8,128)(2,1)S(1)}, u32[]{:S(2)}, u32[]{:S(2)}) collective-permute-start(bf16[640,384]{1,0:T(8,128)(2,1)} %get-tuple-element.118), channel_id=1, source_target_pairs={{0,1},{1,0},{2,3},{3,2},{4,5},{5,4},{6,7},{7,6},{8,9},{9,8},{10,11... | collective-permute-start | bytes 1474568 | tf_op jit(solution)/shard_map/ppermute | solution.py:960
  98.6 28.4 %collective-permute-start.18 = (bf16[640,384]{1,0:T(8,128)(2,1)}, bf16[640,384]{1,0:T(8,128)(2,1)S(1)}, u32[]{:S(2)}, u32[]{:S(2)}) collective-permute-start(bf16[640,384]{1,0:T(8,128)(2,1)} %get-tuple-element.119), channel_id=1, source_target_pairs={{0,5},{1,4},{2,7},{3,6},{4,1},{5,0},{6,3},{7,2},{8,13},{9,12},{10,... | collective-permute-start | bytes 1474568 | tf_op jit(solution)/shard_map/ppermute | solution.py:969
  127.0 8.6 %collective-permute-start.19 = (bf16[2,768,384]{2,1,0:T(8,128)(2,1)}, bf16[2,768,384]{2,1,0:T(8,128)(2,1)S(1)}, u32[]{:S(2)}, u32[]{:S(2)}) collective-permute-start(bf16[2,768,384]{2,1,0:T(8,128)(2,1)} %get-tuple-element.124), channel_id=1, source_target_pairs={{0,2},{2,0},{4,6},{6,4},{8,10},{10,8},{12,14},{14,12},{16,18},{18,... | collective-permute-start | bytes 3538952 | tf_op jit(solution)/shard_map/ppermute | solution.py:964
  131.2 12.0 %collective-permute-start.33 = (bf16[160,384]{1,0:T(8,128)(2,1)}, bf16[160,384]{1,0:T(8,128)(2,1)S(1)}, u32[]{:S(2)}, u32[]{:S(2)}) collective-permute-start(bf16[160,384]{1,0:T(8,128)(2,1)} %get-tuple-element.154), channel_id=1, source_target_pairs={{0,8},{2,10},{4,12},{6,14},{8,0},{10,2},{12,4},{14,6},{16,24},{18,... | collective-permute-start | bytes 368648 | tf_op jit(solution)/shard_map/ppermute | solution.py:975
  133.0 12.3 %collective-permute-start.34 = (bf16[160,384]{1,0:T(8,128)(2,1)}, bf16[160,384]{1,0:T(8,128)(2,1)S(1)}, u32[]{:S(2)}, u32[]{:S(2)}) collective-permute-start(bf16[160,384]{1,0:T(8,128)(2,1)} %get-tuple-element.155), channel_id=1, source_target_pairs={{0,16},{2,18},{4,20},{6,22},{8,24},{10,26},{12,28},{14,30},{16,0},... | collective-permute-start | bytes 368648 | tf_op jit(solution)/shard_map/ppermute | solution.py:975
  135.6 9.8 %collective-permute-start.35 = (bf16[160,384]{1,0:T(8,128)(2,1)}, bf16[160,384]{1,0:T(8,128)(2,1)S(1)}, u32[]{:S(2)}, u32[]{:S(2)}) collective-permute-start(bf16[160,384]{1,0:T(8,128)(2,1)} %get-tuple-element.156), channel_id=1, source_target_pairs={{0,24},{2,26},{4,28},{6,30},{8,16},{10,18},{12,20},{14,22},{16,8},... | collective-permute-start | bytes 368648 | tf_op jit(solution)/shard_map/ppermute | solution.py:975
  140.0 10.2 %collective-permute-start.20 = (bf16[384,384]{1,0:T(8,128)(2,1)}, bf16[384,384]{1,0:T(8,128)(2,1)S(1)}, u32[]{:S(2)}, u32[]{:S(2)}) collective-permute-start(bf16[384,384]{1,0:T(8,128)(2,1)} %get-tuple-element.126), channel_id=1, source_target_pairs={{0,4},{2,6},{4,0},{6,2},{8,12},{10,14},{12,8},{14,10},{16,20},{18,... | collective-permute-start | bytes 884744 | tf_op jit(solution)/shard_map/ppermute | solution.py:964
  141.7 14.1 %collective-permute-start.21 = (bf16[384,384]{1,0:T(8,128)(2,1)}, bf16[384,384]{1,0:T(8,128)(2,1)S(1)}, u32[]{:S(2)}, u32[]{:S(2)}) collective-permute-start(bf16[384,384]{1,0:T(8,128)(2,1)} %get-tuple-element.127), channel_id=1, source_target_pairs={{0,1},{1,0},{2,3},{3,2},{4,5},{5,4},{6,7},{7,6},{8,9},{9,8},{10,11... | collective-permute-start | bytes 884744 | tf_op jit(solution)/shard_map/ppermute | solution.py:960
  143.2 12.5 %collective-permute-start.22 = (bf16[384,384]{1,0:T(8,128)(2,1)}, bf16[384,384]{1,0:T(8,128)(2,1)S(1)}, u32[]{:S(2)}, u32[]{:S(2)}) collective-permute-start(bf16[384,384]{1,0:T(8,128)(2,1)} %get-tuple-element.128), channel_id=1, source_target_pairs={{0,5},{1,4},{2,7},{3,6},{4,1},{5,0},{6,3},{7,2},{8,13},{9,12},{10,... | collective-permute-start | bytes 884744 | tf_op jit(solution)/shard_map/ppermute | solution.py:969
  145.4 15.5 %collective-permute-start.38 = (bf16[160,384]{1,0:T(8,128)(2,1)S(1)}, bf16[160,384]{1,0:T(8,128)(2,1)S(1)}, u32[]{:S(2)}, u32[]{:S(2)}) collective-permute-start(bf16[160,384]{1,0:T(8,128)(2,1)S(1)} %add_convert_fusion), channel_id=1, source_target_pairs={{0,24},{2,26},{4,28},{6,30},{8,16},{10,18},{12,20},{14,22},{16,8},... | collective-permute-start | bytes 368648 | tf_op jit(solution)/shard_map/ppermute | solution.py:975
  148.0 12.9 %collective-permute-start.37 = (bf16[160,384]{1,0:T(8,128)(2,1)S(1)}, bf16[160,384]{1,0:T(8,128)(2,1)S(1)}, u32[]{:S(2)}, u32[]{:S(2)}) collective-permute-start(bf16[160,384]{1,0:T(8,128)(2,1)S(1)} %add_convert_fusion), channel_id=1, source_target_pairs={{0,16},{2,18},{4,20},{6,22},{8,24},{10,26},{12,28},{14,30},{16,0},... | collective-permute-start | bytes 368648 | tf_op jit(solution)/shard_map/ppermute | solution.py:975
  150.1 10.8 %collective-permute-start.36 = (bf16[160,384]{1,0:T(8,128)(2,1)S(1)}, bf16[160,384]{1,0:T(8,128)(2,1)S(1)}, u32[]{:S(2)}, u32[]{:S(2)}) collective-permute-start(bf16[160,384]{1,0:T(8,128)(2,1)S(1)} %add_convert_fusion), channel_id=1, source_target_pairs={{0,8},{2,10},{4,12},{6,14},{8,0},{10,2},{12,4},{14,6},{16,24},{18,... | collective-permute-start | bytes 368648 | tf_op jit(solution)/shard_map/ppermute | solution.py:975
  159.3 21.5 %collective-permute-start.29 = (bf16[1024,384]{1,0:T(8,128)(2,1)}, bf16[1024,384]{1,0:T(8,128)(2,1)S(1)}, u32[]{:S(2)}, u32[]{:S(2)}) collective-permute-start(bf16[1024,384]{1,0:T(8,128)(2,1)} %get-tuple-element.137), channel_id=1, source_target_pairs={{0,1},{1,0},{2,3},{3,2},{4,5},{5,4},{6,7},{7,6},{8,9},{9,8},{10,11... | collective-permute-start | bytes 2359304 | tf_op jit(solution)/shard_map/ppermute | solution.py:960
  161.0 16.5 %collective-permute-start.39 = (bf16[640,384]{1,0:T(8,128)(2,1)S(1)}, bf16[640,384]{1,0:T(8,128)(2,1)S(1)}, u32[]{:S(2)}, u32[]{:S(2)}) collective-permute-start(bf16[640,384]{1,0:T(8,128)(2,1)S(1)} %pad_maximum_fusion.p0), channel_id=1, source_target_pairs={{0,4},{2,6},{4,0},{6,2},{8,12},{10,14},{12,8},{14,10},{16,20},{18,... | collective-permute-start | bytes 1474568 | tf_op jit(solution)/shard_map/ppermute | solution.py:964
  177.4 12.5 %collective-permute-start.40 = (bf16[640,384]{1,0:T(8,128)(2,1)S(1)}, bf16[640,384]{1,0:T(8,128)(2,1)S(1)}, u32[]{:S(2)}, u32[]{:S(2)}) collective-permute-start(bf16[640,384]{1,0:T(8,128)(2,1)S(1)} %pad_maximum_fusion.p0), channel_id=1, source_target_pairs={{0,2},{2,0},{4,6},{6,4},{8,10},{10,8},{12,14},{14,12},{16,18},{18,... | collective-permute-start | bytes 1474568 | tf_op jit(solution)/shard_map/ppermute | solution.py:964
  179.3 10.7 %collective-permute-start.41 = (bf16[640,384]{1,0:T(8,128)(2,1)S(1)}, bf16[640,384]{1,0:T(8,128)(2,1)}, u32[]{:S(2)}, u32[]{:S(2)}) collective-permute-start(bf16[640,384]{1,0:T(8,128)(2,1)S(1)} %collective-permute-done.39.p1), channel_id=1, source_target_pairs={{0,2},{2,0},{4,6},{6,4},{8,10},{10,8},{12,14},{14,12},{16,18},{18,... | collective-permute-start | bytes 1474568 | tf_op jit(solution)/shard_map/ppermute | solution.py:964
  180.8 8.1 %collective-permute-start.30 = (bf16[384,384]{1,0:T(8,128)(2,1)S(1)}, bf16[384,384]{1,0:T(8,128)(2,1)S(1)}, u32[]{:S(2)}, u32[]{:S(2)}) collective-permute-start(bf16[384,384]{1,0:T(8,128)(2,1)S(1)} %pad_maximum_fusion.1.p0), channel_id=1, source_target_pairs={{0,4},{2,6},{4,0},{6,2},{8,12},{10,14},{12,8},{14,10},{16,20},{18,... | collective-permute-start | bytes 884744 | tf_op jit(solution)/shard_map/ppermute | solution.py:964
  183.6 12.8 %collective-permute-start.31 = (bf16[384,384]{1,0:T(8,128)(2,1)S(1)}, bf16[384,384]{1,0:T(8,128)(2,1)S(1)}, u32[]{:S(2)}, u32[]{:S(2)}) collective-permute-start(bf16[384,384]{1,0:T(8,128)(2,1)S(1)} %pad_maximum_fusion.1.p0), channel_id=1, source_target_pairs={{0,2},{2,0},{4,6},{6,4},{8,10},{10,8},{12,14},{14,12},{16,18},{18,... | collective-permute-start | bytes 884744 | tf_op jit(solution)/shard_map/ppermute | solution.py:964
  (38 other events, 268.7 us)
where the time goes:
time: 201 us
  Pallas kernels  94.4 us (47%)
  waiting for transfers between devices  47.5 us (24%)
  starting transfers between devices  43.6 us (22%)
  local copies, waits for them, and re-layouts  11.7 us (6%)
  other arithmetic  2.51 us (1%)
    pallas_call x1, Pallas kernels, dense(): pl.pallas_call(functools.partial(dense_kernel, steps=steps), out_shape=tu...  32 us
    ppermute x8, waiting for transfers between devices, swap_narrow(): return lax.ppermute(values, 'narrow', [(0, 1), (1, 0)])  21.6 us
    pallas_call x1, Pallas kernels, mixer_backward(): pl.pallas_call(functools.partial(mixer_backward_kernel, steps=steps, shar...  21.4 us
    ppermute x12, starting transfers between devices, shift_wide(): return lax.ppermute(values, 'wide', [(i, i ^ flip) for i in range(size)])  17.5 us
    ppermute x20, waiting for transfers between devices, swap_wide(): lax.ppermute(values, 'wide', [(i, i ^ 1 << bit) for i in range(size)])  14.6 us
    ppermute x8, starting transfers between devices, swap_narrow(): return lax.ppermute(values, 'narrow', [(0, 1), (1, 0)])  13.1 us
    pallas_call x1, Pallas kernels, mixer_forward(): pl.pallas_call(mixer_forward_kernel, out_shape=tuple(outs), grid_spec=plt...  12.6 us
    ppermute x20, starting transfers between devices, swap_wide(): lax.ppermute(values, 'wide', [(i, i ^ 1 << bit) for i in range(size)])  12.5 us
  transfers between devices with their start and end apart: 42, of which 18 were waited for; matrix products, arithmetic and copies ran while one was open for 3% of the time, Pallas kernels for 28%

commit v1 on v0

--- a/solution.py
+++ b/solution.py
@@ -28,8 +28,8 @@
 BACK_TILE = 256
 VMEM = 60 << 20
 
-FILTER_ROW = 6 * QUARTER
-VECTOR_ROW = FILTER_ROW + ORDER // 4
+FILTER_ROW = 3 * QUARTER
+VECTOR_ROW = FILTER_ROW + ORDER // 8
 MIX_W = VECTOR_ROW + 16
 FFN_W = 7 * QUARTER
 FFN_G = 1280
@@ -85,6 +85,10 @@
     return out
 
 
+def light():
+    return pl.CostEstimate(flops=0, bytes_accessed=1 << 20, transcendentals=0)
+
+
 def rows_of(block, size):
     return pl.ds(pl.multiple_of(block * size, size), size)
 
@@ -126,16 +130,10 @@
 def pack_kernel(
     s_ref, il, ir, ol, orr, ul, ur, dl, dr, weight, mask, gain1, gain2, skip, decay, mix_ref, ffn_ref
 ):
-    def pairs(ref):
-        return jnp.concatenate([ref[0], ref[1]], axis=1)
-
     q = QUARTER
-    mix_ref[0:q, :] = pairs(il)
-    wide_in = pairs(ir)
-    for c in range(3):
-        mix_ref[(1 + c) * q : (2 + c) * q, :] = wide_in[:, c * HALF : (c + 1) * HALF]
-    mix_ref[4 * q : 5 * q, :] = pairs(ol)
-    mix_ref[5 * q : 6 * q, :] = pairs(orr)
+    mix_ref[0:q, :] = jnp.concatenate([il[0], ol[0]], axis=1)
+    mix_ref[q : 2 * q, :] = ir[0][:, :HALF]
+    mix_ref[2 * q : 3 * q, :] = jnp.concatenate([ir[0][:, HALF:], orr[0]], axis=1)
     mix_ref[FILTER_ROW:VECTOR_ROW, :] = weight[...]
     rest = decay[...].reshape(1, HALF)
     rows = [item[...].reshape(1, HALF).astype(f32) for item in (mask, gain1, gain2, skip)]
@@ -156,9 +154,6 @@
 
 
 def pack_weights(scalars, mixer_weights, dense_weights, filter_weight, vectors):
-    def quarter(item):
-        return pl.BlockSpec((2, QUARTER, item.shape[2]), lambda i, s: (0, s[1], 0))
-
     def eighth(item):
         return pl.BlockSpec((1, QUARTER, item.shape[2]), lambda i, s: (s[2], s[1], 0))
 
@@ -171,21 +166,14 @@
         grid_spec=pltpu.PrefetchScalarGridSpec(
             num_scalar_prefetch=1,
             grid=(1,),
-            in_specs=[quarter(item) for item in mixer_weights]
-            + [eighth(item) for item in dense_weights]
-            + [pl.BlockSpec((ORDER // 4, HALF), lambda i, s: (s[1], 0))]
+            in_specs=[eighth(item) for item in mixer_weights + dense_weights]
+            + [pl.BlockSpec((ORDER // 8, HALF), lambda i, s: (4 * s[2] + s[1], 0))]
             + [whole(item.shape) for item in vectors],
             out_specs=(whole((MIX_W, HALF)), whole((FFN_W, HALF))),
         ),
         name="pack_weights",
+        cost_estimate=light(),
     )(scalars, *mixer_weights, *dense_weights, filter_weight, *vectors)
-
-
-def unpack_narrow(dst, other, row, piece, base):
-    for j in range(2):
-        dst[2 * other + j, pl.ds(row, QUARTER), :] = piece[
-            base : base + QUARTER, j * BS : (j + 1) * BS
-        ]
 
 
 def own_blocks(dst, side, src):
@@ -194,14 +182,16 @@
 
 
 def filter_kernel(
-    s_ref, own, mine, p0, p1, p2, p3, feats, fwd, taps_ref, spec_ref, pen_ref, cols_ref, weight
+    s_ref, own, mine, *refs
 ):
+    pieces = refs[:8]
+    feats, fwd, taps_ref, spec_ref, pen_ref, cols_ref, weight = refs[8:]
     side = s_ref[0]
-    q = ORDER // 4
-    for p, piece in enumerate((p0, p1, p2, p3)):
-        row = pl.multiple_of(jnp.bitwise_xor(s_ref[1], p) * q, q)
-        weight[pl.ds(row, q), :] = piece[FILTER_ROW:VECTOR_ROW, :]
-    for which, src, rows in ((side, own, mine), (1 - side, weight, p0)):
+    q = ORDER // 8
+    for p, piece in enumerate(pieces):
+        place = 4 * jnp.bitwise_xor(s_ref[2], p >> 2) + jnp.bitwise_xor(s_ref[1], p & 3)
+        weight[pl.ds(pl.multiple_of(place * q, q), q), :] = piece[FILTER_ROW:VECTOR_ROW, :]
+    for which, src, rows in ((side, own, mine), (1 - side, weight, pieces[0])):
         table = src[...]
         basis = tn(table, feats[2]) + tn(table, feats[1]) + tn(table, feats[0])
         taps_ref[rows_of(which, HALF), :] = basis
@@ -242,6 +232,7 @@
             scratch_shapes=[pltpu.VMEM((ORDER, HALF), bf16)],
         ),
         name="filter_spectrum",
+        cost_estimate=light(),
     )(scalars, *ins)
 
 
@@ -258,22 +249,10 @@
     ir,
     ol,
     orr,
-    p0,
-    p1,
-    p2,
-    p3,
-    middle,
-    first,
-    kept,
-    scale,
-    wil,
-    wir,
-    wol,
-    wor,
-    enter,
-    half,
-    conv,
+    *refs,
 ):
+    pieces = refs[:8]
+    middle, first, kept, scale, wil, wir, wol, wor, enter, half, conv = refs[8:]
     side = s_ref[0]
 
     @pl.when(pl.program_id(0) == 0)
@@ -284,16 +263,14 @@
         own_blocks(wol, side, ol)
         own_blocks(wor, side, orr)
         q = QUARTER
-        for p, piece in enumerate((p0, p1, p2, p3)):
-            row = pl.multiple_of(jnp.bitwise_xor(s_ref[1], p) * q, q)
-            unpack_narrow(wil, other, row, piece, 0)
-            at = pl.ds(row, q)
-            wir[2 * other, at, 0:HALF] = piece[q : 2 * q, :]
-            wir[2 * other, at, HALF : 3 * BS] = piece[2 * q : 3 * q, 0:BS]
-            wir[2 * other + 1, at, 0:BS] = piece[2 * q : 3 * q, BS:HALF]
-            wir[2 * other + 1, at, BS : 3 * BS] = piece[3 * q : 4 * q, :]
-            unpack_narrow(wol, other, row, piece, 4 * q)
-            unpack_narrow(wor, other, row, piece, 5 * q)
+        for p, piece in enumerate(pieces):
+            at = pl.ds(pl.multiple_of(jnp.bitwise_xor(s_ref[1], p & 3) * q, q), q)
+            blk = 2 * other + jnp.bitwise_xor(s_ref[2], p >> 2)
+            wil[blk, at, :] = piece[0:q, :BS]
+            wol[blk, at, :] = piece[0:q, BS:]
+            wir[blk, at, 0:HALF] = piece[q : 2 * q, :]
+            wir[blk, at, HALF:] = piece[2 * q : 3 * q, :BS]
+            wor[blk, at, :] = piece[2 * q : 3 * q, BS:]
 
     place_halves(enter, side, own[...].T.astype(f32), oth[...].T.astype(f32))
     valid = marks[0:1, :]
@@ -330,7 +307,7 @@
         regroup(kept.at[4], b, tn(wol[b], block(half, b)).astype(bf16))
     for g in range(NB):
         rows = slice(g * BS, (g + 1) * BS)
-        middle[rows, :] = enter[rows, :] + tn(wor[g], block(kept.at[4], g))
+        middle[rows, :] = (enter[rows, :] + tn(wor[g], block(kept.at[4], g))).astype(bf16)
 
 
 def mixer_forward(scalars, own, oth, marks, cols, spec, fwd, inv, weights):
@@ -344,7 +321,7 @@
     ] + [whole(item.shape) for item in ins[3:]]
     full = [(NB, BS, BS), (NB, BS, 3 * BS), (NB, BS, BS), (NB, BS, BS)]
     outs = [
-        jax.ShapeDtypeStruct((D, row_count), f32),
+        jax.ShapeDtypeStruct((D, row_count), bf16),
         jax.ShapeDtypeStruct((2, D, row_count), bf16),
         jax.ShapeDtypeStruct((5, D, row_count), bf16),
         jax.ShapeDtypeStruct((8, row_count), f32),
@@ -450,7 +427,7 @@
             acc[...] = jnp.zeros(acc.shape, f32)
 
     gain = column(cols, 2)
-    normed, scale_row = norm_stats(middle[...])
+    normed, scale_row = norm_stats(middle[...].astype(f32))
     half[...] = (normed * gain).astype(bf16)
     for b in range(NB):
         regroup(moved3, b, tn(wul[b], block(half, b)).astype(bf16))
@@ -459,7 +436,7 @@
         both = tn(wur[g], block(moved3, g))
         gate, up = both[:FB], both[FB:]
         chance = 0.5 + 0.5 * lax.erf(gate * 0.7071067811865476)
-        density = jnp.exp(gate * gate * -0.5) * 0.3989422804014327
+        density = jnp.exp(gate * gate * -0.5 - 0.9189385332046727)
         active = gate * chance
         hid[rows, :] = (active * up).astype(bf16)
         act[rows, :] = active.astype(bf16)
@@ -467,7 +444,7 @@
         regroup(moved4, g, nn(wdl[g], hid[rows, :]).astype(bf16))
     for g in range(NB):
         rows = slice(g * BS, (g + 1) * BS)
-        outs[rows, :] = (middle[rows, :] + tn(wdr[g], block(moved4, g))).astype(bf16)
+        outs[rows, :] = (middle[rows, :].astype(f32) + tn(wdr[g], block(moved4, g))).astype(bf16)
     out_own[...] = outs[rows_of(side, HALF), :].T
     out_send[...] = outs[rows_of(1 - side, HALF), :].T
     place_halves(top, side, own[...].T, oth[...].T)
@@ -480,8 +457,9 @@
         returned = block(back, b)
         grad_hidden = tn(wdl[b], returned)
         gdl[b] += nt(returned, hid[rows, :])
-        gated[:FB, :] = (grad_hidden * slope[rows, :].astype(f32)).astype(bf16)
-        gated[FB:, :] = (grad_hidden * act[rows, :].astype(f32)).astype(bf16)
+        lowered = grad_hidden.astype(bf16)
+        gated[:FB, :] = lowered * slope[rows, :]
+        gated[FB:, :] = lowered * act[rows, :]
         moved = block(moved3, b)
         gur[b] += nt(moved, gated[...])
         regroup(moved4, b, nn(wur[b], gated[...]).astype(bf16))
@@ -492,7 +470,9 @@
         gul[b] += nt(block(half, b), returned)
     grad_in = jnp.concatenate(grads, axis=0)
     ggain[...] += fold(grad_in * normed)
-    grad_middle[...] = top[...].astype(f32) + norm_back(grad_in, normed, scale_row, gain)
+    grad_middle[...] = (
+        top[...].astype(f32) + norm_back(grad_in, normed, scale_row, gain)
+    ).astype(bf16)
 
     @pl.when(pl.program_id(0) == steps - 1)
     def _():
@@ -549,7 +529,7 @@
     outs = [
         jax.ShapeDtypeStruct((2 * row_count, HALF), bf16),
         jax.ShapeDtypeStruct((row_count, HALF), bf16),
-        jax.ShapeDtypeStruct((D, row_count), f32),
+        jax.ShapeDtypeStruct((D, row_count), bf16),
         jax.ShapeDtypeStruct(half_shape, bf16),
         jax.ShapeDtypeStruct(half_shape, bf16),
         jax.ShapeDtypeStruct((2, BS, HALF), bf16),
@@ -579,7 +559,7 @@
             out_specs=tuple(out_specs),
             scratch_shapes=scratch,
         ),
-        compiler_params=pltpu.CompilerParams(vmem_limit_bytes=VMEM),
+        compiler_params=pltpu.CompilerParams(vmem_limit_bytes=46 << 20),
         name="dense",
         cost_estimate=pl.CostEstimate(
             flops=row_count * 2 * 8000000, bytes_accessed=row_count * 10000, transcendentals=0
@@ -647,9 +627,8 @@
             acc[...] = jnp.zeros(acc.shape, f32)
 
     valid = marks[0:1, :]
-    half[...] = grad_middle[...].astype(bf16)
     for g in range(NB):
-        grad = block(half, g)
+        grad = block(grad_middle, g)
         regroup(back, g, nn(wor[g], grad).astype(bf16))
         gor[g] += nt(block(kept.at[4], g), grad)
     for b in range(NB):
@@ -704,7 +683,7 @@
     grad_in = jnp.concatenate(grads, axis=0)
     normed = first[0].astype(f32) * (1.0 / gain)
     ggain[...] += fold(grad_in * normed)
-    entered = grad_middle[...] + norm_back(grad_in, normed, scale[0:1, :], gain)
+    entered = grad_middle[...].astype(f32) + norm_back(grad_in, normed, scale[0:1, :], gain)
     gmask[...] += fold(entered * masked)
     total[...] = entered * (1.0 - masked)
     out_own[...] = total[rows_of(side, HALF), :].T
@@ -802,7 +781,7 @@
             out_specs=tuple(out_specs),
             scratch_shapes=scratch,
         ),
-        compiler_params=pltpu.CompilerParams(vmem_limit_bytes=VMEM),
+        compiler_params=pltpu.CompilerParams(vmem_limit_bytes=40 << 20),
         name="mixer_backward",
         cost_estimate=pl.CostEstimate(
             flops=row_count * 2 * 6000000, bytes_accessed=row_count * 20000, transcendentals=0
@@ -875,8 +854,9 @@
             out_specs=tuple(whole(shape) for shape in shapes),
             scratch_shapes=[pltpu.VMEM((2, rows, HALF), bf16)],
         ),
-        compiler_params=pltpu.CompilerParams(vmem_limit_bytes=VMEM),
+        compiler_params=pltpu.CompilerParams(vmem_limit_bytes=16 << 20),
         name=name,
+        cost_estimate=light(),
     )(scalars, *parts)
 
 
@@ -923,8 +903,9 @@
             in_specs=specs + specs,
             out_specs=(whole((rows, HALF)),) * 4,
         ),
-        compiler_params=pltpu.CompilerParams(vmem_limit_bytes=VMEM),
+        compiler_params=pltpu.CompilerParams(vmem_limit_bytes=16 << 20),
         name="sum_corners",
+        cost_estimate=light(),
     )(scalars, *([kept] * 4 + [got] * 4))
 
 
@@ -951,8 +932,9 @@
             out_specs=(whole((rows // 4, HALF)),) * 4,
             scratch_shapes=[pltpu.VMEM((rows, HALF), f32)],
         ),
-        compiler_params=pltpu.CompilerParams(vmem_limit_bytes=VMEM),
+        compiler_params=pltpu.CompilerParams(vmem_limit_bytes=12 << 20),
         name="sum_columns",
+        cost_estimate=light(),
     )(scalars, *parts)
 
 
@@ -994,28 +976,44 @@
 
 def over_columns(parts, size):
     own, *others = parts
-    packed = add_low(
-        own, *(shift_wide(item, (k + 1) << 2, size) for k, item in enumerate(others))
-    )
+    return (own,) + tuple(
+        shift_wide(item, (k + 1) << 2, size) for k, item in enumerate(others)
+    )
+
+
+def sum_columns(parts, size):
+    packed = add_low(*parts)
     bit = 4
     while 1 << bit < size:
         packed = add_low(packed, swap_wide(packed, bit, size))
         bit += 1
-    return jnp.concatenate(
-        [packed] + [shift_wide(packed, k << 2, size) for k in (1, 2, 3)], axis=0
-    )
-
-
-def over_rows(near, size):
-    far = swap_wide(near, 1, size)
+    return packed
+
+
+def along_columns(packed, size):
+    return (packed,) + tuple(shift_wide(packed, k << 2, size) for k in (1, 2, 3))
+
+
+def tie(*groups):
+    held = lax.optimization_barrier(groups)
+    return held
+
+
+def over_cores(near, far, size):
     return (near, far, swap_wide(near, 0, size), swap_wide(far, 0, size))
 
 
-def gather_pieces(piece, bits, size):
-    pieces = [swap_narrow(piece)]
-    for bit in bits:
-        pieces = pieces + [swap_wide(item, bit, size) for item in pieces]
-    return pieces
+def gather_chips(piece, size):
+    near = swap_narrow(piece)
+    high = swap_wide(near, 2, size)
+    return near, swap_wide(near, 1, size), high
+
+
+def gather_cores(items, size):
+    pieces = []
+    for item in items:
+        pieces += [item, swap_wide(item, 0, size)]
+    return tuple(pieces)
 
 
 def on_device(
@@ -1056,15 +1054,10 @@
     mix_piece, ffn_piece = pack_weights(
         scalars, mixer_weights, dense_weights, filter_weight, vectors
     )
-    first, third = gather_pieces(mix_piece, (1,), wide_size)
-    mix_pieces = (first, swap_wide(first, 0, wide_size), third, swap_wide(third, 0, wide_size))
-    y0, z0, x0, xz0 = gather_pieces(ffn_piece, (2, 1), wide_size)
-    ffn_pieces = tuple(
-        piece
-        for near in ((y0, x0), (z0, xz0))
-        for item in near
-        for piece in (item, swap_wide(item, 0, wide_size))
-    )
+    mix_chips = gather_chips(mix_piece, wide_size)
+    mix_chips += (swap_wide(mix_chips[2], 1, wide_size),)
+    mix_pieces = gather_cores(mix_chips, wide_size)
+    ffn_chips = gather_chips(ffn_piece, wide_size)
     tokens_other = swap_narrow(sent_rows(tokens))
     cot_other = swap_narrow(sent_rows(cotangent))
 
@@ -1081,15 +1074,18 @@
         scalars, filter_weight, mix_piece, mix_pieces, feats, fwd
     )
 
+    ffn_chips, spec = tie(ffn_chips, spec)
+    ffn_last = swap_wide(ffn_chips[2], 1, wide_size)
     middle, first, kept, scale, *full = mixer_forward(
         scalars, tokens, tokens_other, marks, cols, spec, fwd, inv, mixer_weights + mix_pieces
     )
+    middle, penalty, ffn_last = tie(middle, penalty, ffn_last)
+    ffn_pieces = gather_cores(ffn_chips + (ffn_last,), wide_size)
     output, output_sent, grad_middle, ffn_keep, ffn_send, packed_dr = dense(
         scalars, middle, cotangent, cot_other, cols, dense_weights + ffn_pieces
     )
-    output_other = swap_narrow(output_sent)
     ffn_parts = corners(scalars, ffn_keep, swap_wide(ffn_send, 0, wide_size))
-    grad_middle, *ffn_parts = lax.optimization_barrier((grad_middle, *ffn_parts))
+    grad_middle, ffn_parts, penalty = tie(grad_middle, ffn_parts, penalty[0, 0])
     ffn_parts = over_corners(ffn_parts, wide_size)
     tokens_grad, grad_sent, mix_keep, mix_send = mixer_backward(
         share,
@@ -1099,28 +1095,41 @@
         full,
         (taps, feats, packed_dr),
     )
-    mix_keep, mix_send, output_other, *ffn_parts = lax.optimization_barrier(
-        (mix_keep, mix_send, output_other, *ffn_parts)
-    )
-    mix_parts = corners(scalars, mix_keep, swap_wide(mix_send, 0, wide_size))
+    mix_keep, mix_send, ffn_parts = tie(mix_keep, mix_send, ffn_parts)
+    mix_got = swap_wide(mix_send, 0, wide_size)
     ffn_parts = columns(scalars, ffn_parts)
-    mix_parts = columns(scalars, over_corners(mix_parts, wide_size))
-    grad_sent, *mix_parts = lax.optimization_barrier((grad_sent, *mix_parts))
+    mix_parts = corners(scalars, mix_keep, mix_got)
+
+    ffn_parts = over_columns(ffn_parts, wide_size)
+    mix_parts = over_corners(mix_parts, wide_size)
+    ffn_sum = sum_columns(ffn_parts, wide_size)
+    ffn_parts = along_columns(ffn_sum, wide_size)
+    mix_parts = columns(scalars, mix_parts)
+    mix_parts, grad_sent, output_sent = tie(mix_parts, grad_sent, output_sent)
+    output_other = swap_narrow(output_sent)
     grad_other = swap_narrow(grad_sent)
-    ffn_near = over_columns(ffn_parts, wide_size)
-    mix_near = over_columns(mix_parts, wide_size)
-    ffn_parts = over_rows(ffn_near, wide_size)
-    mix_near, grad_other = lax.optimization_barrier((mix_near, grad_other))
-    mix_parts = over_rows(mix_near, wide_size)
+    mix_parts = over_columns(mix_parts, wide_size)
+    mix_sum = sum_columns(mix_parts, wide_size)
+    ffn_near = jnp.concatenate(ffn_parts, axis=0)
+    mix_sum, ffn_near, output_other = tie(mix_sum, ffn_near, output_other)
+    mix_parts = along_columns(mix_sum, wide_size)
+    ffn_far = swap_wide(ffn_near, 1, wide_size)
+    mix_near = jnp.concatenate(mix_parts, axis=0)
+    mix_far = swap_wide(mix_near, 1, wide_size)
+    ffn_parts = over_cores(ffn_near, ffn_far, wide_size)
     gain_two, g_ul, g_ur, g_dl = unpack(
         dense_unpack_kernel, scalars, ffn_parts, DENSE_OUTS, "dense_unpack"
-    )
-    g_mask, g_gain, g_skip, g_decay, g_filter, g_il, g_ir, g_ol, g_or, g_dr = unpack(
-        mixer_unpack_kernel, scalars, mix_parts, MIXER_OUTS, "mixer_unpack"
     )
     start = (1 - side) * row_count
     output = lax.dynamic_update_slice_in_dim(output, output_other, start, 0)
     tokens_grad = lax.dynamic_update_slice_in_dim(tokens_grad, grad_other.astype(f32), start, 0)
+    mix_far, gain_two, g_ul, g_ur, g_dl, output, tokens_grad = tie(
+        mix_far, gain_two, g_ul, g_ur, g_dl, output, tokens_grad
+    )
+    mix_parts = over_cores(mix_near, mix_far, wide_size)
+    g_mask, g_gain, g_skip, g_decay, g_filter, g_il, g_ir, g_ol, g_or, g_dr = unpack(
+        mixer_unpack_kernel, scalars, mix_parts, MIXER_OUTS, "mixer_unpack"
+    )
     return (
         output,
         tokens_grad,
@@ -1138,7 +1147,7 @@
         g_ur,
         jnp.swapaxes(g_dl, 1, 2),
         g_dr,
-        penalty[0, 0],
+        penalty,
     )
 
 

time: 201 us -> 179 us (0.89)
  Pallas kernels: 94.4 us -> 77.3 us
  starting transfers between devices: 43.6 us -> 56 us
  waiting for transfers between devices: 47.5 us -> 36.7 us
  local copies, waits for them, and re-layouts: 11.7 us -> 7.41 us
  other arithmetic: 2.51 us -> 0.46 us
    ppermute x12, starting transfers between devices: 17.5 us -> 27.4 us  [shift_wide(): return lax.ppermute(values, 'wide', [(i, i ^ flip) for i in range(size)])]
    ppermute x8, waiting for transfers between devices: 21.6 us -> 11.8 us  [swap_narrow(): return lax.ppermute(values, 'narrow', [(0, 1), (1, 0)])]
    pallas_call x2, Pallas kernels: 7.45 us -> 1.85 us  [corners(): pl.pallas_call(corners_kernel, out_shape=(shape,) * 4, grid_spec=pltpu.Pr...]
    unnamed x58 -> x73, local copies, waits for them, and re-layouts: 6.83 us -> 2.49 us
    pallas_call x2, Pallas kernels: 6.1 us -> 1.78 us  [columns(): pl.pallas_call(columns_kernel, out_shape=(shape,) * 4, grid_spec=pltpu.Pr...]
    ppermute x12, waiting for transfers between devices: 11.3 us -> 8.04 us  [shift_wide(): return lax.ppermute(values, 'wide', [(i, i ^ flip) for i in range(size)])]
    ppermute x20 -> x24, starting transfers between devices: 12.5 us -> 15.8 us  [swap_wide(): lax.ppermute(values, 'wide', [(i, i ^ 1 << bit) for i in range(size)])]
    pallas_call x2, Pallas kernels: 8.06 us -> 5.19 us  [unpack(): pl.pallas_call(kernel, out_shape=outs, grid_spec=pltpu.PrefetchScalarGrid...]
  transfers between devices with their start and end apart: 42 -> 46, of which waited for: 18 -> 20; matrix products, arithmetic and copies ran while one was open for 3% -> 3% of each run, Pallas kernels for 28% -> 23%
where the time goes in v1:
time: 179 us
  Pallas kernels  77.3 us (43%)
  starting transfers between devices  56 us (31%)
  waiting for transfers between devices  36.7 us (21%)
  local copies, waits for them, and re-layouts  7.41 us (4%)
    pallas_call x1, Pallas kernels, dense(): pl.pallas_call(functools.partial(dense_kernel, steps=steps), out_shape=tu...  29.3 us
    ppermute x12, starting transfers between devices, shift_wide(): return lax.ppermute(values, 'wide', [(i, i ^ flip) for i in range(size)])  27.4 us
    pallas_call x1, Pallas kernels, mixer_backward(): pl.pallas_call(functools.partial(mixer_backward_kernel, steps=steps, shar...  20.1 us
    ppermute x24, starting transfers between devices, swap_wide(): lax.ppermute(values, 'wide', [(i, i ^ 1 << bit) for i in range(size)])  15.8 us
    ppermute x24, waiting for transfers between devices, swap_wide(): lax.ppermute(values, 'wide', [(i, i ^ 1 << bit) for i in range(size)])  15.2 us
    pallas_call x1, Pallas kernels, mixer_forward(): pl.pallas_call(mixer_forward_kernel, out_shape=tuple(outs), grid_spec=plt...  12.5 us
    ppermute x8, waiting for transfers between devices, swap_narrow(): return lax.ppermute(values, 'narrow', [(0, 1), (1, 0)])  11.8 us
    ppermute x8, starting transfers between devices, swap_narrow(): return lax.ppermute(values, 'narrow', [(0, 1), (1, 0)])  11.1 us
  transfers between devices with their start and end apart: 46, of which 20 were waited for; matrix products, arithmetic and copies ran while one was open for 3% of the time, Pallas kernels for 23%

profile of v1, /device:TPU:0, one launch (start us, length us, event | category | flops | bytes accessed | tf_op | source)
XLA Modules:
  0.0 179.1 jit_solution(412505830476710358)
XLA Ops:
  1.3 2.7 %pack_weights.1 = (bf16[176,384]{1,0:T(8,128)(2,1)}, bf16[336,384]{1,0:T(8,128)(2,1)}) custom-call(s32[6]{0:T(128)} %stack.34.s_ref, bf16[2,192,192]{2,1,0:T(8,128)(2,1)} %il.3, bf16[2,192,576]{2,1,0:T(8,128)(2,1)} %ir.3, bf16[2,192,192]{2,1,0:T(8,128)(2,1)} %ol.3, bf16[2,192,192]{2,1,0:T(8,128)(2,1)} %orr.3, bf16[2,192,192]{2,1,0:T(8,128)(2,1)} %ul.3, ...), custom_call_target="tpu_custom_call" | custom-call | bytes 1048576 | tf_op jit(solution)/shard_map/pack_weights/pallas_call | solution.py:160
  4.1 3.0 %collective-permute-start.1 = (bf16[176,384]{1,0:T(8,128)(2,1)}, bf16[176,384]{1,0:T(8,128)(2,1)S(1)}, u32[]{:S(2)}, u32[]{:S(2)}) collective-permute-start(bf16[176,384]{1,0:T(8,128)(2,1)} %get-tuple-element.106.mine), channel_id=1, source_target_pairs={{0,1},{1,0},{2,3},{3,2},{4,5},{5,4},{6,7},{7,6},{8,9},{9,8},{10,11... | collective-permute-start | bytes 405512 | tf_op jit(solution)/shard_map/ppermute | solution.py:942
  7.1 4.5 %collective-permute-done.1.refs_0_ = bf16[176,384]{1,0:T(8,128)(2,1)S(1)} collective-permute-done((bf16[176,384]{1,0:T(8,128)(2,1)}, bf16[176,384]{1,0:T(8,128)(2,1)S(1)}, u32[]{:S(2)}, u32[]{:S(2)}) %collective-permute-start.1) | collective-permute-done | bytes 135200 | tf_op jit(solution)/shard_map/ppermute | solution.py:942
  11.7 2.1 %collective-permute-start.5 = (bf16[176,384]{1,0:T(8,128)(2,1)S(1)}, bf16[176,384]{1,0:T(8,128)(2,1)S(1)}, u32[]{:S(2)}, u32[]{:S(2)}) collective-permute-start(bf16[176,384]{1,0:T(8,128)(2,1)S(1)} %collective-permute-done.1.refs_0_), channel_id=1, source_target_pairs={{0,8},{2,10},{4,12},{6,14},{8,0},{10,2},{12,4},{14,6},{16,24},{18,... | collective-permute-start | bytes 405512 | tf_op jit(solution)/shard_map/ppermute | solution.py:946
  13.9 1.6 collective-permute-start
  17.0 1.8 collective-permute-start.7
  18.8 2.1 %constant_dynamic-slice_fusion = bf16[1024,384]{1,0:T(8,128)(2,1)} fusion(bf16[2048,384]{1,0:T(8,128)(2,1)} %own.5, s32[]{:T(128)S(6)} %select_n.10), kind=kLoop, calls=%fused_computation.16 | loop fusion | bytes 1572868 | tf_op jit(solution)/shard_map/dynamic_slice | solution.py:1049
  20.9 1.6 collective-permute-start.13
  22.5 1.6 collective-permute-start.11
  28.3 3.8 %filter_spectrum.1 = (f32[768,128]{1,0:T(8,128)}, f32[768,256]{1,0:T(8,128)}, f32[8,128]{1,0:T(8,128)}, f32[768,128]{1,0:T(8,128)}) custom-call(s32[6]{0:T(128)} %stack.34.s_ref, bf16[128,384]{1,0:T(8,128)(2,1)} %own.3, bf16[176,384]{1,0:T(8,128)(2,1)} %get-tuple-element.106.mine, bf16[176,384]{1,0:T(8,128)(2,1)} %copy-done.20, bf16[176,384]{1,0:T(8,128)(2,1)} %copy-done.23, ...), custom_call_target="tpu_custom_call" | custom-call | bytes 1048576 | tf_op jit(solution)/shard_map/filter_spectrum/pallas_call | solution.py:224
  34.6 12.5 %mixer_forward.1 = (bf16[768,1024]{1,0:T(8,128)(2,1)}, bf16[2,768,1024]{2,1,0:T(8,128)(2,1)}, bf16[5,768,1024]{2,1,0:T(8,128)(2,1)}, f32[8,1024]{1,0:T(8,128)}, ...) custom-call(s32[6]{0:T(128)} %stack.34.s_ref, ...), custom_call_target="tpu_custom_call" | custom-call | flops 3072000000 | bytes 20480000 | tf_op jit(solution)/shard_map/mixer_forward/pallas_call | solution.py:335
  47.7 2.4 %collective-permute-done.13.oth = bf16[1024,384]{1,0:T(8,128)(2,1)S(1)} collective-permute-done((bf16[1024,384]{1,0:T(8,128)(2,1)}, bf16[1024,384]{1,0:T(8,128)(2,1)S(1)}, u32[]{:S(2)}, u32[]{:S(2)}) %collective-permute-start.13) | collective-permute-done | bytes 786464 | tf_op jit(solution)/shard_map/ppermute | solution.py:942
  50.2 29.3 %dense.1 = (bf16[2048,384]{1,0:T(8,128)(2,1)}, bf16[1024,384]{1,0:T(8,128)(2,1)S(1)}, bf16[768,1024]{1,0:T(8,128)(2,1)S(1)}, bf16[2,1280,384]{2,1,0:T(8,128)(2,1...) custom-call(s32[6]{0:T(128)S(1)} %copy-done.7, bf16[768,1024]{1,0:T(8,128)(2,1)} %get-tuple-element.114.middle, ...), custom_call_target="tpu_custom_call" | custom-call | flops 16384000000 | bytes 10240000 | tf_op jit(solution)/shard_map/dense/pallas_call | solution.py:552
  80.7 3.0 %collective-permute-done.18.refs_4_.refs_5_.refs_6_.refs_7_ = bf16[2,1280,384]{2,1,0:T(8,128)(2,1)S(1)} collective-permute-done((bf16[2,1280,384]{2,1,0:T(8,128)(2,1)}, bf16[2,1280,384]{2,1,0:T(8,128)(2,1)S(1)}, u32[]{:S(2)}, u32[]{:S(2)}) %collective-permute-start.18) | collective-permute-done | bytes 1966112 | tf_op jit(solution)/shard_map/ppermute | solution.py:946
  86.4 1.8 collective-permute-start.19
  90.0 20.1 %mixer_backward.1 = (f32[2048,384]{1,0:T(8,128)}, bf16[1024,384]{1,0:T(8,128)(2,1)S(1)}, bf16[2,768,384]{2,1,0:T(8,128)(2,1)S(1)}, bf16[2,768,384]{2,1,0:T(8,128)(2,1)S(1)}) custom-call(s32[6]{0:T(128)S(1)} %copy-done.7, bf16[768,1024]{1,0:T(8,128)(2,1)S(1)} %get-tuple-element.126.grad_middle, bf16[2,768,1024]{2,1,0:T(8,128)(2,1)S(1)} %copy-done.13, ...), custom_call_target="tpu_custom_call" | custom-call | flops 12288000000 | bytes 20480000 | tf_op jit(solution)/shard_map/mixer_backward/pallas_call | solution.py:774
  111.7 2.8 %collective-permute-done.22.refs_4_.refs_5_.refs_6_.refs_7_ = bf16[2,768,384]{2,1,0:T(8,128)(2,1)S(1)} collective-permute-done((bf16[2,768,384]{2,1,0:T(8,128)(2,1)S(1)}, bf16[2,768,384]{2,1,0:T(8,128)(2,1)S(1)}, u32[]{:S(2)}, u32[]{:S(2)}) %collective-permute-start.22) | collective-permute-done | bytes 1179680 | tf_op jit(solution)/shard_map/ppermute | solution.py:946
  119.9 1.6 collective-permute-start.29
  121.5 2.6 %collective-permute-start.30 = (bf16[160,384]{1,0:T(8,128)(2,1)S(1)}, bf16[160,384]{1,0:T(8,128)(2,1)S(1)}, u32[]{:S(2)}, u32[]{:S(2)}) collective-permute-start(bf16[160,384]{1,0:T(8,128)(2,1)S(1)} %get-tuple-element.164), channel_id=1, source_target_pairs={{0,16},{2,18},{4,20},{6,22},{8,24},{10,26},{12,28},{14,30},{16,0},... | collective-permute-start | bytes 368648 | tf_op jit(solution)/shard_map/ppermute | solution.py:957
  125.3 3.6 %collective-permute-start.31 = (bf16[160,384]{1,0:T(8,128)(2,1)S(1)}, bf16[160,384]{1,0:T(8,128)(2,1)S(1)}, u32[]{:S(2)}, u32[]{:S(2)}) collective-permute-start(bf16[160,384]{1,0:T(8,128)(2,1)S(1)} %get-tuple-element.165), channel_id=1, source_target_pairs={{0,24},{2,26},{4,28},{6,30},{8,16},{10,18},{12,20},{14,22},{16,8},... | collective-permute-start | bytes 368648 | tf_op jit(solution)/shard_map/ppermute | solution.py:957
  130.1 1.6 collective-permute-done.25.d
  133.5 3.7 %collective-permute-start.34 = (bf16[160,384]{1,0:T(8,128)(2,1)S(1)}, bf16[160,384]{1,0:T(8,128)(2,1)S(1)}, u32[]{:S(2)}, u32[]{:S(2)}) collective-permute-start(bf16[160,384]{1,0:T(8,128)(2,1)S(1)} %add_convert_fusion), channel_id=1, source_target_pairs={{0,24},{2,26},{4,28},{6,30},{8,16},{10,18},{12,20},{14,22},{16,8},... | collective-permute-start | bytes 368648 | tf_op jit(solution)/shard_map/ppermute | solution.py:957
  139.2 2.4 %collective-permute-done.34 = bf16[160,384]{1,0:T(8,128)(2,1)S(1)} collective-permute-done((bf16[160,384]{1,0:T(8,128)(2,1)S(1)}, bf16[160,384]{1,0:T(8,128)(2,1)S(1)}, u32[]{:S(2)}, u32[]{:S(2)}) %collective-permute-start.34) | collective-permute-done | bytes 122912 | tf_op jit(solution)/shard_map/ppermute | solution.py:957
  141.6 5.6 %collective-permute-start.27 = (bf16[96,384]{1,0:T(8,128)(2,1)S(1)}, bf16[96,384]{1,0:T(8,128)(2,1)S(1)}, u32[]{:S(2)}, u32[]{:S(2)}) collective-permute-start(bf16[96,384]{1,0:T(8,128)(2,1)S(1)} %get-tuple-element.156), channel_id=1, source_target_pairs={{0,16},{2,18},{4,20},{6,22},{8,24},{10,26},{12,28},{14,30},{16,0},... | collective-permute-start | bytes 221192 | tf_op jit(solution)/shard_map/ppermute | solution.py:957
  147.6 3.8 %collective-permute-start.28 = (bf16[96,384]{1,0:T(8,128)(2,1)S(1)}, bf16[96,384]{1,0:T(8,128)(2,1)S(1)}, u32[]{:S(2)}, u32[]{:S(2)}) collective-permute-start(bf16[96,384]{1,0:T(8,128)(2,1)S(1)} %get-tuple-element.157), channel_id=1, source_target_pairs={{0,24},{2,26},{4,28},{6,30},{8,16},{10,18},{12,20},{14,22},{16,8},... | collective-permute-start | bytes 221192 | tf_op jit(solution)/shard_map/ppermute | solution.py:957
  151.4 1.6 collective-permute-start.43
  155.3 3.9 %collective-permute-start.38 = (bf16[96,384]{1,0:T(8,128)(2,1)S(1)}, bf16[96,384]{1,0:T(8,128)(2,1)S(1)}, u32[]{:S(2)}, u32[]{:S(2)}) collective-permute-start(bf16[96,384]{1,0:T(8,128)(2,1)S(1)} %add_convert_fusion.1), channel_id=1, source_target_pairs={{0,24},{2,26},{4,28},{6,30},{8,16},{10,18},{12,20},{14,22},{16,8},... | collective-permute-start | bytes 221192 | tf_op jit(solution)/shard_map/ppermute | solution.py:957
  159.8 3.8 %collective-permute-done.36 = bf16[96,384]{1,0:T(8,128)(2,1)S(1)} collective-permute-done((bf16[96,384]{1,0:T(8,128)(2,1)S(1)}, bf16[96,384]{1,0:T(8,128)(2,1)S(1)}, u32[]{:S(2)}, u32[]{:S(2)}) %collective-permute-start.36) | collective-permute-done | bytes 73760 | tf_op jit(solution)/shard_map/ppermute | solution.py:957
  168.5 2.8 %dense_unpack.1 = (f32[384]{0:T(512)}, f32[2,192,192]{2,1,0:T(8,128)}, f32[2,192,1536]{2,1,0:T(8,128)}, f32[2,192,768]{2,1,0:T(8,128)}) custom-call(s32[6]{0:T(128)S(1)} %copy-done.7, bf16[640,384]{1,0:T(8,128)(2,1)S(1)} %pad_maximum_fusion.p0, bf16[640,384]{1,0:T(8,128)(2,1)S(1)} %collective-permute-done.40.p1, ...), custom_call_target="tpu_custom_call" | custom-call | bytes 1048576 | tf_op jit(solution)/shard_map/dense_unpack/pallas_call | solution.py:847
  171.3 3.8 %collective-permute-done.39.p1 = bf16[384,384]{1,0:T(8,128)(2,1)S(1)} collective-permute-done((bf16[384,384]{1,0:T(8,128)(2,1)S(1)}, bf16[384,384]{1,0:T(8,128)(2,1)S(1)}, u32[]{:S(2)}, u32[]{:S(2)}) %collective-permute-start.39) | collective-permute-done | bytes 294944 | tf_op jit(solution)/shard_map/ppermute | solution.py:946
  175.1 1.6 collective-permute-done.45.p3
  176.7 2.3 %mixer_unpack.1 = (f32[384]{0:T(512)}, f32[384]{0:T(512)}, f32[384]{0:T(512)}, f32[384]{0:T(512)}, f32[128,384]{1,0:T(8,128)}, /*index=5*/f32[2,192,192]{2,1,0:T...) custom-call(s32[6]{0:T(128)S(1)} %copy-done.7, ...), custom_call_target="tpu_custom_call" | custom-call | bytes 1048576 | tf_op jit(solution)/shard_map/mixer_unpack/pallas_call | solution.py:847
  (162 shorter events, 36.3 us)
Async XLA Ops:
  4.1 7.6 %collective-permute-start.1 = (bf16[176,384]{1,0:T(8,128)(2,1)}, bf16[176,384]{1,0:T(8,128)(2,1)S(1)}, u32[]{:S(2)}, u32[]{:S(2)}) collective-permute-start(bf16[176,384]{1,0:T(8,128)(2,1)} %get-tuple-element.106.mine), channel_id=1, source_target_pairs={{0,1},{1,0},{2,3},{3,2},{4,5},{5,4},{6,7},{7,6},{8,9},{9,8},{10,11... | collective-permute-start | bytes 405512 | tf_op jit(solution)/shard_map/ppermute | solution.py:942
  7.1 11.7 %collective-permute-start.9 = (bf16[336,384]{1,0:T(8,128)(2,1)}, bf16[336,384]{1,0:T(8,128)(2,1)S(1)}, u32[]{:S(2)}, u32[]{:S(2)}) collective-permute-start(bf16[336,384]{1,0:T(8,128)(2,1)} %get-tuple-element.108), channel_id=1, source_target_pairs={{0,1},{1,0},{2,3},{3,2},{4,5},{5,4},{6,7},{7,6},{8,9},{9,8},{10,11... | collective-permute-start | bytes 774152 | tf_op jit(solution)/shard_map/ppermute | solution.py:942
  13.9 20.7 %collective-permute-start = (bf16[1024,384]{1,0:T(8,128)(2,1)S(1)}, bf16[1024,384]{1,0:T(8,128)(2,1)}, u32[]{:S(2)}, u32[]{:S(2)}) collective-permute-start(bf16[1024,384]{1,0:T(8,128)(2,1)S(1)} %constant_dynamic-slice_fusion.1), channel_id=1, source_target_pairs={{0,1},{1,0},{2,3},{3,2},{4,5},{5,4},{6,7},{7,6},{8,9},{9,8},{10,11... | collective-permute-start | bytes 2359304 | tf_op jit(solution)/shard_map/ppermute | solution.py:942
  17.0 7.1 %collective-permute-start.7 = (bf16[176,384]{1,0:T(8,128)(2,1)S(1)}, bf16[176,384]{1,0:T(8,128)(2,1)S(1)}, u32[]{:S(2)}, u32[]{:S(2)}) collective-permute-start(bf16[176,384]{1,0:T(8,128)(2,1)S(1)} %collective-permute-done.5.refs_4_), channel_id=1, source_target_pairs={{0,4},{2,6},{4,0},{6,2},{8,12},{10,14},{12,8},{14,10},{16,20},{18,... | collective-permute-start | bytes 405512 | tf_op jit(solution)/shard_map/ppermute | solution.py:946
  20.9 29.1 %collective-permute-start.13 = (bf16[1024,384]{1,0:T(8,128)(2,1)}, bf16[1024,384]{1,0:T(8,128)(2,1)S(1)}, u32[]{:S(2)}, u32[]{:S(2)}) collective-permute-start(bf16[1024,384]{1,0:T(8,128)(2,1)} %constant_dynamic-slice_fusion), channel_id=1, source_target_pairs={{0,1},{1,0},{2,3},{3,2},{4,5},{5,4},{6,7},{7,6},{8,9},{9,8},{10,11... | collective-permute-start | bytes 2359304 | tf_op jit(solution)/shard_map/ppermute | solution.py:942
  22.5 9.6 %collective-permute-start.11 = (bf16[336,384]{1,0:T(8,128)(2,1)S(1)}, bf16[336,384]{1,0:T(8,128)(2,1)S(1)}, u32[]{:S(2)}, u32[]{:S(2)}) collective-permute-start(bf16[336,384]{1,0:T(8,128)(2,1)S(1)} %collective-permute-done.9.p0), channel_id=1, source_target_pairs={{0,8},{2,10},{4,12},{6,14},{8,0},{10,2},{12,4},{14,6},{16,24},{18,... | collective-permute-start | bytes 774152 | tf_op jit(solution)/shard_map/ppermute | solution.py:946
  24.1 8.1 %collective-permute-start.10 = (bf16[336,384]{1,0:T(8,128)(2,1)S(1)}, bf16[336,384]{1,0:T(8,128)(2,1)S(1)}, u32[]{:S(2)}, u32[]{:S(2)}) collective-permute-start(bf16[336,384]{1,0:T(8,128)(2,1)S(1)} %collective-permute-done.9.p0), channel_id=1, source_target_pairs={{0,4},{2,6},{4,0},{6,2},{8,12},{10,14},{12,8},{14,10},{16,20},{18,... | collective-permute-start | bytes 774152 | tf_op jit(solution)/shard_map/ppermute | solution.py:946
  32.2 17.9 %collective-permute-start.16 = (bf16[336,384]{1,0:T(8,128)(2,1)S(1)}, bf16[336,384]{1,0:T(8,128)(2,1)}, u32[]{:S(2)}, u32[]{:S(2)}) collective-permute-start(bf16[336,384]{1,0:T(8,128)(2,1)S(1)} %collective-permute-done.11.p4), channel_id=1, source_target_pairs={{0,2},{2,0},{4,6},{6,4},{8,10},{10,8},{12,14},{14,12},{16,18},{18,... | collective-permute-start | bytes 774152 | tf_op jit(solution)/shard_map/ppermute | solution.py:946
  32.4 14.8 %collective-permute-start.12 = (bf16[336,384]{1,0:T(8,128)(2,1)S(1)}, bf16[336,384]{1,0:T(8,128)(2,1)}, u32[]{:S(2)}, u32[]{:S(2)}) collective-permute-start(bf16[336,384]{1,0:T(8,128)(2,1)S(1)} %collective-permute-done.11.p4), channel_id=1, source_target_pairs={{0,4},{2,6},{4,0},{6,2},{8,12},{10,14},{12,8},{14,10},{16,20},{18,... | collective-permute-start | bytes 774152 | tf_op jit(solution)/shard_map/ppermute | solution.py:946
  33.6 16.5 %collective-permute-start.14 = (bf16[336,384]{1,0:T(8,128)(2,1)S(1)}, bf16[336,384]{1,0:T(8,128)(2,1)}, u32[]{:S(2)}, u32[]{:S(2)}) collective-permute-start(bf16[336,384]{1,0:T(8,128)(2,1)S(1)} %collective-permute-done.9.p0), channel_id=1, source_target_pairs={{0,2},{2,0},{4,6},{6,4},{8,10},{10,8},{12,14},{14,12},{16,18},{18,... | collective-permute-start | bytes 774152 | tf_op jit(solution)/shard_map/ppermute | solution.py:946
  34.5 15.6 %collective-permute-start.15 = (bf16[336,384]{1,0:T(8,128)(2,1)S(1)}, bf16[336,384]{1,0:T(8,128)(2,1)}, u32[]{:S(2)}, u32[]{:S(2)}) collective-permute-start(bf16[336,384]{1,0:T(8,128)(2,1)S(1)} %collective-permute-done.10.p2), channel_id=1, source_target_pairs={{0,2},{2,0},{4,6},{6,4},{8,10},{10,8},{12,14},{14,12},{16,18},{18,... | collective-permute-start | bytes 774152 | tf_op jit(solution)/shard_map/ppermute | solution.py:946
  86.4 23.7 %collective-permute-start.19 = (bf16[640,384]{1,0:T(8,128)(2,1)S(1)}, bf16[640,384]{1,0:T(8,128)(2,1)S(1)}, u32[]{:S(2)}, u32[]{:S(2)}) collective-permute-start(bf16[640,384]{1,0:T(8,128)(2,1)S(1)} %get-tuple-element.139), channel_id=1, source_target_pairs={{0,4},{2,6},{4,0},{6,2},{8,12},{10,14},{12,8},{14,10},{16,20},{18,... | collective-permute-start | bytes 1474568 | tf_op jit(solution)/shard_map/ppermute | solution.py:946
  88.1 23.5 %collective-permute-start.20 = (bf16[640,384]{1,0:T(8,128)(2,1)S(1)}, bf16[640,384]{1,0:T(8,128)(2,1)S(1)}, u32[]{:S(2)}, u32[]{:S(2)}) collective-permute-start(bf16[640,384]{1,0:T(8,128)(2,1)S(1)} %get-tuple-element.140), channel_id=1, source_target_pairs={{0,1},{1,0},{2,3},{3,2},{4,5},{5,4},{6,7},{7,6},{8,9},{9,8},{10,11... | collective-permute-start | bytes 1474568 | tf_op jit(solution)/shard_map/ppermute | solution.py:942
  89.7 22.0 %collective-permute-start.21 = (bf16[640,384]{1,0:T(8,128)(2,1)S(1)}, bf16[640,384]{1,0:T(8,128)(2,1)S(1)}, u32[]{:S(2)}, u32[]{:S(2)}) collective-permute-start(bf16[640,384]{1,0:T(8,128)(2,1)S(1)} %get-tuple-element.141), channel_id=1, source_target_pairs={{0,5},{1,4},{2,7},{3,6},{4,1},{5,0},{6,3},{7,2},{8,13},{9,12},{10,... | collective-permute-start | bytes 1474568 | tf_op jit(solution)/shard_map/ppermute | solution.py:951
  115.4 9.9 %collective-permute-start.23 = (bf16[384,384]{1,0:T(8,128)(2,1)S(1)}, bf16[384,384]{1,0:T(8,128)(2,1)S(1)}, u32[]{:S(2)}, u32[]{:S(2)}) collective-permute-start(bf16[384,384]{1,0:T(8,128)(2,1)S(1)} %get-tuple-element.145), channel_id=1, source_target_pairs={{0,4},{2,6},{4,0},{6,2},{8,12},{10,14},{12,8},{14,10},{16,20},{18,... | collective-permute-start | bytes 884744 | tf_op jit(solution)/shard_map/ppermute | solution.py:946
  116.6 13.5 %collective-permute-start.24 = (bf16[384,384]{1,0:T(8,128)(2,1)S(1)}, bf16[384,384]{1,0:T(8,128)(2,1)S(1)}, u32[]{:S(2)}, u32[]{:S(2)}) collective-permute-start(bf16[384,384]{1,0:T(8,128)(2,1)S(1)} %get-tuple-element.146), channel_id=1, source_target_pairs={{0,1},{1,0},{2,3},{3,2},{4,5},{5,4},{6,7},{7,6},{8,9},{9,8},{10,11... | collective-permute-start | bytes 884744 | tf_op jit(solution)/shard_map/ppermute | solution.py:942
  117.5 14.3 %collective-permute-start.25 = (bf16[384,384]{1,0:T(8,128)(2,1)S(1)}, bf16[384,384]{1,0:T(8,128)(2,1)S(1)}, u32[]{:S(2)}, u32[]{:S(2)}) collective-permute-start(bf16[384,384]{1,0:T(8,128)(2,1)S(1)} %get-tuple-element.147), channel_id=1, source_target_pairs={{0,5},{1,4},{2,7},{3,6},{4,1},{5,0},{6,3},{7,2},{8,13},{9,12},{10,... | collective-permute-start | bytes 884744 | tf_op jit(solution)/shard_map/ppermute | solution.py:951
  119.9 13.5 %collective-permute-start.29 = (bf16[160,384]{1,0:T(8,128)(2,1)S(1)}, bf16[160,384]{1,0:T(8,128)(2,1)S(1)}, u32[]{:S(2)}, u32[]{:S(2)}) collective-permute-start(bf16[160,384]{1,0:T(8,128)(2,1)S(1)} %get-tuple-element.163), channel_id=1, source_target_pairs={{0,8},{2,10},{4,12},{6,14},{8,0},{10,2},{12,4},{14,6},{16,24},{18,... | collective-permute-start | bytes 368648 | tf_op jit(solution)/shard_map/ppermute | solution.py:957
  121.5 11.9 %collective-permute-start.30 = (bf16[160,384]{1,0:T(8,128)(2,1)S(1)}, bf16[160,384]{1,0:T(8,128)(2,1)S(1)}, u32[]{:S(2)}, u32[]{:S(2)}) collective-permute-start(bf16[160,384]{1,0:T(8,128)(2,1)S(1)} %get-tuple-element.164), channel_id=1, source_target_pairs={{0,16},{2,18},{4,20},{6,22},{8,24},{10,26},{12,28},{14,30},{16,0},... | collective-permute-start | bytes 368648 | tf_op jit(solution)/shard_map/ppermute | solution.py:957
  125.3 8.2 %collective-permute-start.31 = (bf16[160,384]{1,0:T(8,128)(2,1)S(1)}, bf16[160,384]{1,0:T(8,128)(2,1)S(1)}, u32[]{:S(2)}, u32[]{:S(2)}) collective-permute-start(bf16[160,384]{1,0:T(8,128)(2,1)S(1)} %get-tuple-element.165), channel_id=1, source_target_pairs={{0,24},{2,26},{4,28},{6,30},{8,16},{10,18},{12,20},{14,22},{16,8},... | collective-permute-start | bytes 368648 | tf_op jit(solution)/shard_map/ppermute | solution.py:957
  132.5 21.3 %collective-permute-start.35 = (bf16[1024,384]{1,0:T(8,128)(2,1)S(1)}, bf16[1024,384]{1,0:T(8,128)(2,1)S(1)}, u32[]{:S(2)}, u32[]{:S(2)}) collective-permute-start(bf16[1024,384]{1,0:T(8,128)(2,1)S(1)} %get-tuple-element.166), channel_id=1, source_target_pairs={{0,1},{1,0},{2,3},{3,2},{4,5},{5,4},{6,7},{7,6},{8,9},{9,8},{10,11... | collective-permute-start | bytes 2359304 | tf_op jit(solution)/shard_map/ppermute | solution.py:942
  133.5 8.1 %collective-permute-start.34 = (bf16[160,384]{1,0:T(8,128)(2,1)S(1)}, bf16[160,384]{1,0:T(8,128)(2,1)S(1)}, u32[]{:S(2)}, u32[]{:S(2)}) collective-permute-start(bf16[160,384]{1,0:T(8,128)(2,1)S(1)} %add_convert_fusion), channel_id=1, source_target_pairs={{0,24},{2,26},{4,28},{6,30},{8,16},{10,18},{12,20},{14,22},{16,8},... | collective-permute-start | bytes 368648 | tf_op jit(solution)/shard_map/ppermute | solution.py:957
  137.2 10.3 %collective-permute-start.33 = (bf16[160,384]{1,0:T(8,128)(2,1)S(1)}, bf16[160,384]{1,0:T(8,128)(2,1)S(1)}, u32[]{:S(2)}, u32[]{:S(2)}) collective-permute-start(bf16[160,384]{1,0:T(8,128)(2,1)S(1)} %add_convert_fusion), channel_id=1, source_target_pairs={{0,16},{2,18},{4,20},{6,22},{8,24},{10,26},{12,28},{14,30},{16,0},... | collective-permute-start | bytes 368648 | tf_op jit(solution)/shard_map/ppermute | solution.py:957
  137.2 14.2 %collective-permute-start.32 = (bf16[160,384]{1,0:T(8,128)(2,1)S(1)}, bf16[160,384]{1,0:T(8,128)(2,1)S(1)}, u32[]{:S(2)}, u32[]{:S(2)}) collective-permute-start(bf16[160,384]{1,0:T(8,128)(2,1)S(1)} %add_convert_fusion), channel_id=1, source_target_pairs={{0,8},{2,10},{4,12},{6,14},{8,0},{10,2},{12,4},{14,6},{16,24},{18,... | collective-permute-start | bytes 368648 | tf_op jit(solution)/shard_map/ppermute | solution.py:957
  138.0 15.1 %collective-permute-start.26 = (bf16[96,384]{1,0:T(8,128)(2,1)S(1)}, bf16[96,384]{1,0:T(8,128)(2,1)S(1)}, u32[]{:S(2)}, u32[]{:S(2)}) collective-permute-start(bf16[96,384]{1,0:T(8,128)(2,1)S(1)} %get-tuple-element.155), channel_id=1, source_target_pairs={{0,8},{2,10},{4,12},{6,14},{8,0},{10,2},{12,4},{14,6},{16,24},{18,... | collective-permute-start | bytes 221192 | tf_op jit(solution)/shard_map/ppermute | solution.py:957
  141.6 11.4 %collective-permute-start.27 = (bf16[96,384]{1,0:T(8,128)(2,1)S(1)}, bf16[96,384]{1,0:T(8,128)(2,1)S(1)}, u32[]{:S(2)}, u32[]{:S(2)}) collective-permute-start(bf16[96,384]{1,0:T(8,128)(2,1)S(1)} %get-tuple-element.156), channel_id=1, source_target_pairs={{0,16},{2,18},{4,20},{6,22},{8,24},{10,26},{12,28},{14,30},{16,0},... | collective-permute-start | bytes 221192 | tf_op jit(solution)/shard_map/ppermute | solution.py:957
  147.6 6.2 %collective-permute-start.28 = (bf16[96,384]{1,0:T(8,128)(2,1)S(1)}, bf16[96,384]{1,0:T(8,128)(2,1)S(1)}, u32[]{:S(2)}, u32[]{:S(2)}) collective-permute-start(bf16[96,384]{1,0:T(8,128)(2,1)S(1)} %get-tuple-element.157), channel_id=1, source_target_pairs={{0,24},{2,26},{4,28},{6,30},{8,16},{10,18},{12,20},{14,22},{16,8},... | collective-permute-start | bytes 221192 | tf_op jit(solution)/shard_map/ppermute | solution.py:957
  151.4 16.8 %collective-permute-start.43 = (bf16[1024,384]{1,0:T(8,128)(2,1)S(1)}, bf16[1024,384]{1,0:T(8,128)(2,1)S(1)}, u32[]{:S(2)}, u32[]{:S(2)}) collective-permute-start(bf16[1024,384]{1,0:T(8,128)(2,1)S(1)} %get-tuple-element.176), channel_id=1, source_target_pairs={{0,1},{1,0},{2,3},{3,2},{4,5},{5,4},{6,7},{7,6},{8,9},{9,8},{10,11... | collective-permute-start | bytes 2359304 | tf_op jit(solution)/shard_map/ppermute | solution.py:942
  153.8 11.8 %collective-permute-start.40 = (bf16[640,384]{1,0:T(8,128)(2,1)S(1)}, bf16[640,384]{1,0:T(8,128)(2,1)S(1)}, u32[]{:S(2)}, u32[]{:S(2)}) collective-permute-start(bf16[640,384]{1,0:T(8,128)(2,1)S(1)} %pad_maximum_fusion.p0), channel_id=1, source_target_pairs={{0,4},{2,6},{4,0},{6,2},{8,12},{10,14},{12,8},{14,10},{16,20},{18,... | collective-permute-start | bytes 1474568 | tf_op jit(solution)/shard_map/ppermute | solution.py:946
  155.3 10.3 %collective-permute-start.38 = (bf16[96,384]{1,0:T(8,128)(2,1)S(1)}, bf16[96,384]{1,0:T(8,128)(2,1)S(1)}, u32[]{:S(2)}, u32[]{:S(2)}) collective-permute-start(bf16[96,384]{1,0:T(8,128)(2,1)S(1)} %add_convert_fusion.1), channel_id=1, source_target_pairs={{0,24},{2,26},{4,28},{6,30},{8,16},{10,18},{12,20},{14,22},{16,8},... | collective-permute-start | bytes 221192 | tf_op jit(solution)/shard_map/ppermute | solution.py:957
  165.6 9.5 %collective-permute-start.39 = (bf16[384,384]{1,0:T(8,128)(2,1)S(1)}, bf16[384,384]{1,0:T(8,128)(2,1)S(1)}, u32[]{:S(2)}, u32[]{:S(2)}) collective-permute-start(bf16[384,384]{1,0:T(8,128)(2,1)S(1)} %constant_dynamic-update-slice_fusion.p0), channel_id=1, source_target_pairs={{0,4},{2,6},{4,0},{6,2},{8,12},{10,14},{12,8},{14,10},{16,20},{18,... | collective-permute-start | bytes 884744 | tf_op jit(solution)/shard_map/ppermute | solution.py:946
  168.4 6.8 %collective-permute-start.44 = (bf16[384,384]{1,0:T(8,128)(2,1)S(1)}, bf16[384,384]{1,0:T(8,128)(2,1)S(1)}, u32[]{:S(2)}, u32[]{:S(2)}) collective-permute-start(bf16[384,384]{1,0:T(8,128)(2,1)S(1)} %constant_dynamic-update-slice_fusion.p0), channel_id=1, source_target_pairs={{0,2},{2,0},{4,6},{6,4},{8,10},{10,8},{12,14},{14,12},{16,18},{18,... | collective-permute-start | bytes 884744 | tf_op jit(solution)/shard_map/ppermute | solution.py:946
  (48 other events, 375.0 us)

commit v2 on v1

--- a/solution.py
+++ b/solution.py
@@ -476,7 +476,9 @@
 
     @pl.when(pl.program_id(0) == steps - 1)
     def _():
-        sums = exact_nt(jnp.ones((16, LEN), f32), ggain[...]).astype(bf16)
+        lane = lax.broadcasted_iota(jnp.int32, (D, LEN), 1)
+        sums = jnp.where(lane == 0, jnp.sum(ggain[...], axis=1, keepdims=True), 0.0)
+        sums = sums.T[:16, :].astype(bf16)
 
         def write(dst, j):
             part = BS // 2
@@ -637,22 +639,20 @@
         grad_mixed = nn(wol[b], returned)
         gate = kept[1, rows, :].astype(f32)
         inner = kept[3, rows, :].astype(f32)
-        gol[b] += nt((gate * inner).astype(bf16), returned)
+        gol[b] += nt(kept[1, rows, :] * kept[3, rows, :], returned)
         grad_inner = grad_mixed * gate
         inner_grad[rows, :] = grad_inner
         conv[rows, :] = grad_inner.astype(bf16)
         proj[b * 3 * BS + BS : b * 3 * BS + 2 * BS, :] = (grad_mixed * inner).astype(bf16)
-        source = (
-            kept[0, rows, :].astype(f32) * kept[2, rows, :].astype(f32) * valid
-        ).astype(bf16)
+        source = kept[0, rows, :] * kept[2, rows, :] * valid.astype(bf16)
         half[rows, :] = source
         gskip[rows, :] += fold(grad_inner * source.astype(f32))
     hc, hs = spec[:, :LEN], spec[:, LEN:]
     for s in range(BACK_TILE // LEN):
         lanes = slice(s * LEN, (s + 1) * LEN)
-        wave = nn(conv[:, lanes], fwd[...])
-        wc, ws = wave[:, :LEN], wave[:, LEN:]
-        seen = nn(half[:, lanes], fwd[...])
+        wave = nn(jnp.concatenate([conv[:, lanes], half[:, lanes]], axis=0), fwd[...])
+        wc, ws = wave[:D, :LEN], wave[:D, LEN:]
+        seen = wave[D:]
         sc, ss = seen[:, :LEN], seen[:, LEN:]
         gspec[:, :LEN] += wc * sc + ws * ss
         gspec[:, LEN:] += ws * sc - wc * ss
@@ -662,12 +662,10 @@
         total[:, lanes] = nn(product, inv[...])
     for g in range(NB):
         rows = slice(g * BS, (g + 1) * BS)
-        grad_source = (total[rows, :] + cols[rows, 3:4] * inner_grad[rows, :]) * valid
+        grad_source = ((total[rows, :] + cols[rows, 3:4] * inner_grad[rows, :]) * valid).astype(bf16)
         start = g * 3 * BS
-        proj[start : start + BS, :] = (grad_source * kept[2, rows, :].astype(f32)).astype(bf16)
-        proj[start + 2 * BS : start + 3 * BS, :] = (
-            grad_source * kept[0, rows, :].astype(f32)
-        ).astype(bf16)
+        proj[start : start + BS, :] = grad_source * kept[2, rows, :]
+        proj[start + 2 * BS : start + 3 * BS, :] = grad_source * kept[0, rows, :]
 
     masked = marks[1:2, :]
     for g in range(NB):
@@ -703,12 +701,11 @@
         low = (decayed - high.astype(f32)).astype(bf16)
         sum_weight = (nt(feats[0], high) + nt(feats[1], high) + nt(feats[0], low)).astype(bf16)
         grad_decay = grad_taps * tap * (-positions)
-        ones = jnp.ones((16, LEN), f32)
-        line = lax.broadcasted_iota(jnp.int32, (16, D), 0)
-        vectors = exact_nt(ones, gmask[...])
-        vectors = jnp.where(line == 1, exact_nt(ones, ggain[...]), vectors)
-        vectors = jnp.where(line == 2, exact_nt(ones, gskip[...]), vectors)
-        vectors = jnp.where(line == 3, exact_nt(ones, grad_decay), vectors).astype(bf16)
+        lane = lax.broadcasted_iota(jnp.int32, (D, LEN), 1)
+        vectors = jnp.zeros((D, LEN), f32)
+        for index, item in enumerate((gmask[...], ggain[...], gskip[...], grad_decay)):
+            vectors = jnp.where(lane == index, jnp.sum(item, axis=1, keepdims=True), vectors)
+        vectors = vectors.T[:16, :].astype(bf16)
 
         def write(dst, j):
             part = BS // 2
@@ -1098,6 +1095,7 @@
     mix_keep, mix_send, ffn_parts = tie(mix_keep, mix_send, ffn_parts)
     mix_got = swap_wide(mix_send, 0, wide_size)
     ffn_parts = columns(scalars, ffn_parts)
+    mix_got, ffn_parts = tie(mix_got, ffn_parts)
     mix_parts = corners(scalars, mix_keep, mix_got)
 
     ffn_parts = over_columns(ffn_parts, wide_size)

time: 179 us -> 179 us (level)
  Pallas kernels: 77.3 us -> 75 us
    ppermute x8, waiting for transfers between devices: 11.8 us -> 14.4 us  [swap_narrow(): return lax.ppermute(values, 'narrow', [(0, 1), (1, 0)])]
    pallas_call x1, Pallas kernels: 20.1 us -> 17.9 us  [mixer_backward(): pl.pallas_call(functools.partial(mixer_backward_kernel, steps=steps, shar...]
    ppermute x24, waiting for transfers between devices: 15.2 us -> 13.4 us  [swap_wide(): lax.ppermute(values, 'wide', [(i, i ^ 1 << bit) for i in range(size)])]
  transfers between devices with their start and end apart: 46 -> 46, of which waited for: 20 -> 19; matrix products, arithmetic and copies ran while one was open for 3% -> 3% of each run, Pallas kernels for 23% -> 22%
where the time goes in v2:
time: 179 us; the launch traced here: 178 us
  Pallas kernels  75 us (42%)
  starting transfers between devices  56.4 us (32%)
  waiting for transfers between devices  37.7 us (21%)
  local copies, waits for them, and re-layouts  7.41 us (4%)
    pallas_call x1, Pallas kernels, dense(): pl.pallas_call(functools.partial(dense_kernel, steps=steps), out_shape=tu...  29.1 us
    ppermute x12, starting transfers between devices, shift_wide(): return lax.ppermute(values, 'wide', [(i, i ^ flip) for i in range(size)])  27.8 us
    pallas_call x1, Pallas kernels, mixer_backward(): pl.pallas_call(functools.partial(mixer_backward_kernel, steps=steps, shar...  17.9 us
    ppermute x24, starting transfers between devices, swap_wide(): lax.ppermute(values, 'wide', [(i, i ^ 1 << bit) for i in range(size)])  15.9 us
    ppermute x8, waiting for transfers between devices, swap_narrow(): return lax.ppermute(values, 'narrow', [(0, 1), (1, 0)])  14.4 us
    ppermute x24, waiting for transfers between devices, swap_wide(): lax.ppermute(values, 'wide', [(i, i ^ 1 << bit) for i in range(size)])  13.4 us
    pallas_call x1, Pallas kernels, mixer_forward(): pl.pallas_call(mixer_forward_kernel, out_shape=tuple(outs), grid_spec=plt...  12.5 us
    ppermute x8, starting transfers between devices, swap_narrow(): return lax.ppermute(values, 'narrow', [(0, 1), (1, 0)])  11 us
  transfers between devices with their start and end apart: 46, of which 19 were waited for; matrix products, arithmetic and copies ran while one was open for 3% of the time, Pallas kernels for 22%

profile of v2, /device:TPU:0, one launch (start us, length us, event | category | flops | bytes accessed | tf_op | source)
XLA Modules:
  0.0 178.2 jit_solution(10288258653627509240)
XLA Ops:
  1.3 2.7 %pack_weights.1 = (bf16[176,384]{1,0:T(8,128)(2,1)}, bf16[336,384]{1,0:T(8,128)(2,1)}) custom-call(s32[6]{0:T(128)} %stack.34.s_ref, bf16[2,192,192]{2,1,0:T(8,128)(2,1)} %il.3, bf16[2,192,576]{2,1,0:T(8,128)(2,1)} %ir.3, bf16[2,192,192]{2,1,0:T(8,128)(2,1)} %ol.3, bf16[2,192,192]{2,1,0:T(8,128)(2,1)} %orr.3, bf16[2,192,192]{2,1,0:T(8,128)(2,1)} %ul.3, ...), custom_call_target="tpu_custom_call" | custom-call | bytes 1048576 | tf_op jit(solution)/shard_map/pack_weights/pallas_call | solution.py:160
  4.1 3.0 %collective-permute-start.1 = (bf16[176,384]{1,0:T(8,128)(2,1)}, bf16[176,384]{1,0:T(8,128)(2,1)S(1)}, u32[]{:S(2)}, u32[]{:S(2)}) collective-permute-start(bf16[176,384]{1,0:T(8,128)(2,1)} %get-tuple-element.111.mine), channel_id=1, source_target_pairs={{0,1},{1,0},{2,3},{3,2},{4,5},{5,4},{6,7},{7,6},{8,9},{9,8},{10,11... | collective-permute-start | bytes 405512 | tf_op jit(solution)/shard_map/ppermute | solution.py:939
  7.1 4.5 %collective-permute-done.1.refs_0_ = bf16[176,384]{1,0:T(8,128)(2,1)S(1)} collective-permute-done((bf16[176,384]{1,0:T(8,128)(2,1)}, bf16[176,384]{1,0:T(8,128)(2,1)S(1)}, u32[]{:S(2)}, u32[]{:S(2)}) %collective-permute-start.1) | collective-permute-done | bytes 135200 | tf_op jit(solution)/shard_map/ppermute | solution.py:939
  11.7 2.1 %collective-permute-start.5 = (bf16[176,384]{1,0:T(8,128)(2,1)S(1)}, bf16[176,384]{1,0:T(8,128)(2,1)S(1)}, u32[]{:S(2)}, u32[]{:S(2)}) collective-permute-start(bf16[176,384]{1,0:T(8,128)(2,1)S(1)} %collective-permute-done.1.refs_0_), channel_id=1, source_target_pairs={{0,8},{2,10},{4,12},{6,14},{8,0},{10,2},{12,4},{14,6},{16,24},{18,... | collective-permute-start | bytes 405512 | tf_op jit(solution)/shard_map/ppermute | solution.py:943
  13.9 1.6 collective-permute-start
  17.0 1.8 collective-permute-start.7
  18.8 2.1 %constant_dynamic-slice_fusion = bf16[1024,384]{1,0:T(8,128)(2,1)} fusion(bf16[2048,384]{1,0:T(8,128)(2,1)} %own.5, s32[]{:T(128)S(6)} %select_n.10), kind=kLoop, calls=%fused_computation.16 | loop fusion | bytes 1572868 | tf_op jit(solution)/shard_map/dynamic_slice | solution.py:1046
  20.9 1.6 collective-permute-start.13
  28.3 3.8 %filter_spectrum.1 = (f32[768,128]{1,0:T(8,128)}, f32[768,256]{1,0:T(8,128)}, f32[8,128]{1,0:T(8,128)}, f32[768,128]{1,0:T(8,128)}) custom-call(s32[6]{0:T(128)} %stack.34.s_ref, bf16[128,384]{1,0:T(8,128)(2,1)} %own.3, bf16[176,384]{1,0:T(8,128)(2,1)} %get-tuple-element.111.mine, bf16[176,384]{1,0:T(8,128)(2,1)} %copy-done.20, bf16[176,384]{1,0:T(8,128)(2,1)} %copy-done.23, ...), custom_call_target="tpu_custom_call" | custom-call | bytes 1048576 | tf_op jit(solution)/shard_map/filter_spectrum/pallas_call | solution.py:224
  34.6 12.5 %mixer_forward.1 = (bf16[768,1024]{1,0:T(8,128)(2,1)}, bf16[2,768,1024]{2,1,0:T(8,128)(2,1)}, bf16[5,768,1024]{2,1,0:T(8,128)(2,1)}, f32[8,1024]{1,0:T(8,128)}, ...) custom-call(s32[6]{0:T(128)} %stack.34.s_ref, ...), custom_call_target="tpu_custom_call" | custom-call | flops 3072000000 | bytes 20480000 | tf_op jit(solution)/shard_map/mixer_forward/pallas_call | solution.py:335
  47.7 2.4 %collective-permute-done.13.oth = bf16[1024,384]{1,0:T(8,128)(2,1)S(1)} collective-permute-done((bf16[1024,384]{1,0:T(8,128)(2,1)}, bf16[1024,384]{1,0:T(8,128)(2,1)S(1)}, u32[]{:S(2)}, u32[]{:S(2)}) %collective-permute-start.13) | collective-permute-done | bytes 786464 | tf_op jit(solution)/shard_map/ppermute | solution.py:939
  50.2 29.1 %dense.1 = (bf16[2048,384]{1,0:T(8,128)(2,1)}, bf16[1024,384]{1,0:T(8,128)(2,1)S(1)}, bf16[768,1024]{1,0:T(8,128)(2,1)S(1)}, bf16[2,1280,384]{2,1,0:T(8,128)(2,1...) custom-call(s32[6]{0:T(128)S(1)} %copy-done.7, bf16[768,1024]{1,0:T(8,128)(2,1)} %get-tuple-element.119.middle, ...), custom_call_target="tpu_custom_call" | custom-call | flops 16384000000 | bytes 10240000 | tf_op jit(solution)/shard_map/dense/pallas_call | solution.py:554
  80.6 3.0 %collective-permute-done.18.refs_4_.refs_5_.refs_6_.refs_7_ = bf16[2,1280,384]{2,1,0:T(8,128)(2,1)S(1)} collective-permute-done((bf16[2,1280,384]{2,1,0:T(8,128)(2,1)}, bf16[2,1280,384]{2,1,0:T(8,128)(2,1)S(1)}, u32[]{:S(2)}, u32[]{:S(2)}) %collective-permute-start.18) | collective-permute-done | bytes 1966112 | tf_op jit(solution)/shard_map/ppermute | solution.py:943
  86.2 1.8 collective-permute-start.19
  89.9 17.9 %mixer_backward.1 = (f32[2048,384]{1,0:T(8,128)}, bf16[1024,384]{1,0:T(8,128)(2,1)S(1)}, bf16[2,768,384]{2,1,0:T(8,128)(2,1)S(1)}, bf16[2,768,384]{2,1,0:T(8,128)(2,1)S(1)}) custom-call(s32[6]{0:T(128)S(1)} %copy-done.7, bf16[768,1024]{1,0:T(8,128)(2,1)S(1)} %get-tuple-element.131.grad_middle, bf16[2,768,1024]{2,1,0:T(8,128)(2,1)S(1)} %copy-done.13, ...), custom_call_target="tpu_custom_call" | custom-call | flops 12288000000 | bytes 20480000 | tf_op jit(solution)/shard_map/mixer_backward/pallas_call | solution.py:771
  107.8 3.7 %collective-permute-done.20.c = bf16[640,384]{1,0:T(8,128)(2,1)S(1)} collective-permute-done((bf16[640,384]{1,0:T(8,128)(2,1)S(1)}, bf16[640,384]{1,0:T(8,128)(2,1)S(1)}, u32[]{:S(2)}, u32[]{:S(2)}) %collective-permute-start.20) | collective-permute-done | bytes 491552 | tf_op jit(solution)/shard_map/ppermute | solution.py:939
  112.5 1.9 %collective-permute-done.22.refs_4_.refs_5_.refs_6_.refs_7_ = bf16[2,768,384]{2,1,0:T(8,128)(2,1)S(1)} collective-permute-done((bf16[2,768,384]{2,1,0:T(8,128)(2,1)S(1)}, bf16[2,768,384]{2,1,0:T(8,128)(2,1)S(1)}, u32[]{:S(2)}, u32[]{:S(2)}) %collective-permute-start.22) | collective-permute-done | bytes 1179680 | tf_op jit(solution)/shard_map/ppermute | solution.py:943
  118.8 1.6 collective-permute-start.29
  120.3 2.6 %collective-permute-start.30 = (bf16[160,384]{1,0:T(8,128)(2,1)S(1)}, bf16[160,384]{1,0:T(8,128)(2,1)S(1)}, u32[]{:S(2)}, u32[]{:S(2)}) collective-permute-start(bf16[160,384]{1,0:T(8,128)(2,1)S(1)} %get-tuple-element.174), channel_id=1, source_target_pairs={{0,16},{2,18},{4,20},{6,22},{8,24},{10,26},{12,28},{14,30},{16,0},... | collective-permute-start | bytes 368648 | tf_op jit(solution)/shard_map/ppermute | solution.py:954
  122.9 2.2 %collective-permute-done.23.b = bf16[384,384]{1,0:T(8,128)(2,1)S(1)} collective-permute-done((bf16[384,384]{1,0:T(8,128)(2,1)S(1)}, bf16[384,384]{1,0:T(8,128)(2,1)S(1)}, u32[]{:S(2)}, u32[]{:S(2)}) %collective-permute-start.23) | collective-permute-done | bytes 294944 | tf_op jit(solution)/shard_map/ppermute | solution.py:943
  125.1 3.6 %collective-permute-start.31 = (bf16[160,384]{1,0:T(8,128)(2,1)S(1)}, bf16[160,384]{1,0:T(8,128)(2,1)S(1)}, u32[]{:S(2)}, u32[]{:S(2)}) collective-permute-start(bf16[160,384]{1,0:T(8,128)(2,1)S(1)} %get-tuple-element.175), channel_id=1, source_target_pairs={{0,24},{2,26},{4,28},{6,30},{8,16},{10,18},{12,20},{14,22},{16,8},... | collective-permute-start | bytes 368648 | tf_op jit(solution)/shard_map/ppermute | solution.py:954
  130.0 1.6 collective-permute-done.25.d
  133.4 3.7 %collective-permute-start.34 = (bf16[160,384]{1,0:T(8,128)(2,1)S(1)}, bf16[160,384]{1,0:T(8,128)(2,1)S(1)}, u32[]{:S(2)}, u32[]{:S(2)}) collective-permute-start(bf16[160,384]{1,0:T(8,128)(2,1)S(1)} %add_convert_fusion), channel_id=1, source_target_pairs={{0,24},{2,26},{4,28},{6,30},{8,16},{10,18},{12,20},{14,22},{16,8},... | collective-permute-start | bytes 368648 | tf_op jit(solution)/shard_map/ppermute | solution.py:954
  139.1 2.0 %collective-permute-done.34 = bf16[160,384]{1,0:T(8,128)(2,1)S(1)} collective-permute-done((bf16[160,384]{1,0:T(8,128)(2,1)S(1)}, bf16[160,384]{1,0:T(8,128)(2,1)S(1)}, u32[]{:S(2)}, u32[]{:S(2)}) %collective-permute-start.34) | collective-permute-done | bytes 122912 | tf_op jit(solution)/shard_map/ppermute | solution.py:954
  141.1 6.1 %collective-permute-start.27 = (bf16[96,384]{1,0:T(8,128)(2,1)S(1)}, bf16[96,384]{1,0:T(8,128)(2,1)S(1)}, u32[]{:S(2)}, u32[]{:S(2)}) collective-permute-start(bf16[96,384]{1,0:T(8,128)(2,1)S(1)} %get-tuple-element.170), channel_id=1, source_target_pairs={{0,16},{2,18},{4,20},{6,22},{8,24},{10,26},{12,28},{14,30},{16,0},... | collective-permute-start | bytes 221192 | tf_op jit(solution)/shard_map/ppermute | solution.py:954
  148.1 3.8 %collective-permute-start.28 = (bf16[96,384]{1,0:T(8,128)(2,1)S(1)}, bf16[96,384]{1,0:T(8,128)(2,1)S(1)}, u32[]{:S(2)}, u32[]{:S(2)}) collective-permute-start(bf16[96,384]{1,0:T(8,128)(2,1)S(1)} %get-tuple-element.171), channel_id=1, source_target_pairs={{0,24},{2,26},{4,28},{6,30},{8,16},{10,18},{12,20},{14,22},{16,8},... | collective-permute-start | bytes 221192 | tf_op jit(solution)/shard_map/ppermute | solution.py:954
  155.7 3.7 %collective-permute-start.38 = (bf16[96,384]{1,0:T(8,128)(2,1)S(1)}, bf16[96,384]{1,0:T(8,128)(2,1)S(1)}, u32[]{:S(2)}, u32[]{:S(2)}) collective-permute-start(bf16[96,384]{1,0:T(8,128)(2,1)S(1)} %add_convert_fusion.1), channel_id=1, source_target_pairs={{0,24},{2,26},{4,28},{6,30},{8,16},{10,18},{12,20},{14,22},{16,8},... | collective-permute-start | bytes 221192 | tf_op jit(solution)/shard_map/ppermute | solution.py:954
  160.1 3.6 %collective-permute-done.36 = bf16[96,384]{1,0:T(8,128)(2,1)S(1)} collective-permute-done((bf16[96,384]{1,0:T(8,128)(2,1)S(1)}, bf16[96,384]{1,0:T(8,128)(2,1)S(1)}, u32[]{:S(2)}, u32[]{:S(2)}) %collective-permute-start.36) | collective-permute-done | bytes 73760 | tf_op jit(solution)/shard_map/ppermute | solution.py:954
  166.4 1.7 collective-permute-done.43
  168.3 2.8 %dense_unpack.1 = (f32[384]{0:T(512)}, f32[2,192,192]{2,1,0:T(8,128)}, f32[2,192,1536]{2,1,0:T(8,128)}, f32[2,192,768]{2,1,0:T(8,128)}) custom-call(s32[6]{0:T(128)S(1)} %copy-done.7, bf16[640,384]{1,0:T(8,128)(2,1)S(1)} %pad_maximum_fusion.p0, bf16[640,384]{1,0:T(8,128)(2,1)S(1)} %collective-permute-done.40.p1, ...), custom_call_target="tpu_custom_call" | custom-call | bytes 1048576 | tf_op jit(solution)/shard_map/dense_unpack/pallas_call | solution.py:844
  171.1 3.1 %collective-permute-done.39.p1 = bf16[384,384]{1,0:T(8,128)(2,1)S(1)} collective-permute-done((bf16[384,384]{1,0:T(8,128)(2,1)S(1)}, bf16[384,384]{1,0:T(8,128)(2,1)S(1)}, u32[]{:S(2)}, u32[]{:S(2)}) %collective-permute-start.39) | collective-permute-done | bytes 294944 | tf_op jit(solution)/shard_map/ppermute | solution.py:943
  175.8 2.3 %mixer_unpack.1 = (f32[384]{0:T(512)}, f32[384]{0:T(512)}, f32[384]{0:T(512)}, f32[384]{0:T(512)}, f32[128,384]{1,0:T(8,128)}, /*index=5*/f32[2,192,192]{2,1,0:T...) custom-call(s32[6]{0:T(128)S(1)} %copy-done.7, ...), custom_call_target="tpu_custom_call" | custom-call | bytes 1048576 | tf_op jit(solution)/shard_map/mixer_unpack/pallas_call | solution.py:844
  (162 shorter events, 37.0 us)
Async XLA Ops:
  4.1 7.6 %collective-permute-start.1 = (bf16[176,384]{1,0:T(8,128)(2,1)}, bf16[176,384]{1,0:T(8,128)(2,1)S(1)}, u32[]{:S(2)}, u32[]{:S(2)}) collective-permute-start(bf16[176,384]{1,0:T(8,128)(2,1)} %get-tuple-element.111.mine), channel_id=1, source_target_pairs={{0,1},{1,0},{2,3},{3,2},{4,5},{5,4},{6,7},{7,6},{8,9},{9,8},{10,11... | collective-permute-start | bytes 405512 | tf_op jit(solution)/shard_map/ppermute | solution.py:939
  7.1 11.7 %collective-permute-start.9 = (bf16[336,384]{1,0:T(8,128)(2,1)}, bf16[336,384]{1,0:T(8,128)(2,1)S(1)}, u32[]{:S(2)}, u32[]{:S(2)}) collective-permute-start(bf16[336,384]{1,0:T(8,128)(2,1)} %get-tuple-element.113), channel_id=1, source_target_pairs={{0,1},{1,0},{2,3},{3,2},{4,5},{5,4},{6,7},{7,6},{8,9},{9,8},{10,11... | collective-permute-start | bytes 774152 | tf_op jit(solution)/shard_map/ppermute | solution.py:939
  13.9 20.7 %collective-permute-start = (bf16[1024,384]{1,0:T(8,128)(2,1)S(1)}, bf16[1024,384]{1,0:T(8,128)(2,1)}, u32[]{:S(2)}, u32[]{:S(2)}) collective-permute-start(bf16[1024,384]{1,0:T(8,128)(2,1)S(1)} %constant_dynamic-slice_fusion.1), channel_id=1, source_target_pairs={{0,1},{1,0},{2,3},{3,2},{4,5},{5,4},{6,7},{7,6},{8,9},{9,8},{10,11... | collective-permute-start | bytes 2359304 | tf_op jit(solution)/shard_map/ppermute | solution.py:939
  17.0 7.1 %collective-permute-start.7 = (bf16[176,384]{1,0:T(8,128)(2,1)S(1)}, bf16[176,384]{1,0:T(8,128)(2,1)S(1)}, u32[]{:S(2)}, u32[]{:S(2)}) collective-permute-start(bf16[176,384]{1,0:T(8,128)(2,1)S(1)} %collective-permute-done.5.refs_4_), channel_id=1, source_target_pairs={{0,4},{2,6},{4,0},{6,2},{8,12},{10,14},{12,8},{14,10},{16,20},{18,... | collective-permute-start | bytes 405512 | tf_op jit(solution)/shard_map/ppermute | solution.py:943
  18.7 6.1 %collective-permute-start.6 = (bf16[176,384]{1,0:T(8,128)(2,1)S(1)}, bf16[176,384]{1,0:T(8,128)(2,1)S(1)}, u32[]{:S(2)}, u32[]{:S(2)}) collective-permute-start(bf16[176,384]{1,0:T(8,128)(2,1)S(1)} %collective-permute-done.5.refs_4_), channel_id=1, source_target_pairs={{0,2},{2,0},{4,6},{6,4},{8,10},{10,8},{12,14},{14,12},{16,18},{18,... | collective-permute-start | bytes 405512 | tf_op jit(solution)/shard_map/ppermute | solution.py:943
  20.9 29.1 %collective-permute-start.13 = (bf16[1024,384]{1,0:T(8,128)(2,1)}, bf16[1024,384]{1,0:T(8,128)(2,1)S(1)}, u32[]{:S(2)}, u32[]{:S(2)}) collective-permute-start(bf16[1024,384]{1,0:T(8,128)(2,1)} %constant_dynamic-slice_fusion), channel_id=1, source_target_pairs={{0,1},{1,0},{2,3},{3,2},{4,5},{5,4},{6,7},{7,6},{8,9},{9,8},{10,11... | collective-permute-start | bytes 2359304 | tf_op jit(solution)/shard_map/ppermute | solution.py:939
  22.5 9.6 %collective-permute-start.11 = (bf16[336,384]{1,0:T(8,128)(2,1)S(1)}, bf16[336,384]{1,0:T(8,128)(2,1)S(1)}, u32[]{:S(2)}, u32[]{:S(2)}) collective-permute-start(bf16[336,384]{1,0:T(8,128)(2,1)S(1)} %collective-permute-done.9.p0), channel_id=1, source_target_pairs={{0,8},{2,10},{4,12},{6,14},{8,0},{10,2},{12,4},{14,6},{16,24},{18,... | collective-permute-start | bytes 774152 | tf_op jit(solution)/shard_map/ppermute | solution.py:943
  24.1 8.1 %collective-permute-start.10 = (bf16[336,384]{1,0:T(8,128)(2,1)S(1)}, bf16[336,384]{1,0:T(8,128)(2,1)S(1)}, u32[]{:S(2)}, u32[]{:S(2)}) collective-permute-start(bf16[336,384]{1,0:T(8,128)(2,1)S(1)} %collective-permute-done.9.p0), channel_id=1, source_target_pairs={{0,4},{2,6},{4,0},{6,2},{8,12},{10,14},{12,8},{14,10},{16,20},{18,... | collective-permute-start | bytes 774152 | tf_op jit(solution)/shard_map/ppermute | solution.py:943
  32.2 17.9 %collective-permute-start.16 = (bf16[336,384]{1,0:T(8,128)(2,1)S(1)}, bf16[336,384]{1,0:T(8,128)(2,1)}, u32[]{:S(2)}, u32[]{:S(2)}) collective-permute-start(bf16[336,384]{1,0:T(8,128)(2,1)S(1)} %collective-permute-done.11.p4), channel_id=1, source_target_pairs={{0,2},{2,0},{4,6},{6,4},{8,10},{10,8},{12,14},{14,12},{16,18},{18,... | collective-permute-start | bytes 774152 | tf_op jit(solution)/shard_map/ppermute | solution.py:943
  32.4 14.8 %collective-permute-start.12 = (bf16[336,384]{1,0:T(8,128)(2,1)S(1)}, bf16[336,384]{1,0:T(8,128)(2,1)}, u32[]{:S(2)}, u32[]{:S(2)}) collective-permute-start(bf16[336,384]{1,0:T(8,128)(2,1)S(1)} %collective-permute-done.11.p4), channel_id=1, source_target_pairs={{0,4},{2,6},{4,0},{6,2},{8,12},{10,14},{12,8},{14,10},{16,20},{18,... | collective-permute-start | bytes 774152 | tf_op jit(solution)/shard_map/ppermute | solution.py:943
  33.6 16.5 %collective-permute-start.14 = (bf16[336,384]{1,0:T(8,128)(2,1)S(1)}, bf16[336,384]{1,0:T(8,128)(2,1)}, u32[]{:S(2)}, u32[]{:S(2)}) collective-permute-start(bf16[336,384]{1,0:T(8,128)(2,1)S(1)} %collective-permute-done.9.p0), channel_id=1, source_target_pairs={{0,2},{2,0},{4,6},{6,4},{8,10},{10,8},{12,14},{14,12},{16,18},{18,... | collective-permute-start | bytes 774152 | tf_op jit(solution)/shard_map/ppermute | solution.py:943
  34.5 15.6 %collective-permute-start.15 = (bf16[336,384]{1,0:T(8,128)(2,1)S(1)}, bf16[336,384]{1,0:T(8,128)(2,1)}, u32[]{:S(2)}, u32[]{:S(2)}) collective-permute-start(bf16[336,384]{1,0:T(8,128)(2,1)S(1)} %collective-permute-done.10.p2), channel_id=1, source_target_pairs={{0,2},{2,0},{4,6},{6,4},{8,10},{10,8},{12,14},{14,12},{16,18},{18,... | collective-permute-start | bytes 774152 | tf_op jit(solution)/shard_map/ppermute | solution.py:943
  86.2 21.6 %collective-permute-start.19 = (bf16[640,384]{1,0:T(8,128)(2,1)S(1)}, bf16[640,384]{1,0:T(8,128)(2,1)S(1)}, u32[]{:S(2)}, u32[]{:S(2)}) collective-permute-start(bf16[640,384]{1,0:T(8,128)(2,1)S(1)} %get-tuple-element.144), channel_id=1, source_target_pairs={{0,4},{2,6},{4,0},{6,2},{8,12},{10,14},{12,8},{14,10},{16,20},{18,... | collective-permute-start | bytes 1474568 | tf_op jit(solution)/shard_map/ppermute | solution.py:943
  88.0 23.5 %collective-permute-start.20 = (bf16[640,384]{1,0:T(8,128)(2,1)S(1)}, bf16[640,384]{1,0:T(8,128)(2,1)S(1)}, u32[]{:S(2)}, u32[]{:S(2)}) collective-permute-start(bf16[640,384]{1,0:T(8,128)(2,1)S(1)} %get-tuple-element.145), channel_id=1, source_target_pairs={{0,1},{1,0},{2,3},{3,2},{4,5},{5,4},{6,7},{7,6},{8,9},{9,8},{10,11... | collective-permute-start | bytes 1474568 | tf_op jit(solution)/shard_map/ppermute | solution.py:939
  89.5 22.0 %collective-permute-start.21 = (bf16[640,384]{1,0:T(8,128)(2,1)S(1)}, bf16[640,384]{1,0:T(8,128)(2,1)S(1)}, u32[]{:S(2)}, u32[]{:S(2)}) collective-permute-start(bf16[640,384]{1,0:T(8,128)(2,1)S(1)} %get-tuple-element.146), channel_id=1, source_target_pairs={{0,5},{1,4},{2,7},{3,6},{4,1},{5,0},{6,3},{7,2},{8,13},{9,12},{10,... | collective-permute-start | bytes 1474568 | tf_op jit(solution)/shard_map/ppermute | solution.py:948
  115.2 9.9 %collective-permute-start.23 = (bf16[384,384]{1,0:T(8,128)(2,1)S(1)}, bf16[384,384]{1,0:T(8,128)(2,1)S(1)}, u32[]{:S(2)}, u32[]{:S(2)}) collective-permute-start(bf16[384,384]{1,0:T(8,128)(2,1)S(1)} %get-tuple-element.159), channel_id=1, source_target_pairs={{0,4},{2,6},{4,0},{6,2},{8,12},{10,14},{12,8},{14,10},{16,20},{18,... | collective-permute-start | bytes 884744 | tf_op jit(solution)/shard_map/ppermute | solution.py:943
  116.5 13.5 %collective-permute-start.24 = (bf16[384,384]{1,0:T(8,128)(2,1)S(1)}, bf16[384,384]{1,0:T(8,128)(2,1)S(1)}, u32[]{:S(2)}, u32[]{:S(2)}) collective-permute-start(bf16[384,384]{1,0:T(8,128)(2,1)S(1)} %get-tuple-element.160), channel_id=1, source_target_pairs={{0,1},{1,0},{2,3},{3,2},{4,5},{5,4},{6,7},{7,6},{8,9},{9,8},{10,11... | collective-permute-start | bytes 884744 | tf_op jit(solution)/shard_map/ppermute | solution.py:939
  117.3 14.3 %collective-permute-start.25 = (bf16[384,384]{1,0:T(8,128)(2,1)S(1)}, bf16[384,384]{1,0:T(8,128)(2,1)S(1)}, u32[]{:S(2)}, u32[]{:S(2)}) collective-permute-start(bf16[384,384]{1,0:T(8,128)(2,1)S(1)} %get-tuple-element.161), channel_id=1, source_target_pairs={{0,5},{1,4},{2,7},{3,6},{4,1},{5,0},{6,3},{7,2},{8,13},{9,12},{10,... | collective-permute-start | bytes 884744 | tf_op jit(solution)/shard_map/ppermute | solution.py:948
  118.8 14.5 %collective-permute-start.29 = (bf16[160,384]{1,0:T(8,128)(2,1)S(1)}, bf16[160,384]{1,0:T(8,128)(2,1)S(1)}, u32[]{:S(2)}, u32[]{:S(2)}) collective-permute-start(bf16[160,384]{1,0:T(8,128)(2,1)S(1)} %get-tuple-element.173), channel_id=1, source_target_pairs={{0,8},{2,10},{4,12},{6,14},{8,0},{10,2},{12,4},{14,6},{16,24},{18,... | collective-permute-start | bytes 368648 | tf_op jit(solution)/shard_map/ppermute | solution.py:954
  120.3 13.0 %collective-permute-start.30 = (bf16[160,384]{1,0:T(8,128)(2,1)S(1)}, bf16[160,384]{1,0:T(8,128)(2,1)S(1)}, u32[]{:S(2)}, u32[]{:S(2)}) collective-permute-start(bf16[160,384]{1,0:T(8,128)(2,1)S(1)} %get-tuple-element.174), channel_id=1, source_target_pairs={{0,16},{2,18},{4,20},{6,22},{8,24},{10,26},{12,28},{14,30},{16,0},... | collective-permute-start | bytes 368648 | tf_op jit(solution)/shard_map/ppermute | solution.py:954
  125.1 8.2 %collective-permute-start.31 = (bf16[160,384]{1,0:T(8,128)(2,1)S(1)}, bf16[160,384]{1,0:T(8,128)(2,1)S(1)}, u32[]{:S(2)}, u32[]{:S(2)}) collective-permute-start(bf16[160,384]{1,0:T(8,128)(2,1)S(1)} %get-tuple-element.175), channel_id=1, source_target_pairs={{0,24},{2,26},{4,28},{6,30},{8,16},{10,18},{12,20},{14,22},{16,8},... | collective-permute-start | bytes 368648 | tf_op jit(solution)/shard_map/ppermute | solution.py:954
  132.4 22.1 %collective-permute-start.35 = (bf16[1024,384]{1,0:T(8,128)(2,1)S(1)}, bf16[1024,384]{1,0:T(8,128)(2,1)S(1)}, u32[]{:S(2)}, u32[]{:S(2)}) collective-permute-start(bf16[1024,384]{1,0:T(8,128)(2,1)S(1)} %get-tuple-element.176), channel_id=1, source_target_pairs={{0,1},{1,0},{2,3},{3,2},{4,5},{5,4},{6,7},{7,6},{8,9},{9,8},{10,11... | collective-permute-start | bytes 2359304 | tf_op jit(solution)/shard_map/ppermute | solution.py:939
  133.4 7.7 %collective-permute-start.34 = (bf16[160,384]{1,0:T(8,128)(2,1)S(1)}, bf16[160,384]{1,0:T(8,128)(2,1)S(1)}, u32[]{:S(2)}, u32[]{:S(2)}) collective-permute-start(bf16[160,384]{1,0:T(8,128)(2,1)S(1)} %add_convert_fusion), channel_id=1, source_target_pairs={{0,24},{2,26},{4,28},{6,30},{8,16},{10,18},{12,20},{14,22},{16,8},... | collective-permute-start | bytes 368648 | tf_op jit(solution)/shard_map/ppermute | solution.py:954
  137.1 11.1 %collective-permute-start.33 = (bf16[160,384]{1,0:T(8,128)(2,1)S(1)}, bf16[160,384]{1,0:T(8,128)(2,1)S(1)}, u32[]{:S(2)}, u32[]{:S(2)}) collective-permute-start(bf16[160,384]{1,0:T(8,128)(2,1)S(1)} %add_convert_fusion), channel_id=1, source_target_pairs={{0,16},{2,18},{4,20},{6,22},{8,24},{10,26},{12,28},{14,30},{16,0},... | collective-permute-start | bytes 368648 | tf_op jit(solution)/shard_map/ppermute | solution.py:954
  137.1 14.9 %collective-permute-start.32 = (bf16[160,384]{1,0:T(8,128)(2,1)S(1)}, bf16[160,384]{1,0:T(8,128)(2,1)S(1)}, u32[]{:S(2)}, u32[]{:S(2)}) collective-permute-start(bf16[160,384]{1,0:T(8,128)(2,1)S(1)} %add_convert_fusion), channel_id=1, source_target_pairs={{0,8},{2,10},{4,12},{6,14},{8,0},{10,2},{12,4},{14,6},{16,24},{18,... | collective-permute-start | bytes 368648 | tf_op jit(solution)/shard_map/ppermute | solution.py:954
  137.8 15.7 %collective-permute-start.26 = (bf16[96,384]{1,0:T(8,128)(2,1)S(1)}, bf16[96,384]{1,0:T(8,128)(2,1)S(1)}, u32[]{:S(2)}, u32[]{:S(2)}) collective-permute-start(bf16[96,384]{1,0:T(8,128)(2,1)S(1)} %get-tuple-element.169), channel_id=1, source_target_pairs={{0,8},{2,10},{4,12},{6,14},{8,0},{10,2},{12,4},{14,6},{16,24},{18,... | collective-permute-start | bytes 221192 | tf_op jit(solution)/shard_map/ppermute | solution.py:954
  141.1 12.5 %collective-permute-start.27 = (bf16[96,384]{1,0:T(8,128)(2,1)S(1)}, bf16[96,384]{1,0:T(8,128)(2,1)S(1)}, u32[]{:S(2)}, u32[]{:S(2)}) collective-permute-start(bf16[96,384]{1,0:T(8,128)(2,1)S(1)} %get-tuple-element.170), channel_id=1, source_target_pairs={{0,16},{2,18},{4,20},{6,22},{8,24},{10,26},{12,28},{14,30},{16,0},... | collective-permute-start | bytes 221192 | tf_op jit(solution)/shard_map/ppermute | solution.py:954
  148.1 6.3 %collective-permute-start.28 = (bf16[96,384]{1,0:T(8,128)(2,1)S(1)}, bf16[96,384]{1,0:T(8,128)(2,1)S(1)}, u32[]{:S(2)}, u32[]{:S(2)}) collective-permute-start(bf16[96,384]{1,0:T(8,128)(2,1)S(1)} %get-tuple-element.171), channel_id=1, source_target_pairs={{0,24},{2,26},{4,28},{6,30},{8,16},{10,18},{12,20},{14,22},{16,8},... | collective-permute-start | bytes 221192 | tf_op jit(solution)/shard_map/ppermute | solution.py:954
  152.0 16.0 %collective-permute-start.43 = (bf16[1024,384]{1,0:T(8,128)(2,1)S(1)}, bf16[1024,384]{1,0:T(8,128)(2,1)S(1)}, u32[]{:S(2)}, u32[]{:S(2)}) collective-permute-start(bf16[1024,384]{1,0:T(8,128)(2,1)S(1)} %get-tuple-element.186), channel_id=1, source_target_pairs={{0,1},{1,0},{2,3},{3,2},{4,5},{5,4},{6,7},{7,6},{8,9},{9,8},{10,11... | collective-permute-start | bytes 2359304 | tf_op jit(solution)/shard_map/ppermute | solution.py:939
  154.5 10.2 %collective-permute-start.40 = (bf16[640,384]{1,0:T(8,128)(2,1)S(1)}, bf16[640,384]{1,0:T(8,128)(2,1)S(1)}, u32[]{:S(2)}, u32[]{:S(2)}) collective-permute-start(bf16[640,384]{1,0:T(8,128)(2,1)S(1)} %pad_maximum_fusion.p0), channel_id=1, source_target_pairs={{0,4},{2,6},{4,0},{6,2},{8,12},{10,14},{12,8},{14,10},{16,20},{18,... | collective-permute-start | bytes 1474568 | tf_op jit(solution)/shard_map/ppermute | solution.py:943
  155.7 9.0 %collective-permute-start.38 = (bf16[96,384]{1,0:T(8,128)(2,1)S(1)}, bf16[96,384]{1,0:T(8,128)(2,1)S(1)}, u32[]{:S(2)}, u32[]{:S(2)}) collective-permute-start(bf16[96,384]{1,0:T(8,128)(2,1)S(1)} %add_convert_fusion.1), channel_id=1, source_target_pairs={{0,24},{2,26},{4,28},{6,30},{8,16},{10,18},{12,20},{14,22},{16,8},... | collective-permute-start | bytes 221192 | tf_op jit(solution)/shard_map/ppermute | solution.py:954
  164.8 9.5 %collective-permute-start.39 = (bf16[384,384]{1,0:T(8,128)(2,1)S(1)}, bf16[384,384]{1,0:T(8,128)(2,1)S(1)}, u32[]{:S(2)}, u32[]{:S(2)}) collective-permute-start(bf16[384,384]{1,0:T(8,128)(2,1)S(1)} %constant_dynamic-update-slice_fusion.p0), channel_id=1, source_target_pairs={{0,4},{2,6},{4,0},{6,2},{8,12},{10,14},{12,8},{14,10},{16,20},{18,... | collective-permute-start | bytes 884744 | tf_op jit(solution)/shard_map/ppermute | solution.py:943
  (48 other events, 374.7 us)

commit v3 on v2

--- a/solution.py
+++ b/solution.py
@@ -426,6 +426,7 @@
         for acc in (gur, gdl, gul, gdr, ggain):
             acc[...] = jnp.zeros(acc.shape, f32)
 
+    place_halves(top, side, own[...].T, oth[...].T)
     gain = column(cols, 2)
     normed, scale_row = norm_stats(middle[...].astype(f32))
     half[...] = (normed * gain).astype(bf16)
@@ -438,16 +439,16 @@
         chance = 0.5 + 0.5 * lax.erf(gate * 0.7071067811865476)
         density = jnp.exp(gate * gate * -0.5 - 0.9189385332046727)
         active = gate * chance
-        hid[rows, :] = (active * up).astype(bf16)
-        act[rows, :] = active.astype(bf16)
-        slope[rows, :] = (up * (chance + gate * density)).astype(bf16)
+        active, up = active.astype(bf16), up.astype(bf16)
+        hid[rows, :] = active * up
+        act[rows, :] = active
+        slope[rows, :] = up * (chance + gate * density).astype(bf16)
         regroup(moved4, g, nn(wdl[g], hid[rows, :]).astype(bf16))
     for g in range(NB):
         rows = slice(g * BS, (g + 1) * BS)
         outs[rows, :] = (middle[rows, :].astype(f32) + tn(wdr[g], block(moved4, g))).astype(bf16)
     out_own[...] = outs[rows_of(side, HALF), :].T
     out_send[...] = outs[rows_of(1 - side, HALF), :].T
-    place_halves(top, side, own[...].T, oth[...].T)
     for g in range(NB):
         grad = block(top, g)
         regroup(back, g, nn(wdr[g], grad).astype(bf16))

time: 179 us -> 178 us (level)
  no operation moved by 1% of the time
where the time goes in v3:
time: 178 us
  Pallas kernels  74.8 us (42%)
  starting transfers between devices  56.4 us (32%)
  waiting for transfers between devices  37.7 us (21%)
  local copies, waits for them, and re-layouts  7.41 us (4%)
    pallas_call x1, Pallas kernels, dense(): pl.pallas_call(functools.partial(dense_kernel, steps=steps), out_shape=tu...  29 us
    ppermute x12, starting transfers between devices, shift_wide(): return lax.ppermute(values, 'wide', [(i, i ^ flip) for i in range(size)])  27.8 us
    pallas_call x1, Pallas kernels, mixer_backward(): pl.pallas_call(functools.partial(mixer_backward_kernel, steps=steps, shar...  17.9 us
    ppermute x24, starting transfers between devices, swap_wide(): lax.ppermute(values, 'wide', [(i, i ^ 1 << bit) for i in range(size)])  15.9 us
    ppermute x8, waiting for transfers between devices, swap_narrow(): return lax.ppermute(values, 'narrow', [(0, 1), (1, 0)])  14.4 us
    ppermute x24, waiting for transfers between devices, swap_wide(): lax.ppermute(values, 'wide', [(i, i ^ 1 << bit) for i in range(size)])  13.4 us
    pallas_call x1, Pallas kernels, mixer_forward(): pl.pallas_call(mixer_forward_kernel, out_shape=tuple(outs), grid_spec=plt...  12.5 us
    ppermute x8, starting transfers between devices, swap_narrow(): return lax.ppermute(values, 'narrow', [(0, 1), (1, 0)])  11 us
  transfers between devices with their start and end apart: 46, of which 19 were waited for; matrix products, arithmetic and copies ran while one was open for 3% of the time, Pallas kernels for 22%

profile of v3, /device:TPU:0, one launch (start us, length us, event | category | flops | bytes accessed | tf_op | source)
XLA Modules:
  0.0 178.0 jit_solution(938644453069990550)
XLA Ops:
  1.3 2.7 %pack_weights.1 = (bf16[176,384]{1,0:T(8,128)(2,1)}, bf16[336,384]{1,0:T(8,128)(2,1)}) custom-call(s32[6]{0:T(128)} %stack.34.s_ref, bf16[2,192,192]{2,1,0:T(8,128)(2,1)} %il.3, bf16[2,192,576]{2,1,0:T(8,128)(2,1)} %ir.3, bf16[2,192,192]{2,1,0:T(8,128)(2,1)} %ol.3, bf16[2,192,192]{2,1,0:T(8,128)(2,1)} %orr.3, bf16[2,192,192]{2,1,0:T(8,128)(2,1)} %ul.3, ...), custom_call_target="tpu_custom_call" | custom-call | bytes 1048576 | tf_op jit(solution)/shard_map/pack_weights/pallas_call | solution.py:160
  4.1 3.0 %collective-permute-start.1 = (bf16[176,384]{1,0:T(8,128)(2,1)}, bf16[176,384]{1,0:T(8,128)(2,1)S(1)}, u32[]{:S(2)}, u32[]{:S(2)}) collective-permute-start(bf16[176,384]{1,0:T(8,128)(2,1)} %get-tuple-element.111.mine), channel_id=1, source_target_pairs={{0,1},{1,0},{2,3},{3,2},{4,5},{5,4},{6,7},{7,6},{8,9},{9,8},{10,11... | collective-permute-start | bytes 405512 | tf_op jit(solution)/shard_map/ppermute | solution.py:940
  7.1 4.5 %collective-permute-done.1.refs_0_ = bf16[176,384]{1,0:T(8,128)(2,1)S(1)} collective-permute-done((bf16[176,384]{1,0:T(8,128)(2,1)}, bf16[176,384]{1,0:T(8,128)(2,1)S(1)}, u32[]{:S(2)}, u32[]{:S(2)}) %collective-permute-start.1) | collective-permute-done | bytes 135200 | tf_op jit(solution)/shard_map/ppermute | solution.py:940
  11.7 2.1 %collective-permute-start.5 = (bf16[176,384]{1,0:T(8,128)(2,1)S(1)}, bf16[176,384]{1,0:T(8,128)(2,1)S(1)}, u32[]{:S(2)}, u32[]{:S(2)}) collective-permute-start(bf16[176,384]{1,0:T(8,128)(2,1)S(1)} %collective-permute-done.1.refs_0_), channel_id=1, source_target_pairs={{0,8},{2,10},{4,12},{6,14},{8,0},{10,2},{12,4},{14,6},{16,24},{18,... | collective-permute-start | bytes 405512 | tf_op jit(solution)/shard_map/ppermute | solution.py:944
  13.9 1.6 collective-permute-start
  17.0 1.8 collective-permute-start.7
  18.8 2.1 %constant_dynamic-slice_fusion = bf16[1024,384]{1,0:T(8,128)(2,1)} fusion(bf16[2048,384]{1,0:T(8,128)(2,1)} %own.5, s32[]{:T(128)S(6)} %select_n.10), kind=kLoop, calls=%fused_computation.16 | loop fusion | bytes 1572868 | tf_op jit(solution)/shard_map/dynamic_slice | solution.py:1047
  20.9 1.6 collective-permute-start.13
  28.3 3.8 %filter_spectrum.1 = (f32[768,128]{1,0:T(8,128)}, f32[768,256]{1,0:T(8,128)}, f32[8,128]{1,0:T(8,128)}, f32[768,128]{1,0:T(8,128)}) custom-call(s32[6]{0:T(128)} %stack.34.s_ref, bf16[128,384]{1,0:T(8,128)(2,1)} %own.3, bf16[176,384]{1,0:T(8,128)(2,1)} %get-tuple-element.111.mine, bf16[176,384]{1,0:T(8,128)(2,1)} %copy-done.20, bf16[176,384]{1,0:T(8,128)(2,1)} %copy-done.23, ...), custom_call_target="tpu_custom_call" | custom-call | bytes 1048576 | tf_op jit(solution)/shard_map/filter_spectrum/pallas_call | solution.py:224
  34.6 12.5 %mixer_forward.1 = (bf16[768,1024]{1,0:T(8,128)(2,1)}, bf16[2,768,1024]{2,1,0:T(8,128)(2,1)}, bf16[5,768,1024]{2,1,0:T(8,128)(2,1)}, f32[8,1024]{1,0:T(8,128)}, ...) custom-call(s32[6]{0:T(128)} %stack.34.s_ref, ...), custom_call_target="tpu_custom_call" | custom-call | flops 3072000000 | bytes 20480000 | tf_op jit(solution)/shard_map/mixer_forward/pallas_call | solution.py:335
  47.7 2.4 %collective-permute-done.13.oth = bf16[1024,384]{1,0:T(8,128)(2,1)S(1)} collective-permute-done((bf16[1024,384]{1,0:T(8,128)(2,1)}, bf16[1024,384]{1,0:T(8,128)(2,1)S(1)}, u32[]{:S(2)}, u32[]{:S(2)}) %collective-permute-start.13) | collective-permute-done | bytes 786464 | tf_op jit(solution)/shard_map/ppermute | solution.py:940
  50.2 29.0 %dense.1 = (bf16[2048,384]{1,0:T(8,128)(2,1)}, bf16[1024,384]{1,0:T(8,128)(2,1)S(1)}, bf16[768,1024]{1,0:T(8,128)(2,1)S(1)}, bf16[2,1280,384]{2,1,0:T(8,128)(2,1...) custom-call(s32[6]{0:T(128)S(1)} %copy-done.7, bf16[768,1024]{1,0:T(8,128)(2,1)} %get-tuple-element.119.middle, ...), custom_call_target="tpu_custom_call" | custom-call | flops 16384000000 | bytes 10240000 | tf_op jit(solution)/shard_map/dense/pallas_call | solution.py:555
  80.4 3.0 %collective-permute-done.18.refs_4_.refs_5_.refs_6_.refs_7_ = bf16[2,1280,384]{2,1,0:T(8,128)(2,1)S(1)} collective-permute-done((bf16[2,1280,384]{2,1,0:T(8,128)(2,1)}, bf16[2,1280,384]{2,1,0:T(8,128)(2,1)S(1)}, u32[]{:S(2)}, u32[]{:S(2)}) %collective-permute-start.18) | collective-permute-done | bytes 1966112 | tf_op jit(solution)/shard_map/ppermute | solution.py:944
  86.1 1.8 collective-permute-start.19
  89.7 17.9 %mixer_backward.1 = (f32[2048,384]{1,0:T(8,128)}, bf16[1024,384]{1,0:T(8,128)(2,1)S(1)}, bf16[2,768,384]{2,1,0:T(8,128)(2,1)S(1)}, bf16[2,768,384]{2,1,0:T(8,128)(2,1)S(1)}) custom-call(s32[6]{0:T(128)S(1)} %copy-done.7, bf16[768,1024]{1,0:T(8,128)(2,1)S(1)} %get-tuple-element.131.grad_middle, bf16[2,768,1024]{2,1,0:T(8,128)(2,1)S(1)} %copy-done.13, ...), custom_call_target="tpu_custom_call" | custom-call | flops 12288000000 | bytes 20480000 | tf_op jit(solution)/shard_map/mixer_backward/pallas_call | solution.py:772
  107.7 3.7 %collective-permute-done.20.c = bf16[640,384]{1,0:T(8,128)(2,1)S(1)} collective-permute-done((bf16[640,384]{1,0:T(8,128)(2,1)S(1)}, bf16[640,384]{1,0:T(8,128)(2,1)S(1)}, u32[]{:S(2)}, u32[]{:S(2)}) %collective-permute-start.20) | collective-permute-done | bytes 491552 | tf_op jit(solution)/shard_map/ppermute | solution.py:940
  112.3 1.9 %collective-permute-done.22.refs_4_.refs_5_.refs_6_.refs_7_ = bf16[2,768,384]{2,1,0:T(8,128)(2,1)S(1)} collective-permute-done((bf16[2,768,384]{2,1,0:T(8,128)(2,1)S(1)}, bf16[2,768,384]{2,1,0:T(8,128)(2,1)S(1)}, u32[]{:S(2)}, u32[]{:S(2)}) %collective-permute-start.22) | collective-permute-done | bytes 1179680 | tf_op jit(solution)/shard_map/ppermute | solution.py:944
  118.6 1.6 collective-permute-start.29
  120.2 2.6 %collective-permute-start.30 = (bf16[160,384]{1,0:T(8,128)(2,1)S(1)}, bf16[160,384]{1,0:T(8,128)(2,1)S(1)}, u32[]{:S(2)}, u32[]{:S(2)}) collective-permute-start(bf16[160,384]{1,0:T(8,128)(2,1)S(1)} %get-tuple-element.174), channel_id=1, source_target_pairs={{0,16},{2,18},{4,20},{6,22},{8,24},{10,26},{12,28},{14,30},{16,0},... | collective-permute-start | bytes 368648 | tf_op jit(solution)/shard_map/ppermute | solution.py:955
  122.8 2.2 %collective-permute-done.23.b = bf16[384,384]{1,0:T(8,128)(2,1)S(1)} collective-permute-done((bf16[384,384]{1,0:T(8,128)(2,1)S(1)}, bf16[384,384]{1,0:T(8,128)(2,1)S(1)}, u32[]{:S(2)}, u32[]{:S(2)}) %collective-permute-start.23) | collective-permute-done | bytes 294944 | tf_op jit(solution)/shard_map/ppermute | solution.py:944
  125.0 3.6 %collective-permute-start.31 = (bf16[160,384]{1,0:T(8,128)(2,1)S(1)}, bf16[160,384]{1,0:T(8,128)(2,1)S(1)}, u32[]{:S(2)}, u32[]{:S(2)}) collective-permute-start(bf16[160,384]{1,0:T(8,128)(2,1)S(1)} %get-tuple-element.175), channel_id=1, source_target_pairs={{0,24},{2,26},{4,28},{6,30},{8,16},{10,18},{12,20},{14,22},{16,8},... | collective-permute-start | bytes 368648 | tf_op jit(solution)/shard_map/ppermute | solution.py:955
  129.8 1.6 collective-permute-done.25.d
  133.2 3.7 %collective-permute-start.34 = (bf16[160,384]{1,0:T(8,128)(2,1)S(1)}, bf16[160,384]{1,0:T(8,128)(2,1)S(1)}, u32[]{:S(2)}, u32[]{:S(2)}) collective-permute-start(bf16[160,384]{1,0:T(8,128)(2,1)S(1)} %add_convert_fusion), channel_id=1, source_target_pairs={{0,24},{2,26},{4,28},{6,30},{8,16},{10,18},{12,20},{14,22},{16,8},... | collective-permute-start | bytes 368648 | tf_op jit(solution)/shard_map/ppermute | solution.py:955
  138.9 2.0 %collective-permute-done.34 = bf16[160,384]{1,0:T(8,128)(2,1)S(1)} collective-permute-done((bf16[160,384]{1,0:T(8,128)(2,1)S(1)}, bf16[160,384]{1,0:T(8,128)(2,1)S(1)}, u32[]{:S(2)}, u32[]{:S(2)}) %collective-permute-start.34) | collective-permute-done | bytes 122912 | tf_op jit(solution)/shard_map/ppermute | solution.py:955
  140.9 6.1 %collective-permute-start.27 = (bf16[96,384]{1,0:T(8,128)(2,1)S(1)}, bf16[96,384]{1,0:T(8,128)(2,1)S(1)}, u32[]{:S(2)}, u32[]{:S(2)}) collective-permute-start(bf16[96,384]{1,0:T(8,128)(2,1)S(1)} %get-tuple-element.170), channel_id=1, source_target_pairs={{0,16},{2,18},{4,20},{6,22},{8,24},{10,26},{12,28},{14,30},{16,0},... | collective-permute-start | bytes 221192 | tf_op jit(solution)/shard_map/ppermute | solution.py:955
  148.0 3.8 %collective-permute-start.28 = (bf16[96,384]{1,0:T(8,128)(2,1)S(1)}, bf16[96,384]{1,0:T(8,128)(2,1)S(1)}, u32[]{:S(2)}, u32[]{:S(2)}) collective-permute-start(bf16[96,384]{1,0:T(8,128)(2,1)S(1)} %get-tuple-element.171), channel_id=1, source_target_pairs={{0,24},{2,26},{4,28},{6,30},{8,16},{10,18},{12,20},{14,22},{16,8},... | collective-permute-start | bytes 221192 | tf_op jit(solution)/shard_map/ppermute | solution.py:955
  155.6 3.7 %collective-permute-start.38 = (bf16[96,384]{1,0:T(8,128)(2,1)S(1)}, bf16[96,384]{1,0:T(8,128)(2,1)S(1)}, u32[]{:S(2)}, u32[]{:S(2)}) collective-permute-start(bf16[96,384]{1,0:T(8,128)(2,1)S(1)} %add_convert_fusion.1), channel_id=1, source_target_pairs={{0,24},{2,26},{4,28},{6,30},{8,16},{10,18},{12,20},{14,22},{16,8},... | collective-permute-start | bytes 221192 | tf_op jit(solution)/shard_map/ppermute | solution.py:955
  160.0 3.6 %collective-permute-done.36 = bf16[96,384]{1,0:T(8,128)(2,1)S(1)} collective-permute-done((bf16[96,384]{1,0:T(8,128)(2,1)S(1)}, bf16[96,384]{1,0:T(8,128)(2,1)S(1)}, u32[]{:S(2)}, u32[]{:S(2)}) %collective-permute-start.36) | collective-permute-done | bytes 73760 | tf_op jit(solution)/shard_map/ppermute | solution.py:955
  166.2 1.7 collective-permute-done.43
  168.1 2.8 %dense_unpack.1 = (f32[384]{0:T(512)}, f32[2,192,192]{2,1,0:T(8,128)}, f32[2,192,1536]{2,1,0:T(8,128)}, f32[2,192,768]{2,1,0:T(8,128)}) custom-call(s32[6]{0:T(128)S(1)} %copy-done.7, bf16[640,384]{1,0:T(8,128)(2,1)S(1)} %pad_maximum_fusion.p0, bf16[640,384]{1,0:T(8,128)(2,1)S(1)} %collective-permute-done.40.p1, ...), custom_call_target="tpu_custom_call" | custom-call | bytes 1048576 | tf_op jit(solution)/shard_map/dense_unpack/pallas_call | solution.py:845
  171.0 3.1 %collective-permute-done.39.p1 = bf16[384,384]{1,0:T(8,128)(2,1)S(1)} collective-permute-done((bf16[384,384]{1,0:T(8,128)(2,1)S(1)}, bf16[384,384]{1,0:T(8,128)(2,1)S(1)}, u32[]{:S(2)}, u32[]{:S(2)}) %collective-permute-start.39) | collective-permute-done | bytes 294944 | tf_op jit(solution)/shard_map/ppermute | solution.py:944
  175.7 2.3 %mixer_unpack.1 = (f32[384]{0:T(512)}, f32[384]{0:T(512)}, f32[384]{0:T(512)}, f32[384]{0:T(512)}, f32[128,384]{1,0:T(8,128)}, /*index=5*/f32[2,192,192]{2,1,0:T...) custom-call(s32[6]{0:T(128)S(1)} %copy-done.7, ...), custom_call_target="tpu_custom_call" | custom-call | bytes 1048576 | tf_op jit(solution)/shard_map/mixer_unpack/pallas_call | solution.py:845
  (162 shorter events, 37.0 us)
Async XLA Ops:
  4.1 7.6 %collective-permute-start.1 = (bf16[176,384]{1,0:T(8,128)(2,1)}, bf16[176,384]{1,0:T(8,128)(2,1)S(1)}, u32[]{:S(2)}, u32[]{:S(2)}) collective-permute-start(bf16[176,384]{1,0:T(8,128)(2,1)} %get-tuple-element.111.mine), channel_id=1, source_target_pairs={{0,1},{1,0},{2,3},{3,2},{4,5},{5,4},{6,7},{7,6},{8,9},{9,8},{10,11... | collective-permute-start | bytes 405512 | tf_op jit(solution)/shard_map/ppermute | solution.py:940
  7.1 11.7 %collective-permute-start.9 = (bf16[336,384]{1,0:T(8,128)(2,1)}, bf16[336,384]{1,0:T(8,128)(2,1)S(1)}, u32[]{:S(2)}, u32[]{:S(2)}) collective-permute-start(bf16[336,384]{1,0:T(8,128)(2,1)} %get-tuple-element.113), channel_id=1, source_target_pairs={{0,1},{1,0},{2,3},{3,2},{4,5},{5,4},{6,7},{7,6},{8,9},{9,8},{10,11... | collective-permute-start | bytes 774152 | tf_op jit(solution)/shard_map/ppermute | solution.py:940
  13.9 20.7 %collective-permute-start = (bf16[1024,384]{1,0:T(8,128)(2,1)S(1)}, bf16[1024,384]{1,0:T(8,128)(2,1)}, u32[]{:S(2)}, u32[]{:S(2)}) collective-permute-start(bf16[1024,384]{1,0:T(8,128)(2,1)S(1)} %constant_dynamic-slice_fusion.1), channel_id=1, source_target_pairs={{0,1},{1,0},{2,3},{3,2},{4,5},{5,4},{6,7},{7,6},{8,9},{9,8},{10,11... | collective-permute-start | bytes 2359304 | tf_op jit(solution)/shard_map/ppermute | solution.py:940
  17.0 7.1 %collective-permute-start.7 = (bf16[176,384]{1,0:T(8,128)(2,1)S(1)}, bf16[176,384]{1,0:T(8,128)(2,1)S(1)}, u32[]{:S(2)}, u32[]{:S(2)}) collective-permute-start(bf16[176,384]{1,0:T(8,128)(2,1)S(1)} %collective-permute-done.5.refs_4_), channel_id=1, source_target_pairs={{0,4},{2,6},{4,0},{6,2},{8,12},{10,14},{12,8},{14,10},{16,20},{18,... | collective-permute-start | bytes 405512 | tf_op jit(solution)/shard_map/ppermute | solution.py:944
  18.7 6.1 %collective-permute-start.6 = (bf16[176,384]{1,0:T(8,128)(2,1)S(1)}, bf16[176,384]{1,0:T(8,128)(2,1)S(1)}, u32[]{:S(2)}, u32[]{:S(2)}) collective-permute-start(bf16[176,384]{1,0:T(8,128)(2,1)S(1)} %collective-permute-done.5.refs_4_), channel_id=1, source_target_pairs={{0,2},{2,0},{4,6},{6,4},{8,10},{10,8},{12,14},{14,12},{16,18},{18,... | collective-permute-start | bytes 405512 | tf_op jit(solution)/shard_map/ppermute | solution.py:944
  20.9 29.1 %collective-permute-start.13 = (bf16[1024,384]{1,0:T(8,128)(2,1)}, bf16[1024,384]{1,0:T(8,128)(2,1)S(1)}, u32[]{:S(2)}, u32[]{:S(2)}) collective-permute-start(bf16[1024,384]{1,0:T(8,128)(2,1)} %constant_dynamic-slice_fusion), channel_id=1, source_target_pairs={{0,1},{1,0},{2,3},{3,2},{4,5},{5,4},{6,7},{7,6},{8,9},{9,8},{10,11... | collective-permute-start | bytes 2359304 | tf_op jit(solution)/shard_map/ppermute | solution.py:940
  22.5 9.6 %collective-permute-start.11 = (bf16[336,384]{1,0:T(8,128)(2,1)S(1)}, bf16[336,384]{1,0:T(8,128)(2,1)S(1)}, u32[]{:S(2)}, u32[]{:S(2)}) collective-permute-start(bf16[336,384]{1,0:T(8,128)(2,1)S(1)} %collective-permute-done.9.p0), channel_id=1, source_target_pairs={{0,8},{2,10},{4,12},{6,14},{8,0},{10,2},{12,4},{14,6},{16,24},{18,... | collective-permute-start | bytes 774152 | tf_op jit(solution)/shard_map/ppermute | solution.py:944
  24.1 8.1 %collective-permute-start.10 = (bf16[336,384]{1,0:T(8,128)(2,1)S(1)}, bf16[336,384]{1,0:T(8,128)(2,1)S(1)}, u32[]{:S(2)}, u32[]{:S(2)}) collective-permute-start(bf16[336,384]{1,0:T(8,128)(2,1)S(1)} %collective-permute-done.9.p0), channel_id=1, source_target_pairs={{0,4},{2,6},{4,0},{6,2},{8,12},{10,14},{12,8},{14,10},{16,20},{18,... | collective-permute-start | bytes 774152 | tf_op jit(solution)/shard_map/ppermute | solution.py:944
  32.2 17.9 %collective-permute-start.16 = (bf16[336,384]{1,0:T(8,128)(2,1)S(1)}, bf16[336,384]{1,0:T(8,128)(2,1)}, u32[]{:S(2)}, u32[]{:S(2)}) collective-permute-start(bf16[336,384]{1,0:T(8,128)(2,1)S(1)} %collective-permute-done.11.p4), channel_id=1, source_target_pairs={{0,2},{2,0},{4,6},{6,4},{8,10},{10,8},{12,14},{14,12},{16,18},{18,... | collective-permute-start | bytes 774152 | tf_op jit(solution)/shard_map/ppermute | solution.py:944
  32.4 14.8 %collective-permute-start.12 = (bf16[336,384]{1,0:T(8,128)(2,1)S(1)}, bf16[336,384]{1,0:T(8,128)(2,1)}, u32[]{:S(2)}, u32[]{:S(2)}) collective-permute-start(bf16[336,384]{1,0:T(8,128)(2,1)S(1)} %collective-permute-done.11.p4), channel_id=1, source_target_pairs={{0,4},{2,6},{4,0},{6,2},{8,12},{10,14},{12,8},{14,10},{16,20},{18,... | collective-permute-start | bytes 774152 | tf_op jit(solution)/shard_map/ppermute | solution.py:944
  33.6 16.5 %collective-permute-start.14 = (bf16[336,384]{1,0:T(8,128)(2,1)S(1)}, bf16[336,384]{1,0:T(8,128)(2,1)}, u32[]{:S(2)}, u32[]{:S(2)}) collective-permute-start(bf16[336,384]{1,0:T(8,128)(2,1)S(1)} %collective-permute-done.9.p0), channel_id=1, source_target_pairs={{0,2},{2,0},{4,6},{6,4},{8,10},{10,8},{12,14},{14,12},{16,18},{18,... | collective-permute-start | bytes 774152 | tf_op jit(solution)/shard_map/ppermute | solution.py:944
  34.5 15.6 %collective-permute-start.15 = (bf16[336,384]{1,0:T(8,128)(2,1)S(1)}, bf16[336,384]{1,0:T(8,128)(2,1)}, u32[]{:S(2)}, u32[]{:S(2)}) collective-permute-start(bf16[336,384]{1,0:T(8,128)(2,1)S(1)} %collective-permute-done.10.p2), channel_id=1, source_target_pairs={{0,2},{2,0},{4,6},{6,4},{8,10},{10,8},{12,14},{14,12},{16,18},{18,... | collective-permute-start | bytes 774152 | tf_op jit(solution)/shard_map/ppermute | solution.py:944
  86.1 21.6 %collective-permute-start.19 = (bf16[640,384]{1,0:T(8,128)(2,1)S(1)}, bf16[640,384]{1,0:T(8,128)(2,1)S(1)}, u32[]{:S(2)}, u32[]{:S(2)}) collective-permute-start(bf16[640,384]{1,0:T(8,128)(2,1)S(1)} %get-tuple-element.144), channel_id=1, source_target_pairs={{0,4},{2,6},{4,0},{6,2},{8,12},{10,14},{12,8},{14,10},{16,20},{18,... | collective-permute-start | bytes 1474568 | tf_op jit(solution)/shard_map/ppermute | solution.py:944
  87.8 23.5 %collective-permute-start.20 = (bf16[640,384]{1,0:T(8,128)(2,1)S(1)}, bf16[640,384]{1,0:T(8,128)(2,1)S(1)}, u32[]{:S(2)}, u32[]{:S(2)}) collective-permute-start(bf16[640,384]{1,0:T(8,128)(2,1)S(1)} %get-tuple-element.145), channel_id=1, source_target_pairs={{0,1},{1,0},{2,3},{3,2},{4,5},{5,4},{6,7},{7,6},{8,9},{9,8},{10,11... | collective-permute-start | bytes 1474568 | tf_op jit(solution)/shard_map/ppermute | solution.py:940
  89.4 22.0 %collective-permute-start.21 = (bf16[640,384]{1,0:T(8,128)(2,1)S(1)}, bf16[640,384]{1,0:T(8,128)(2,1)S(1)}, u32[]{:S(2)}, u32[]{:S(2)}) collective-permute-start(bf16[640,384]{1,0:T(8,128)(2,1)S(1)} %get-tuple-element.146), channel_id=1, source_target_pairs={{0,5},{1,4},{2,7},{3,6},{4,1},{5,0},{6,3},{7,2},{8,13},{9,12},{10,... | collective-permute-start | bytes 1474568 | tf_op jit(solution)/shard_map/ppermute | solution.py:949
  115.0 9.9 %collective-permute-start.23 = (bf16[384,384]{1,0:T(8,128)(2,1)S(1)}, bf16[384,384]{1,0:T(8,128)(2,1)S(1)}, u32[]{:S(2)}, u32[]{:S(2)}) collective-permute-start(bf16[384,384]{1,0:T(8,128)(2,1)S(1)} %get-tuple-element.159), channel_id=1, source_target_pairs={{0,4},{2,6},{4,0},{6,2},{8,12},{10,14},{12,8},{14,10},{16,20},{18,... | collective-permute-start | bytes 884744 | tf_op jit(solution)/shard_map/ppermute | solution.py:944
  116.3 13.5 %collective-permute-start.24 = (bf16[384,384]{1,0:T(8,128)(2,1)S(1)}, bf16[384,384]{1,0:T(8,128)(2,1)S(1)}, u32[]{:S(2)}, u32[]{:S(2)}) collective-permute-start(bf16[384,384]{1,0:T(8,128)(2,1)S(1)} %get-tuple-element.160), channel_id=1, source_target_pairs={{0,1},{1,0},{2,3},{3,2},{4,5},{5,4},{6,7},{7,6},{8,9},{9,8},{10,11... | collective-permute-start | bytes 884744 | tf_op jit(solution)/shard_map/ppermute | solution.py:940
  117.2 14.3 %collective-permute-start.25 = (bf16[384,384]{1,0:T(8,128)(2,1)S(1)}, bf16[384,384]{1,0:T(8,128)(2,1)S(1)}, u32[]{:S(2)}, u32[]{:S(2)}) collective-permute-start(bf16[384,384]{1,0:T(8,128)(2,1)S(1)} %get-tuple-element.161), channel_id=1, source_target_pairs={{0,5},{1,4},{2,7},{3,6},{4,1},{5,0},{6,3},{7,2},{8,13},{9,12},{10,... | collective-permute-start | bytes 884744 | tf_op jit(solution)/shard_map/ppermute | solution.py:949
  118.6 14.5 %collective-permute-start.29 = (bf16[160,384]{1,0:T(8,128)(2,1)S(1)}, bf16[160,384]{1,0:T(8,128)(2,1)S(1)}, u32[]{:S(2)}, u32[]{:S(2)}) collective-permute-start(bf16[160,384]{1,0:T(8,128)(2,1)S(1)} %get-tuple-element.173), channel_id=1, source_target_pairs={{0,8},{2,10},{4,12},{6,14},{8,0},{10,2},{12,4},{14,6},{16,24},{18,... | collective-permute-start | bytes 368648 | tf_op jit(solution)/shard_map/ppermute | solution.py:955
  120.2 13.0 %collective-permute-start.30 = (bf16[160,384]{1,0:T(8,128)(2,1)S(1)}, bf16[160,384]{1,0:T(8,128)(2,1)S(1)}, u32[]{:S(2)}, u32[]{:S(2)}) collective-permute-start(bf16[160,384]{1,0:T(8,128)(2,1)S(1)} %get-tuple-element.174), channel_id=1, source_target_pairs={{0,16},{2,18},{4,20},{6,22},{8,24},{10,26},{12,28},{14,30},{16,0},... | collective-permute-start | bytes 368648 | tf_op jit(solution)/shard_map/ppermute | solution.py:955
  125.0 8.2 %collective-permute-start.31 = (bf16[160,384]{1,0:T(8,128)(2,1)S(1)}, bf16[160,384]{1,0:T(8,128)(2,1)S(1)}, u32[]{:S(2)}, u32[]{:S(2)}) collective-permute-start(bf16[160,384]{1,0:T(8,128)(2,1)S(1)} %get-tuple-element.175), channel_id=1, source_target_pairs={{0,24},{2,26},{4,28},{6,30},{8,16},{10,18},{12,20},{14,22},{16,8},... | collective-permute-start | bytes 368648 | tf_op jit(solution)/shard_map/ppermute | solution.py:955
  132.2 22.1 %collective-permute-start.35 = (bf16[1024,384]{1,0:T(8,128)(2,1)S(1)}, bf16[1024,384]{1,0:T(8,128)(2,1)S(1)}, u32[]{:S(2)}, u32[]{:S(2)}) collective-permute-start(bf16[1024,384]{1,0:T(8,128)(2,1)S(1)} %get-tuple-element.176), channel_id=1, source_target_pairs={{0,1},{1,0},{2,3},{3,2},{4,5},{5,4},{6,7},{7,6},{8,9},{9,8},{10,11... | collective-permute-start | bytes 2359304 | tf_op jit(solution)/shard_map/ppermute | solution.py:940
  133.2 7.7 %collective-permute-start.34 = (bf16[160,384]{1,0:T(8,128)(2,1)S(1)}, bf16[160,384]{1,0:T(8,128)(2,1)S(1)}, u32[]{:S(2)}, u32[]{:S(2)}) collective-permute-start(bf16[160,384]{1,0:T(8,128)(2,1)S(1)} %add_convert_fusion), channel_id=1, source_target_pairs={{0,24},{2,26},{4,28},{6,30},{8,16},{10,18},{12,20},{14,22},{16,8},... | collective-permute-start | bytes 368648 | tf_op jit(solution)/shard_map/ppermute | solution.py:955
  136.9 11.1 %collective-permute-start.33 = (bf16[160,384]{1,0:T(8,128)(2,1)S(1)}, bf16[160,384]{1,0:T(8,128)(2,1)S(1)}, u32[]{:S(2)}, u32[]{:S(2)}) collective-permute-start(bf16[160,384]{1,0:T(8,128)(2,1)S(1)} %add_convert_fusion), channel_id=1, source_target_pairs={{0,16},{2,18},{4,20},{6,22},{8,24},{10,26},{12,28},{14,30},{16,0},... | collective-permute-start | bytes 368648 | tf_op jit(solution)/shard_map/ppermute | solution.py:955
  136.9 14.9 %collective-permute-start.32 = (bf16[160,384]{1,0:T(8,128)(2,1)S(1)}, bf16[160,384]{1,0:T(8,128)(2,1)S(1)}, u32[]{:S(2)}, u32[]{:S(2)}) collective-permute-start(bf16[160,384]{1,0:T(8,128)(2,1)S(1)} %add_convert_fusion), channel_id=1, source_target_pairs={{0,8},{2,10},{4,12},{6,14},{8,0},{10,2},{12,4},{14,6},{16,24},{18,... | collective-permute-start | bytes 368648 | tf_op jit(solution)/shard_map/ppermute | solution.py:955
  137.7 15.7 %collective-permute-start.26 = (bf16[96,384]{1,0:T(8,128)(2,1)S(1)}, bf16[96,384]{1,0:T(8,128)(2,1)S(1)}, u32[]{:S(2)}, u32[]{:S(2)}) collective-permute-start(bf16[96,384]{1,0:T(8,128)(2,1)S(1)} %get-tuple-element.169), channel_id=1, source_target_pairs={{0,8},{2,10},{4,12},{6,14},{8,0},{10,2},{12,4},{14,6},{16,24},{18,... | collective-permute-start | bytes 221192 | tf_op jit(solution)/shard_map/ppermute | solution.py:955
  140.9 12.5 %collective-permute-start.27 = (bf16[96,384]{1,0:T(8,128)(2,1)S(1)}, bf16[96,384]{1,0:T(8,128)(2,1)S(1)}, u32[]{:S(2)}, u32[]{:S(2)}) collective-permute-start(bf16[96,384]{1,0:T(8,128)(2,1)S(1)} %get-tuple-element.170), channel_id=1, source_target_pairs={{0,16},{2,18},{4,20},{6,22},{8,24},{10,26},{12,28},{14,30},{16,0},... | collective-permute-start | bytes 221192 | tf_op jit(solution)/shard_map/ppermute | solution.py:955
  148.0 6.3 %collective-permute-start.28 = (bf16[96,384]{1,0:T(8,128)(2,1)S(1)}, bf16[96,384]{1,0:T(8,128)(2,1)S(1)}, u32[]{:S(2)}, u32[]{:S(2)}) collective-permute-start(bf16[96,384]{1,0:T(8,128)(2,1)S(1)} %get-tuple-element.171), channel_id=1, source_target_pairs={{0,24},{2,26},{4,28},{6,30},{8,16},{10,18},{12,20},{14,22},{16,8},... | collective-permute-start | bytes 221192 | tf_op jit(solution)/shard_map/ppermute | solution.py:955
  151.9 16.0 %collective-permute-start.43 = (bf16[1024,384]{1,0:T(8,128)(2,1)S(1)}, bf16[1024,384]{1,0:T(8,128)(2,1)S(1)}, u32[]{:S(2)}, u32[]{:S(2)}) collective-permute-start(bf16[1024,384]{1,0:T(8,128)(2,1)S(1)} %get-tuple-element.186), channel_id=1, source_target_pairs={{0,1},{1,0},{2,3},{3,2},{4,5},{5,4},{6,7},{7,6},{8,9},{9,8},{10,11... | collective-permute-start | bytes 2359304 | tf_op jit(solution)/shard_map/ppermute | solution.py:940
  154.3 10.2 %collective-permute-start.40 = (bf16[640,384]{1,0:T(8,128)(2,1)S(1)}, bf16[640,384]{1,0:T(8,128)(2,1)S(1)}, u32[]{:S(2)}, u32[]{:S(2)}) collective-permute-start(bf16[640,384]{1,0:T(8,128)(2,1)S(1)} %pad_maximum_fusion.p0), channel_id=1, source_target_pairs={{0,4},{2,6},{4,0},{6,2},{8,12},{10,14},{12,8},{14,10},{16,20},{18,... | collective-permute-start | bytes 1474568 | tf_op jit(solution)/shard_map/ppermute | solution.py:944
  155.6 9.0 %collective-permute-start.38 = (bf16[96,384]{1,0:T(8,128)(2,1)S(1)}, bf16[96,384]{1,0:T(8,128)(2,1)S(1)}, u32[]{:S(2)}, u32[]{:S(2)}) collective-permute-start(bf16[96,384]{1,0:T(8,128)(2,1)S(1)} %add_convert_fusion.1), channel_id=1, source_target_pairs={{0,24},{2,26},{4,28},{6,30},{8,16},{10,18},{12,20},{14,22},{16,8},... | collective-permute-start | bytes 221192 | tf_op jit(solution)/shard_map/ppermute | solution.py:955
  164.6 9.5 %collective-permute-start.39 = (bf16[384,384]{1,0:T(8,128)(2,1)S(1)}, bf16[384,384]{1,0:T(8,128)(2,1)S(1)}, u32[]{:S(2)}, u32[]{:S(2)}) collective-permute-start(bf16[384,384]{1,0:T(8,128)(2,1)S(1)} %constant_dynamic-update-slice_fusion.p0), channel_id=1, source_target_pairs={{0,4},{2,6},{4,0},{6,2},{8,12},{10,14},{12,8},{14,10},{16,20},{18,... | collective-permute-start | bytes 884744 | tf_op jit(solution)/shard_map/ppermute | solution.py:944
  (48 other events, 374.7 us)
